TPU v7x, 32 devices: a whole 2x2x4 slice. The times are simulated.
32 devices in a mesh: elec: 16 (over z, x, core), therm: 2 (over y).
Axes of the slice: x: 2, y: 2, z: 4, core: 2. Of those that a mesh axis runs over, the one named last changes fastest.
Arguments:
- injected_amperage: bfloat16 [1024, 64, 128], P(('elec', 'therm')), may hold values from -6 to 6
- voltage_self_admittance: float32 [1024, 64], P(('elec', 'therm')), may hold values from 1.2 to 2.5
- voltage_coupling_tiles: bfloat16 [1024, 4, 64, 64], P(('elec', 'therm')), may hold values from -0.5 to 0.5
- voltage_partner_tile_ids: int32 [1024, 4], P(('elec', 'therm')), may hold values from 0 to 31
- interface_tiles_per_level: int32 [128, 2], P(('elec', 'therm')), may hold values from 0 to 31
- interface_admittance: bfloat16 [256, 64, 64], P(('elec', 'therm')), may hold values from -0.5 to 0.5
- warmth_receiver_layer: int32 [1024, 1], P(('elec', 'therm')), may hold values from 0 to 1; in each aligned block of 32 rows (0 to 31, 32 to 63, ...) at most 32 rows name the same one
- warmth_receiver_tile: int32 [1024], P(('elec', 'therm')), may hold values from 0 to 31
- warmth_values: bfloat16 [1024, 64, 128], P(('elec', 'therm')), may hold values from -4 to 4
- warmth_self_coefficient: float32 [1024, 64], P(('elec', 'therm')), may hold values from 1 to 3
- warmth_coupling_tiles: bfloat16 [1024, 3, 64, 64], P(('elec', 'therm')), may hold values from -0.4375 to 0.4375
- warmth_partner_tile_ids: int32 [1024, 3], P(('elec', 'therm')), may hold values from 0 to 31
- layer_boundary_couplings: bfloat16 [128, 64, 64], P(('elec', 'therm')), may hold values from -0.4375 to 0.4375
- substance_kind: int32 [1024, 64], P(('elec', 'therm')), may hold values from 0 to 7
- reference_material_kappas: float32 [8], replicated, may hold values from 0.5 to 4
- warmth_storage_per_point: float32 [1024, 64], P(('elec', 'therm')), may hold values from 1 to 4
Outputs:
- voltage_solution: bfloat16 [1024, 64, 128], P(('elec', 'therm'))
- advanced_warmth_values: float32 [1024, 64, 128], P(('elec', 'therm'))
Inputs may be any that keep to these rules, and one draw needn't show every extreme that they name: `warmth_receiver_layer`: among the 32 blocks of one device at most 32 name the same owner, and exactly 32 do for some owner. `voltage_partner_tile_ids`: indexes a block of the same device. `interface_tiles_per_level`: indexes a block of the same device. `warmth_receiver_tile`: indexes a thermal block of the owner. `warmth_partner_tile_ids`: indexes a thermal block of the same device.
All inputs are finite; a program needn't handle non-finite values.
Results may differ from a plain program's by a relative error of at most 0.025.
Values may be sent and summed in bfloat16 or wider, within the bound.
No kernel may reach another device: no remote copies, remote signals or barrier semaphores. Data moves between devices by JAX's collectives and lax.ppermute only.
A program may use at most 64 MiB of HBM per device.

v0:
```python
import functools

import jax
import jax.numpy as jnp
from jax import lax
from jax.experimental import pallas as pl
from jax.experimental.pallas import tpu as pltpu
from jax.sharding import PartitionSpec as P

SWEEPS = 5
ZB = 2

relax_factor = 0.8
time_increment = 0.5

F32 = jnp.float32
BF16 = jnp.bfloat16
I32 = jnp.int32
VM = pl.BlockSpec(memory_space=pltpu.VMEM)
SM = pl.BlockSpec(memory_space=pltpu.SMEM)
HB = pl.BlockSpec(memory_space=pltpu.HBM)
ANY = pl.BlockSpec(memory_space=pl.ANY)
SPACES = {id(VM): pltpu.VMEM, id(HB): pltpu.HBM, id(SM): pltpu.SMEM}
LIMIT = 4 << 20


def call(kernel, outs, ins, name, aliases={}, scratch=(), flops=0, limit=LIMIT):
    args = []
    for x, spec in ins:
        if spec is VM or spec is HB:
            x = pltpu.with_memory_space_constraint(x, SPACES[id(spec)])
        args.append(x)
    return pl.pallas_call(
        kernel,
        out_shape=[SPACES[id(spec)](shape, dtype) for shape, dtype, spec in outs],
        in_specs=[spec for _, spec in ins],
        out_specs=[spec for _, _, spec in outs],
        input_output_aliases=aliases,
        scratch_shapes=scratch,
        compiler_params=pltpu.CompilerParams(vmem_limit_bytes=limit),
        cost_estimate=pl.CostEstimate(flops=flops, bytes_accessed=0, transcendentals=0),
        name=name,
    )(*args)


def on(spec, *arrays):
    return [(x, spec) for x in arrays]


def from_partner(block, axis, bit):
    count = lax.axis_size(axis)
    route = []
    for low in range(count):
        high = low | 1 << bit
        if high != low and high < count:
            route += [(low, high), (high, low)]
    return lax.ppermute(block, axis, route)


def column(table, row, width):
    return jnp.broadcast_to(table[:, row : row + 1], (table.shape[0], width))


def joined(tiles_ref, row):
    return jnp.concatenate([tiles_ref[row, k] for k in range(tiles_ref.shape[1])], axis=1)


def picked(field_ref, ids_ref, row):
    return jnp.concatenate([field_ref[ids_ref[k, row]] for k in range(ids_ref.shape[0])], axis=0)


def start_kernel(levels, amps, diag, face_ids, *refs):
    small = refs[:3]
    amps_v, diag_v, face_ids_s = refs[3:6]
    small_s, faces, sems = refs[6:9], refs[9 : 9 + levels], refs[-1]
    pairs = [(face_ids, face_ids_s), (diag, diag_v), (amps, amps_v)]
    copies = [
        pltpu.make_async_copy(a, b, sems.at[n])
        for n, (a, b) in enumerate(pairs + list(zip(small, small_s)))
    ]
    for c in copies:
        c.start()
    copies[0].wait()
    copies[1].wait()
    scale = relax_factor / diag_v[...]
    rows = lax.broadcasted_iota(I32, scale.shape, 0)
    chosen = []
    for b in range(levels):
        for f in range(face_ids.shape[0]):
            mine = jnp.where(rows == face_ids_s[f, b], scale, 0.0)
            chosen.append(jnp.sum(mine, axis=0, keepdims=True))
    turned = jnp.concatenate(chosen, axis=0).T
    copies[2].wait()
    for b in range(levels):
        for f in range(face_ids.shape[0]):
            s = column(turned, b * face_ids.shape[0] + f, amps.shape[2])
            points = amps.shape[1]
            block = s * amps_v[face_ids_s[f, b]].astype(F32)
            faces[b][f * points : (f + 1) * points] = block.astype(BF16)
    for c in copies[3:]:
        c.wait()


def route(groups, layer, tile, face_ids, slot, rows, flag, place):
    own = lax.axis_index("therm")
    blocks, tiles = slot.shape[0], flag.shape[0]
    levels, width = face_ids.shape[1], face_ids.shape[0]
    early_slots = max(tiles - levels * width, 0)
    lane = lax.broadcasted_iota(I32, rows.shape[1:], 1)

    def away(i):
        a = layer[0, i] - own
        return jnp.where(a < 0, a + groups, a)

    def home(i, c):
        slot[i] = tile[i]
        return c

    lax.fori_loop(0, blocks, home, 0)
    for g in range(1, groups):

        def clear(j, c):
            flag[j] = 0
            return c

        def mark(i, c):
            j = tile[i]
            flag[j] = jnp.where(away(i) == g, 1, flag[j])
            return c

        def late(j, c):
            is_late = flag[j] == 2
            place[j] = jnp.where(is_late, c, 0)
            return c + is_late.astype(I32)

        def early(j, c):
            at, behind, row = c
            is_early = flag[j] == 1
            fits = at < early_slots
            pos = jnp.where(fits, at, behind)
            pos = jnp.where(is_early, pos, place[j])
            place[j] = pos
            used = flag[j] > 0
            row = jnp.where((lane == pos) & used, j, row)
            at = at + (is_early & fits).astype(I32)
            behind = behind + (is_early & jnp.logical_not(fits)).astype(I32)
            return at, behind, row

        def assign(i, c):
            slot[i] = jnp.where(away(i) == g, g * tiles + place[tile[i]], slot[i])
            return c

        lax.fori_loop(0, tiles, clear, 0)
        lax.fori_loop(0, blocks, mark, 0)
        for b in range(levels):
            for f in range(width):
                i = face_ids[f, b]
                j = tile[i]
                flag[j] = jnp.where(away(i) == g, 2, flag[j])
        behind = lax.fori_loop(0, tiles, late, early_slots)
        _, _, row = lax.fori_loop(
            0, tiles, early, (0, behind, jnp.zeros(rows.shape[1:], I32))
        )
        lax.fori_loop(0, blocks, assign, 0)
        rows[g - 1] = row.astype(F32).astype(BF16)


def first_kernel(groups, ids, layer, tile, face_ids, tiles, warmth, kind, amps, diag, *refs):
    packed, state_out, field_out, scale, warmth_v, kind_v, slot, rows = refs[:8]
    tiles_v, field, flag, place, sems, later_sems = refs[8:]
    blocks = packed.shape[0]
    step = blocks // sems.shape[0]
    copies = []
    later = [
        pltpu.make_async_copy(warmth, warmth_v, later_sems.at[0]),
        pltpu.make_async_copy(kind, kind_v, later_sems.at[1]),
    ]
    for p in range(0, blocks, step):
        part = pl.ds(p, step)
        copies.append(
            pltpu.make_async_copy(tiles.at[part], tiles_v.at[part], sems.at[p // step])
        )
    for c in copies + later:
        c.start()
    route(groups, layer, tile, face_ids, slot, rows, flag, place)
    turned = (relax_factor / diag[...]).T
    for i in range(blocks):
        s = column(turned, i, scale.shape[2])
        scale[i] = s
        field[i] = (s * amps[i].astype(F32)).astype(BF16)
    for i in range(blocks):
        if i % step == 0:
            copies[i // step].wait()
        row = joined(tiles_v, i)
        packed[i] = row
        image = jnp.dot(row, picked(field, ids, i), preferred_element_type=F32)
        a = amps[i].astype(F32)
        s = scale[i]
        x = s * a - relax_factor * field[i].astype(F32) + s * (a - image)
        state_out[i] = x
        field_out[i] = x.astype(BF16)
    for c in later:
        c.wait()


def near_kernel(ids, packed, field, state, amps, scale, state_out, field_out, *for_heat):
    for i in range(packed.shape[0]):
        image = jnp.dot(packed[i], picked(field, ids, i), preferred_element_type=F32)
        x = state[i] - relax_factor * field[i].astype(F32)
        x = x + scale[i] * (amps[i].astype(F32) - image)
        state_out[i] = x
        field_out[i] = x.astype(BF16)
    if for_heat:
        heat, diag = for_heat
        heat[...] = jnp.zeros(heat.shape, F32)
        for i in range(packed.shape[0]):
            diag[i] = relax_factor / scale[i]


def face_terms(levels, face_ids, admittance, incoming, terms):
    width, points = face_ids.shape[0], terms.shape[1]
    for b in range(levels):
        for f in range(width):
            block = incoming[b][f * points : (f + 1) * points]
            terms[b * width + f] = jnp.dot(
                admittance[b * width + f], block, preferred_element_type=F32
            )


def in_level_order(refs, order):
    return [refs[order.index(b)] for b in range(len(order))]


def update_faces(face_ids, admittance, scale, incoming, state, field, faces, terms):
    levels, width, points = len(faces), face_ids.shape[0], terms.shape[1]
    face_terms(levels, face_ids, admittance, incoming, terms)
    for b in range(levels):
        for f in range(width):
            i = face_ids[f, b]
            state[i] = state[i] - scale[i] * terms[b * width + f]
    for b in range(levels):
        for f in range(width):
            i = face_ids[f, b]
            x = state[i].astype(BF16)
            field[i] = x
            faces[b][f * points : (f + 1) * points] = x


def face_kernel(order, token, face_ids, admittance, scale, *refs):
    levels = len(order)
    incoming = in_level_order(refs[:levels], order)
    state, field = refs[levels + 2 : levels + 4]
    faces, terms = refs[levels + 4 : 2 * levels + 4], refs[-1]
    update_faces(face_ids, admittance, scale, incoming, state, field, faces, terms)


def heat_kernel(
    order, spots, token, slot, ids, face_ids, admittance, scale, packed, diag, rows, *refs
):
    levels = len(order)
    incoming = in_level_order(refs[:levels], order)
    state, field, heat, soon = refs[levels + 3 : levels + 7]
    faces, terms = refs[levels + 7 : 2 * levels + 7], refs[-1]
    groups, points = soon.shape[0] + 1, heat.shape[1]
    tiles = heat.shape[0] // groups
    update_faces(face_ids, admittance, scale, incoming, state, field, faces, terms)
    for i in range(packed.shape[0]):
        image = jnp.dot(packed[i], picked(field, ids, i), preferred_element_type=F32)
        v = field[i].astype(F32)
        s = slot[i]
        heat[s] = heat[s] + v * (diag[i] * v + image)
    for g in range(1, groups):
        blocks = [heat[g * tiles + p].astype(BF16) for p in range(spots)]
        for p, block in enumerate(blocks):
            soon[g - 1, p * points : (p + 1) * points] = block
        soon[g - 1, len(blocks) * points :] = rows[g - 1]


def heat_face_kernel(order, slot, face_ids, admittance, *refs):
    levels = len(order)
    incoming = in_level_order(refs[:levels], order)
    heat, field, late, terms = refs[levels + 2 :]
    groups, spots = late.shape[0] + 1, late.shape[1]
    tiles = heat.shape[0] // groups
    width = face_ids.shape[0]
    face_terms(levels, face_ids, admittance, incoming, terms)
    for b in range(levels):
        for f in range(width):
            i = face_ids[f, b]
            s = slot[i]
            heat[s] = heat[s] + field[i].astype(F32) * terms[b * width + f]
    for g in range(1, groups):
        late[g - 1] = heat[(g + 1) * tiles - spots : (g + 1) * tiles].astype(BF16)


def kappa_columns(kappas, kind):
    kinds = kind[...]
    kappa = jnp.zeros(kinds.shape, F32)
    for m in range(kappas.shape[0]):
        kappa = jnp.where(kinds == m, kappas[m], kappa)
    return kappa.T


def block_flux(kappa, warmth):
    w = warmth.astype(F32)
    return (kappa * (1.0 + 0.4 * jnp.tanh(w)) * w).astype(BF16)


def edge_kernel(token, kappas, kind, warmth, *edges):
    turned = kappa_columns(kappas, kind)
    tiles, points, width = warmth.shape
    sends_top = lax.axis_index("therm") == 0
    for z in range(ZB):
        top = tiles - ZB + z
        low = block_flux(column(turned, z, width), warmth[z])
        high = block_flux(column(turned, top, width), warmth[top])
        if len(edges) == 1:
            both = jnp.where(sends_top, high.astype(F32), low.astype(F32))
            edges[0][z] = both.astype(BF16)
        else:
            edges[0][z], edges[1][z] = low, high


def conduction_kernel(
    groups,
    ids,
    kappas,
    tiles,
    kind,
    coefficient,
    storage,
    couplings,
    warmth,
    below,
    above,
    heat,
    rest,
    gain,
    flux,
):
    count = tiles.shape[0]
    width = flux.shape[2]
    turned = kappa_columns(kappas, kind)
    for i in range(count):
        flux[i] = block_flux(column(turned, i, width), warmth[i])
    own = lax.axis_index("therm")
    lowest = (own > 0).astype(F32)
    highest = (own < groups - 1).astype(F32)
    diag = coefficient[...].T
    gains = (time_increment / storage[...]).T
    for i in range(count):
        image = jnp.dot(joined(tiles, i), picked(flux, ids, i), preferred_element_type=F32)
        image = image + column(diag, i, width) * flux[i].astype(F32)
        if i < ZB:
            term = jnp.dot(couplings[i], below[i], preferred_element_type=F32)
            image = image + lowest * term
        if i >= count - ZB:
            z = i - (count - ZB)
            term = jnp.dot(couplings[ZB + z], above[z], preferred_element_type=F32)
            image = image + highest * term
        g = column(gains, i, width)
        gain[i] = g
        rest[i] = warmth[i].astype(F32) - g * image


def early_kernel(shifts, heat, gain, *refs):
    maps, soon = refs[:shifts], refs[shifts : 2 * shifts]
    rest, field, out = refs[2 * shifts + 2 : 2 * shifts + 5]
    spots, sem = refs[2 * shifts + 5 : -1], refs[-1]
    tiles, points = rest.shape[:2]
    sent = tiles - spots[0].shape[0]
    for i in range(tiles):
        rest[i] = rest[i] + gain[i] * heat[i]
    for g in range(shifts):
        for p in range(sent):
            j = maps[g][p]
            rest[j] = rest[j] + gain[j] * soon[g][p * points : (p + 1) * points].astype(F32)
    whole = pltpu.make_async_copy(rest, out, sem)
    whole.start()
    for g in range(shifts):
        for p in range(spots[g].shape[0]):
            spots[g][p] = maps[g][tiles - spots[g].shape[0] + p]
    whole.wait()


def late_kernel(shifts, gain, *refs):
    maps, late = refs[:shifts], refs[shifts : 2 * shifts]
    rest, out, sems = refs[2 * shifts], refs[2 * shifts + 2], refs[2 * shifts + 3]
    spots = late[0].shape[0]
    for g in range(shifts):
        for p in range(spots):
            j = maps[g][p]
            rest[j] = rest[j] + gain[j] * late[g][p].astype(F32)
    copies = []
    for g in range(shifts):
        for p in range(spots):
            j = maps[g][p]
            copies.append(pltpu.make_async_copy(rest.at[j], out.at[j], sems.at[g * spots + p]))
    for c in copies:
        c.start()
    for c in copies:
        c.wait()


def body(
    injected_amperage,
    voltage_self_admittance,
    voltage_coupling_tiles,
    voltage_partner_tile_ids,
    interface_tiles_per_level,
    interface_admittance,
    warmth_receiver_layer,
    warmth_receiver_tile,
    warmth_values,
    warmth_self_coefficient,
    warmth_coupling_tiles,
    warmth_partner_tile_ids,
    layer_boundary_couplings,
    substance_kind,
    reference_material_kappas,
    warmth_storage_per_point,
):
    blocks, points, regimes = injected_amperage.shape
    tiles = warmth_values.shape[0]
    levels, width = interface_tiles_per_level.shape
    links = voltage_partner_tile_ids.shape[1]
    groups = lax.axis_size("therm")
    shifts = groups - 1
    whole = (blocks, points, regimes)
    warm = (tiles, points, regimes)
    face = (width * points, regimes)
    late_spots = min(levels * width, tiles)
    early_spots = tiles - late_spots
    sent_rows = early_spots * points
    near_flops = 2 * blocks * links * points * points * regimes
    terms = pltpu.VMEM((levels * width, points, regimes), F32)
    dma = pltpu.SemaphoreType.DMA

    def exchange(faces, order):
        return [from_partner(faces[b], "elec", b) for b in order]

    far_first = list(range(levels))[::-1]
    near, *middle, far = range(levels)
    orders = [far_first, [far] + middle + [near], middle[::-1] + [far, near]]

    amps, diag, face_ids, ids, layer, tile, *faces = call(
        functools.partial(start_kernel, levels),
        [
            (whole, BF16, VM),
            (voltage_self_admittance.shape, F32, VM),
            ((width, levels), I32, SM),
            ((links, blocks), I32, SM),
            ((1, blocks), I32, SM),
            ((blocks,), I32, SM),
        ]
        + [(face, BF16, VM)] * levels,
        on(
            HB,
            injected_amperage,
            voltage_self_admittance,
            interface_tiles_per_level.T,
            voltage_partner_tile_ids.T,
            warmth_receiver_layer.T,
            warmth_receiver_tile,
        ),
        "start",
        scratch=[dma((6,))],
    )
    order = far_first
    incoming = exchange(faces, order)

    packed, state, field, scale, warmth, kind, slot, rows = call(
        functools.partial(first_kernel, groups),
        [
            ((blocks, points, links * points), BF16, VM),
            (whole, F32, VM),
            (whole, BF16, VM),
            (whole, F32, VM),
            (warm, BF16, VM),
            (substance_kind.shape, I32, VM),
            ((blocks,), I32, SM),
            ((shifts, 16, regimes), BF16, VM),
        ],
        on(SM, ids, layer, tile, face_ids)
        + on(HB, voltage_coupling_tiles, warmth_values, substance_kind)
        + on(VM, amps, diag),
        "first",
        scratch=[
            pltpu.VMEM(voltage_coupling_tiles.shape, BF16),
            pltpu.VMEM(whole, BF16),
            pltpu.SMEM((tiles,), I32),
            pltpu.SMEM((tiles,), I32),
            dma((4,)),
            dma((2,)),
        ],
        flops=near_flops,
        limit=8 << 20,
    )
    for sweep_index in range(SWEEPS - 1):
        if sweep_index:
            last = sweep_index == SWEEPS - 2
            state, field, *for_heat = call(
                near_kernel,
                [(whole, F32, VM), (whole, BF16, VM)]
                + [((groups * tiles, points, regimes), F32, VM), (whole, F32, VM)] * last,
                on(SM, ids) + on(VM, packed, field, state, amps, scale),
                "near",
                flops=near_flops,
            )
        token = scale
        if sweep_index == 1:
            edges = call(
                edge_kernel,
                [((ZB, points, regimes), BF16, VM)] * min(2, shifts),
                on(ANY, field) + on(SM, reference_material_kappas) + on(VM, kind, warmth),
                "edge",
            )
            token = edges[0]
        if sweep_index < SWEEPS - 2:
            state, field, *faces = call(
                functools.partial(face_kernel, order),
                [(whole, F32, VM), (whole, BF16, VM)] + [(face, BF16, VM)] * levels,
                on(ANY, token)
                + on(SM, face_ids)
                + on(VM, interface_admittance, scale, *incoming, state, field),
                "face",
                aliases={levels + 4: 0, levels + 5: 1},
                scratch=[terms],
            )
            order = orders[sweep_index]
            incoming = exchange(faces, order)

    if groups == 2:
        below = above = lax.ppermute(edges[0], "therm", [(0, 1), (1, 0)])
    else:
        up = [(i, i + 1) for i in range(groups - 1)]
        above = lax.ppermute(edges[0], "therm", [(j, i) for i, j in up])
        below = lax.ppermute(edges[1], "therm", up)
    heat, diag = for_heat
    _, field, heat, soon, *faces = call(
        functools.partial(heat_kernel, order, early_spots),
        [
            (whole, F32, VM),
            (whole, BF16, VM),
            (heat.shape, F32, VM),
            ((shifts, sent_rows + rows.shape[1], regimes), BF16, VM),
        ]
        + [(face, BF16, VM)] * levels,
        on(ANY, above)
        + on(SM, slot, ids, face_ids)
        + on(VM, interface_admittance, scale, packed, diag, rows, *incoming)
        + on(VM, state, field, heat),
        "heat",
        aliases={9 + levels + n: n for n in range(3)},
        scratch=[terms],
        flops=near_flops,
    )
    routes = [[(i, (i + s) % groups) for i in range(groups)] for s in range(1, groups)]
    soon = [lax.ppermute(soon[s], "therm", routes[s]) for s in range(shifts)]
    maps = [x[sent_rows, :tiles].astype(I32) for x in soon]
    order = far_first
    incoming = exchange(faces, order)

    rest, gain = call(
        functools.partial(conduction_kernel, groups),
        [(warm, F32, VM), (warm, F32, VM)],
        on(SM, warmth_partner_tile_ids.T, reference_material_kappas)
        + on(
            VM,
            warmth_coupling_tiles,
            kind,
            warmth_self_coefficient,
            warmth_storage_per_point,
            layer_boundary_couplings,
            warmth,
            below,
            above,
        )
        + on(ANY, heat),
        "conduction",
        scratch=[pltpu.VMEM(warm, BF16)],
        flops=near_flops,
    )
    heat, field, late = call(
        functools.partial(heat_face_kernel, order),
        [
            ((groups * tiles, points, regimes), F32, VM),
            (whole, BF16, VM),
            ((shifts, late_spots, points, regimes), BF16, VM),
        ],
        on(SM, slot, face_ids) + on(VM, interface_admittance, *incoming, heat, field),
        "heat_face",
        aliases={levels + 3: 0, levels + 4: 1},
        scratch=[terms],
    )
    late = [lax.ppermute(late[s], "therm", routes[s]) for s in range(shifts)]
    rest, voltage_solution, out, *maps = call(
        functools.partial(early_kernel, shifts),
        [(warm, F32, VM), (whole, BF16, VM), (warm, F32, HB)] + [((late_spots,), I32, SM)] * shifts,
        on(VM, heat, gain) + on(SM, *maps) + on(VM, *soon, rest, field),
        "early",
        aliases={2 + 2 * shifts: 0, 3 + 2 * shifts: 1},
        scratch=[dma],
    )
    (advanced_warmth_values,) = call(
        functools.partial(late_kernel, shifts),
        [(warm, F32, HB)],
        on(VM, gain) + on(SM, *maps) + on(VM, *late, rest) + on(HB, out),
        "late",
        aliases={2 + 2 * shifts: 0},
        scratch=[dma((shifts * late_spots,))],
    )
    return (voltage_solution, advanced_warmth_values)


def solution(mesh):
    split = P(("elec", "therm"))
    return jax.shard_map(
        body,
        mesh=mesh,
        in_specs=(split,) * 14 + (P(), split),
        out_specs=(split, split),
        check_vma=False,
    )
```

profile of v0, /device:TPU:0, one launch (start us, length us, event | category | flops | bytes accessed | tf_op | source)
XLA Modules:
  0.0 46.2 jit_solution(9513706340184528873)
XLA Ops:
  0.6 1.3 %start.1 = (bf16[32,64,128]{2,1,0:T(8,128)(2,1)S(1)}, f32[32,64]{1,0:T(8,128)S(1)}, s32[2,4]{1,0:T(2,128)S(4)}, s32[4,32]{1,0:T(4,128)S(4)}, s32[1,32]{1,0:T(1,1...) custom-call(bf16[32,64,128]{2,1,0:T(8,128)(2,1)} %amps.1, ...), custom_call_target="tpu_custom_call" | custom-call | tf_op jit(solution)/shard_map/start/pallas_call | solution.py:33
  2.0 4.1 %collective-permute-start = (bf16[128,128]{1,0:T(8,128)(2,1)S(1)}, bf16[128,128]{1,0:T(8,128)(2,1)S(1)}, u32[]{:S(2)}, u32[]{:S(2)}) collective-permute-start(bf16[128,128]{1,0:T(8,128)(2,1)S(1)} %get-tuple-element.71), channel_id=1, source_target_pairs={{0,16},{16,0},{2,18},{18,2},{4,20},{20,4},{6,22},{22,6},{8,24},{24... | collective-permute-start | bytes 98312 | tf_op jit(solution)/shard_map/ppermute | solution.py:57
  6.1 1.6 %collective-permute-start.1 = (bf16[128,128]{1,0:T(8,128)(2,1)S(1)}, bf16[128,128]{1,0:T(8,128)(2,1)S(1)}, u32[]{:S(2)}, u32[]{:S(2)}) collective-permute-start(bf16[128,128]{1,0:T(8,128)(2,1)S(1)} %get-tuple-element.72), channel_id=1, source_target_pairs={{0,8},{8,0},{2,10},{10,2},{4,12},{12,4},{6,14},{14,6},{16,24},{24,... | collective-permute-start | bytes 98312 | tf_op jit(solution)/shard_map/ppermute | solution.py:57
  7.6 1.5 %collective-permute-start.2 = (bf16[128,128]{1,0:T(8,128)(2,1)S(1)}, bf16[128,128]{1,0:T(8,128)(2,1)S(1)}, u32[]{:S(2)}, u32[]{:S(2)}) collective-permute-start(bf16[128,128]{1,0:T(8,128)(2,1)S(1)} %get-tuple-element.73), channel_id=1, source_target_pairs={{0,4},{4,0},{2,6},{6,2},{8,12},{12,8},{10,14},{14,10},{16,20},{20,... | collective-permute-start | bytes 98312 | tf_op jit(solution)/shard_map/ppermute | solution.py:57
  9.1 2.9 %first.1 = (bf16[32,64,256]{2,1,0:T(8,128)(2,1)S(1)}, f32[32,64,128]{2,1,0:T(8,128)S(1)}, bf16[32,64,128]{2,1,0:T(8,128)(2,1)S(1)}, f32[32,64,128]{2,1,0:T(8,128...) custom-call(s32[4,32]{1,0:T(4,128)S(4)} %get-tuple-element.62.ids, ...), custom_call_target="tpu_custom_call" | custom-call | flops 134217728 | tf_op jit(solution)/shard_map/first/pallas_call | solution.py:33
  13.1 1.4 %collective-permute-start.7 = (bf16[128,128]{1,0:T(8,128)(2,1)S(1)}, bf16[128,128]{1,0:T(8,128)(2,1)S(1)}, u32[]{:S(2)}, u32[]{:S(2)}) collective-permute-start(bf16[128,128]{1,0:T(8,128)(2,1)S(1)} %get-tuple-element.84), channel_id=1, source_target_pairs={{0,4},{4,0},{2,6},{6,2},{8,12},{12,8},{10,14},{14,10},{16,20},{20,... | collective-permute-start | bytes 98312 | tf_op jit(solution)/shard_map/ppermute | solution.py:57
  14.5 0.6 %near.3 = (f32[32,64,128]{2,1,0:T(8,128)S(1)}, bf16[32,64,128]{2,1,0:T(8,128)(2,1)S(1)}) custom-call(s32[4,32]{1,0:T(4,128)S(4)} %get-tuple-element.62.ids, bf16[32,64,256]{2,1,0:T(8,128)(2,1)S(1)} %get-tuple-element.69.packed, bf16[32,64,128]{2,1,0:T(8,128)(2,1)S(1)} %get-tuple-element.77.field, f32[32,64,128]{2,1,0:T(8,128)S(1)} %get-tuple-element.78.state, ...), custom_call_target="tpu_custom_call" | custom-call | flops 134217728 | tf_op jit(solution)/shard_map/near/pallas_call | solution.py:33
  15.2 0.8 %edge.1.token = bf16[2,64,128]{2,1,0:T(8,128)(2,1)S(1)} custom-call(bf16[32,64,128]{2,1,0:T(8,128)(2,1)S(1)} %get-tuple-element.79.token.refs_5_, f32[8]{0:T(128)S(1)} %copy-done.6, s32[32,64]{1,0:T(8,128)S(1)} %get-tuple-element.80.kind, bf16[32,64,128]{2,1,0:T(8,128)(2,1)S(1)} %get-tuple-element.81.warmth), custom_call_target="tpu_custom_call" | custom-call | tf_op jit(solution)/shard_map/edge/pallas_call | solution.py:33
  15.9 1.5 %collective-permute-done.5.refs_0_ = bf16[128,128]{1,0:T(8,128)(2,1)S(1)} collective-permute-done((bf16[128,128]{1,0:T(8,128)(2,1)S(1)}, bf16[128,128]{1,0:T(8,128)(2,1)S(1)}, u32[]{:S(2)}, u32[]{:S(2)}) %collective-permute-start.5) | collective-permute-done | bytes 32800 | tf_op jit(solution)/shard_map/ppermute | solution.py:57
  17.6 2.3 %collective-permute-start.9 = (bf16[128,128]{1,0:T(8,128)(2,1)S(1)}, bf16[128,128]{1,0:T(8,128)(2,1)S(1)}, u32[]{:S(2)}, u32[]{:S(2)}) collective-permute-start(bf16[128,128]{1,0:T(8,128)(2,1)S(1)} %get-tuple-element.87), channel_id=1, source_target_pairs={{0,16},{16,0},{2,18},{18,2},{4,20},{20,4},{6,22},{22,6},{8,24},{24... | collective-permute-start | bytes 98312 | tf_op jit(solution)/shard_map/ppermute | solution.py:57
  19.9 1.0 %collective-permute-start.10 = (bf16[128,128]{1,0:T(8,128)(2,1)S(1)}, bf16[128,128]{1,0:T(8,128)(2,1)S(1)}, u32[]{:S(2)}, u32[]{:S(2)}) collective-permute-start(bf16[128,128]{1,0:T(8,128)(2,1)S(1)} %get-tuple-element.88), channel_id=1, source_target_pairs={{0,4},{4,0},{2,6},{6,2},{8,12},{12,8},{10,14},{14,10},{16,20},{20,... | collective-permute-start | bytes 98312 | tf_op jit(solution)/shard_map/ppermute | solution.py:57
  20.9 1.6 %collective-permute-start.11 = (bf16[128,128]{1,0:T(8,128)(2,1)S(1)}, bf16[128,128]{1,0:T(8,128)(2,1)S(1)}, u32[]{:S(2)}, u32[]{:S(2)}) collective-permute-start(bf16[128,128]{1,0:T(8,128)(2,1)S(1)} %get-tuple-element.89), channel_id=1, source_target_pairs={{0,8},{8,0},{2,10},{10,2},{4,12},{12,4},{6,14},{14,6},{16,24},{24,... | collective-permute-start | bytes 98312 | tf_op jit(solution)/shard_map/ppermute | solution.py:57
  22.5 1.5 %collective-permute-start.4 = (bf16[2,64,128]{2,1,0:T(8,128)(2,1)S(1)}, bf16[2,64,128]{2,1,0:T(8,128)(2,1)S(1)}, u32[]{:S(2)}, u32[]{:S(2)}) collective-permute-start(bf16[2,64,128]{2,1,0:T(8,128)(2,1)S(1)} %edge.1.token), channel_id=1, source_target_pairs={{0,1},{1,0},{2,3},{3,2},{4,5},{5,4},{6,7},{7,6},{8,9},{9,8},{10,11... | collective-permute-start | bytes 98312 | tf_op jit(solution)/shard_map/ppermute | solution.py:534
  24.0 0.6 %near.4 = (f32[32,64,128]{2,1,0:T(8,128)S(1)}, bf16[32,64,128]{2,1,0:T(8,128)(2,1)S(1)}) custom-call(s32[4,32]{1,0:T(4,128)S(4)} %get-tuple-element.62.ids, bf16[32,64,256]{2,1,0:T(8,128)(2,1)S(1)} %get-tuple-element.69.packed, bf16[32,64,128]{2,1,0:T(8,128)(2,1)S(1)} %get-tuple-element.91.field, f32[32,64,128]{2,1,0:T(8,128)S(1)} %get-tuple-element.92.state, ...), custom_call_target="tpu_custom_call" | custom-call | flops 134217728 | tf_op jit(solution)/shard_map/near/pallas_call | solution.py:33
  25.0 1.6 %collective-permute-start.13 = (bf16[128,128]{1,0:T(8,128)(2,1)S(1)}, bf16[128,128]{1,0:T(8,128)(2,1)S(1)}, u32[]{:S(2)}, u32[]{:S(2)}) collective-permute-start(bf16[128,128]{1,0:T(8,128)(2,1)S(1)} %get-tuple-element.99), channel_id=1, source_target_pairs={{0,8},{8,0},{2,10},{10,2},{4,12},{12,4},{6,14},{14,6},{16,24},{24,... | collective-permute-start | bytes 98312 | tf_op jit(solution)/shard_map/ppermute | solution.py:57
  26.7 1.0 %collective-permute-start.14 = (bf16[128,128]{1,0:T(8,128)(2,1)S(1)}, bf16[128,128]{1,0:T(8,128)(2,1)S(1)}, u32[]{:S(2)}, u32[]{:S(2)}) collective-permute-start(bf16[128,128]{1,0:T(8,128)(2,1)S(1)} %get-tuple-element.100), channel_id=1, source_target_pairs={{0,4},{4,0},{2,6},{6,2},{8,12},{12,8},{10,14},{14,10},{16,20},{20,... | collective-permute-start | bytes 98312 | tf_op jit(solution)/shard_map/ppermute | solution.py:57
  27.7 0.5 collective-permute-start.15
  28.2 0.9 %near.5 = (f32[32,64,128]{2,1,0:T(8,128)S(1)}, bf16[32,64,128]{2,1,0:T(8,128)(2,1)S(1)}, f32[64,64,128]{2,1,0:T(8,128)S(1)}, f32[32,64,128]{2,1,0:T(8,128)S(1)}) custom-call(s32[4,32]{1,0:T(4,128)S(4)} %get-tuple-element.62.ids, bf16[32,64,256]{2,1,0:T(8,128)(2,1)S(1)} %get-tuple-element.69.packed, bf16[32,64,128]{2,1,0:T(8,128)(2,1)S(1)} %get-tuple-element.95.field, ...), custom_call_target="tpu_custom_call" | custom-call | flops 134217728 | tf_op jit(solution)/shard_map/near/pallas_call | solution.py:33
  29.1 1.5 %collective-permute-done.14.refs_1_ = bf16[128,128]{1,0:T(8,128)(2,1)S(1)} collective-permute-done((bf16[128,128]{1,0:T(8,128)(2,1)S(1)}, bf16[128,128]{1,0:T(8,128)(2,1)S(1)}, u32[]{:S(2)}, u32[]{:S(2)}) %collective-permute-start.14) | collective-permute-done | bytes 32800 | tf_op jit(solution)/shard_map/ppermute | solution.py:57
  30.6 2.2 %collective-permute-done.15.refs_2_ = bf16[128,128]{1,0:T(8,128)(2,1)S(1)} collective-permute-done((bf16[128,128]{1,0:T(8,128)(2,1)S(1)}, bf16[128,128]{1,0:T(8,128)(2,1)S(1)}, u32[]{:S(2)}, u32[]{:S(2)}) %collective-permute-start.15) | collective-permute-done | bytes 32800 | tf_op jit(solution)/shard_map/ppermute | solution.py:57
  32.8 0.8 %heat.1 = (f32[32,64,128]{2,1,0:T(8,128)S(1)}, bf16[32,64,128]{2,1,0:T(8,128)(2,1)S(1)}, f32[64,64,128]{2,1,0:T(8,128)S(1)}, bf16[1,1552,128]{2,1,0:T(8,128)(2,1...) custom-call(bf16[2,64,128]{2,1,0:T(8,128)(2,1)S(1)} %collective-perm, ...), custom_call_target="tpu_custom_call", output_to_operand_aliasing={{0}: (13, {}), {1}: (14, {}), {2}: (15, {})} | custom-call | flops 134217728 | tf_op jit(solution)/shard_map/heat/pallas_call | solution.py:33
  33.6 1.6 %collective-permute-start.21 = (bf16[1552,128]{1,0:T(8,128)(2,1)S(1)}, bf16[1552,128]{1,0:T(8,128)(2,1)S(1)}, u32[]{:S(2)}, u32[]{:S(2)}) collective-permute-start(bf16[1552,128]{1,0:T(8,128)(2,1)S(1)} %bitcast.12), channel_id=1, source_target_pairs={{0,1},{1,0},{2,3},{3,2},{4,5},{5,4},{6,7},{7,6},{8,9},{9,8},{10,11... | collective-permute-start | bytes 1191944 | tf_op jit(solution)/shard_map/ppermute | solution.py:559
  35.4 0.7 %collective-permute-start.18 = (bf16[128,128]{1,0:T(8,128)(2,1)S(1)}, bf16[128,128]{1,0:T(8,128)(2,1)S(1)}, u32[]{:S(2)}, u32[]{:S(2)}) collective-permute-start(bf16[128,128]{1,0:T(8,128)(2,1)S(1)} %get-tuple-element.107), channel_id=1, source_target_pairs={{0,8},{8,0},{2,10},{10,2},{4,12},{12,4},{6,14},{14,6},{16,24},{24,... | collective-permute-start | bytes 98312 | tf_op jit(solution)/shard_map/ppermute | solution.py:57
  36.1 1.1 %collective-permute-start.19 = (bf16[128,128]{1,0:T(8,128)(2,1)S(1)}, bf16[128,128]{1,0:T(8,128)(2,1)S(1)}, u32[]{:S(2)}, u32[]{:S(2)}) collective-permute-start(bf16[128,128]{1,0:T(8,128)(2,1)S(1)} %get-tuple-element.108), channel_id=1, source_target_pairs={{0,4},{4,0},{2,6},{6,2},{8,12},{12,8},{10,14},{14,10},{16,20},{20,... | collective-permute-start | bytes 98312 | tf_op jit(solution)/shard_map/ppermute | solution.py:57
  37.2 1.9 %conduction.1 = (f32[32,64,128]{2,1,0:T(8,128)S(1)}, f32[32,64,128]{2,1,0:T(8,128)S(1)}) custom-call(s32[3,32]{1,0:T(4,128)S(1)} %bitcast.11, f32[8]{0:T(128)S(1)} %copy-done.6, bf16[32,3,64,64]{3,2,1,0:T(8,128)(2,1)S(1)} %copy-done.1, s32[32,64]{1,0:T(8,128)S(1)} %get-tuple-element.80.kind, f32[32,64]{1,0:T(8,128)S(1)} %copy-done.3, ...), custom_call_target="tpu_custom_call" | custom-call | flops 134217728 | tf_op jit(solution)/shard_map/conduction/pallas_call | solution.py:33
  39.2 0.9 %collective-permute-done.17.refs_0_ = bf16[128,128]{1,0:T(8,128)(2,1)S(1)} collective-permute-done((bf16[128,128]{1,0:T(8,128)(2,1)S(1)}, bf16[128,128]{1,0:T(8,128)(2,1)S(1)}, u32[]{:S(2)}, u32[]{:S(2)}) %collective-permute-start.17) | collective-permute-done | bytes 32800 | tf_op jit(solution)/shard_map/ppermute | solution.py:57
  40.3 0.6 %collective-permute-start.22 = (bf16[8,64,128]{2,1,0:T(8,128)(2,1)S(1)}, bf16[8,64,128]{2,1,0:T(8,128)(2,1)S(1)}, u32[]{:S(2)}, u32[]{:S(2)}) collective-permute-start(bf16[8,64,128]{2,1,0:T(8,128)(2,1)S(1)} %bitcast.13), channel_id=1, source_target_pairs={{0,1},{1,0},{2,3},{3,2},{4,5},{5,4},{6,7},{7,6},{8,9},{9,8},{10,11... | collective-permute-start | bytes 393224 | tf_op jit(solution)/shard_map/ppermute | solution.py:596
  40.9 0.9 %collective-permute-done.21.refs_1_ = bf16[1552,128]{1,0:T(8,128)(2,1)S(1)} collective-permute-done((bf16[1552,128]{1,0:T(8,128)(2,1)S(1)}, bf16[1552,128]{1,0:T(8,128)(2,1)S(1)}, u32[]{:S(2)}, u32[]{:S(2)}) %collective-permute-start.21) | collective-permute-done | bytes 397344 | tf_op jit(solution)/shard_map/ppermute | solution.py:559
  41.8 1.8 %early.1 = (f32[32,64,128]{2,1,0:T(8,128)S(1)}, bf16[32,64,128]{2,1,0:T(8,128)(2,1)S(1)}, f32[32,64,128]{2,1,0:T(8,128)}, s32[8]{0:T(128)S(4)}) custom-call(f32[64,64,128]{2,1,0:T(8,128)S(1)} %get-tuple-element.112.heat, f32[32,64,128]{2,1,0:T(8,128)S(1)} %get-tuple-element.113.gain, ...), custom_call_target="tpu_custom_call", output_to_operand_aliasing={{0}: (4, {}), {1}: (5, {})} | custom-call | tf_op jit(solution)/shard_map/early/pallas_call | solution.py:33
  43.6 0.8 %copy.46 = bf16[32,64,128]{2,1,0:T(8,128)(2,1)} copy(bf16[32,64,128]{2,1,0:T(8,128)(2,1)S(1)} %get-tuple-element.122) | data formatting | bytes 1048576
  44.4 1.0 %collective-permute-done.22.refs_1_ = bf16[8,64,128]{2,1,0:T(8,128)(2,1)S(1)} collective-permute-done((bf16[8,64,128]{2,1,0:T(8,128)(2,1)S(1)}, bf16[8,64,128]{2,1,0:T(8,128)(2,1)S(1)}, u32[]{:S(2)}, u32[]{:S(2)}) %collective-permute-start.22) | collective-permute-done | bytes 131104 | tf_op jit(solution)/shard_map/ppermute | solution.py:596
  45.4 0.8 %late.1 = f32[32,64,128]{2,1,0:T(8,128)} custom-call(f32[32,64,128]{2,1,0:T(8,128)S(1)} %get-tuple-element.113.gain, s32[8]{0:T(128)S(4)} %get-tuple-element.118.refs_0_, bf16[8,64,128]{2,1,0:T(8,128)(2,1)S(1)} %collective-permute-done.22.refs_1_, f32[32,64,128]{2,1,0:T(8,128)S(1)} %get-tuple-element.120.refs_2_, ...), custom_call_target="tpu_custom_call", output_to_operand_aliasing={{}: (4, {})} | custom-call | tf_op jit(solution)/shard_map/late/pallas_call | solution.py:33
  (44 shorter events, 2.1 us)
Async XLA Ops:
  0.6 11.4 %copy-start = (bf16[8,64,64]{2,1,0:T(8,128)(2,1)S(1)}, bf16[8,64,64]{2,1,0:T(8,128)(2,1)}, u32[]{:S(2)}) copy-start(bf16[8,64,64]{2,1,0:T(8,128)(2,1)} %admittance.9) | copy-start | bytes 196612
  2.0 10.0 %collective-permute-start = (bf16[128,128]{1,0:T(8,128)(2,1)S(1)}, bf16[128,128]{1,0:T(8,128)(2,1)S(1)}, u32[]{:S(2)}, u32[]{:S(2)}) collective-permute-start(bf16[128,128]{1,0:T(8,128)(2,1)S(1)} %get-tuple-element.71), channel_id=1, source_target_pairs={{0,16},{16,0},{2,18},{18,2},{4,20},{20,4},{6,22},{22,6},{8,24},{24... | collective-permute-start | bytes 98312 | tf_op jit(solution)/shard_map/ppermute | solution.py:57
  6.1 6.0 %collective-permute-start.1 = (bf16[128,128]{1,0:T(8,128)(2,1)S(1)}, bf16[128,128]{1,0:T(8,128)(2,1)S(1)}, u32[]{:S(2)}, u32[]{:S(2)}) collective-permute-start(bf16[128,128]{1,0:T(8,128)(2,1)S(1)} %get-tuple-element.72), channel_id=1, source_target_pairs={{0,8},{8,0},{2,10},{10,2},{4,12},{12,4},{6,14},{14,6},{16,24},{24,... | collective-permute-start | bytes 98312 | tf_op jit(solution)/shard_map/ppermute | solution.py:57
  7.6 4.4 %collective-permute-start.2 = (bf16[128,128]{1,0:T(8,128)(2,1)S(1)}, bf16[128,128]{1,0:T(8,128)(2,1)S(1)}, u32[]{:S(2)}, u32[]{:S(2)}) collective-permute-start(bf16[128,128]{1,0:T(8,128)(2,1)S(1)} %get-tuple-element.73), channel_id=1, source_target_pairs={{0,4},{4,0},{2,6},{6,2},{8,12},{12,8},{10,14},{14,10},{16,20},{20,... | collective-permute-start | bytes 98312 | tf_op jit(solution)/shard_map/ppermute | solution.py:57
  9.1 2.9 %collective-permute-start.3 = (bf16[128,128]{1,0:T(8,128)(2,1)S(1)}, bf16[128,128]{1,0:T(8,128)(2,1)S(1)}, u32[]{:S(2)}, u32[]{:S(2)}) collective-permute-start(bf16[128,128]{1,0:T(8,128)(2,1)S(1)} %get-tuple-element.74), channel_id=1, source_target_pairs={{0,2},{2,0},{4,6},{6,4},{8,10},{10,8},{12,14},{14,12},{16,18},{18,... | collective-permute-start | bytes 98312 | tf_op jit(solution)/shard_map/ppermute | solution.py:57
  12.3 5.1 %collective-permute-start.5 = (bf16[128,128]{1,0:T(8,128)(2,1)S(1)}, bf16[128,128]{1,0:T(8,128)(2,1)S(1)}, u32[]{:S(2)}, u32[]{:S(2)}) collective-permute-start(bf16[128,128]{1,0:T(8,128)(2,1)S(1)} %get-tuple-element.82), channel_id=1, source_target_pairs={{0,16},{16,0},{2,18},{18,2},{4,20},{20,4},{6,22},{22,6},{8,24},{24... | collective-permute-start | bytes 98312 | tf_op jit(solution)/shard_map/ppermute | solution.py:57
  12.7 4.7 %collective-permute-start.6 = (bf16[128,128]{1,0:T(8,128)(2,1)S(1)}, bf16[128,128]{1,0:T(8,128)(2,1)S(1)}, u32[]{:S(2)}, u32[]{:S(2)}) collective-permute-start(bf16[128,128]{1,0:T(8,128)(2,1)S(1)} %get-tuple-element.83), channel_id=1, source_target_pairs={{0,8},{8,0},{2,10},{10,2},{4,12},{12,4},{6,14},{14,6},{16,24},{24,... | collective-permute-start | bytes 98312 | tf_op jit(solution)/shard_map/ppermute | solution.py:57
  13.1 4.3 %collective-permute-start.7 = (bf16[128,128]{1,0:T(8,128)(2,1)S(1)}, bf16[128,128]{1,0:T(8,128)(2,1)S(1)}, u32[]{:S(2)}, u32[]{:S(2)}) collective-permute-start(bf16[128,128]{1,0:T(8,128)(2,1)S(1)} %get-tuple-element.84), channel_id=1, source_target_pairs={{0,4},{4,0},{2,6},{6,2},{8,12},{12,8},{10,14},{14,10},{16,20},{20,... | collective-permute-start | bytes 98312 | tf_op jit(solution)/shard_map/ppermute | solution.py:57
  14.5 2.9 %collective-permute-start.8 = (bf16[128,128]{1,0:T(8,128)(2,1)S(1)}, bf16[128,128]{1,0:T(8,128)(2,1)S(1)}, u32[]{:S(2)}, u32[]{:S(2)}) collective-permute-start(bf16[128,128]{1,0:T(8,128)(2,1)S(1)} %get-tuple-element.85), channel_id=1, source_target_pairs={{0,2},{2,0},{4,6},{6,4},{8,10},{10,8},{12,14},{14,12},{16,18},{18,... | collective-permute-start | bytes 98312 | tf_op jit(solution)/shard_map/ppermute | solution.py:57
  14.5 0.7 %copy-start.6 = (f32[8]{0:T(128)S(1)}, f32[8]{0:T(128)}, u32[]{:S(2)}) copy-start(f32[8]{0:T(128)} %kappas.3) | copy-start | bytes 100
  17.6 7.0 %collective-permute-start.9 = (bf16[128,128]{1,0:T(8,128)(2,1)S(1)}, bf16[128,128]{1,0:T(8,128)(2,1)S(1)}, u32[]{:S(2)}, u32[]{:S(2)}) collective-permute-start(bf16[128,128]{1,0:T(8,128)(2,1)S(1)} %get-tuple-element.87), channel_id=1, source_target_pairs={{0,16},{16,0},{2,18},{18,2},{4,20},{20,4},{6,22},{22,6},{8,24},{24... | collective-permute-start | bytes 98312 | tf_op jit(solution)/shard_map/ppermute | solution.py:57
  19.9 4.7 %collective-permute-start.10 = (bf16[128,128]{1,0:T(8,128)(2,1)S(1)}, bf16[128,128]{1,0:T(8,128)(2,1)S(1)}, u32[]{:S(2)}, u32[]{:S(2)}) collective-permute-start(bf16[128,128]{1,0:T(8,128)(2,1)S(1)} %get-tuple-element.88), channel_id=1, source_target_pairs={{0,4},{4,0},{2,6},{6,2},{8,12},{12,8},{10,14},{14,10},{16,20},{20,... | collective-permute-start | bytes 98312 | tf_op jit(solution)/shard_map/ppermute | solution.py:57
  20.9 3.9 %collective-permute-start.11 = (bf16[128,128]{1,0:T(8,128)(2,1)S(1)}, bf16[128,128]{1,0:T(8,128)(2,1)S(1)}, u32[]{:S(2)}, u32[]{:S(2)}) collective-permute-start(bf16[128,128]{1,0:T(8,128)(2,1)S(1)} %get-tuple-element.89), channel_id=1, source_target_pairs={{0,8},{8,0},{2,10},{10,2},{4,12},{12,4},{6,14},{14,6},{16,24},{24,... | collective-permute-start | bytes 98312 | tf_op jit(solution)/shard_map/ppermute | solution.py:57
  22.5 2.3 %collective-permute-start.12 = (bf16[128,128]{1,0:T(8,128)(2,1)S(1)}, bf16[128,128]{1,0:T(8,128)(2,1)S(1)}, u32[]{:S(2)}, u32[]{:S(2)}) collective-permute-start(bf16[128,128]{1,0:T(8,128)(2,1)S(1)} %get-tuple-element.90), channel_id=1, source_target_pairs={{0,2},{2,0},{4,6},{6,4},{8,10},{10,8},{12,14},{14,12},{16,18},{18,... | collective-permute-start | bytes 98312 | tf_op jit(solution)/shard_map/ppermute | solution.py:57
  22.5 6.6 %collective-permute-start.4 = (bf16[2,64,128]{2,1,0:T(8,128)(2,1)S(1)}, bf16[2,64,128]{2,1,0:T(8,128)(2,1)S(1)}, u32[]{:S(2)}, u32[]{:S(2)}) collective-permute-start(bf16[2,64,128]{2,1,0:T(8,128)(2,1)S(1)} %edge.1.token), channel_id=1, source_target_pairs={{0,1},{1,0},{2,3},{3,2},{4,5},{5,4},{6,7},{7,6},{8,9},{9,8},{10,11... | collective-permute-start | bytes 98312 | tf_op jit(solution)/shard_map/ppermute | solution.py:534
  25.0 4.0 %collective-permute-start.13 = (bf16[128,128]{1,0:T(8,128)(2,1)S(1)}, bf16[128,128]{1,0:T(8,128)(2,1)S(1)}, u32[]{:S(2)}, u32[]{:S(2)}) collective-permute-start(bf16[128,128]{1,0:T(8,128)(2,1)S(1)} %get-tuple-element.99), channel_id=1, source_target_pairs={{0,8},{8,0},{2,10},{10,2},{4,12},{12,4},{6,14},{14,6},{16,24},{24,... | collective-permute-start | bytes 98312 | tf_op jit(solution)/shard_map/ppermute | solution.py:57
  26.7 3.9 %collective-permute-start.14 = (bf16[128,128]{1,0:T(8,128)(2,1)S(1)}, bf16[128,128]{1,0:T(8,128)(2,1)S(1)}, u32[]{:S(2)}, u32[]{:S(2)}) collective-permute-start(bf16[128,128]{1,0:T(8,128)(2,1)S(1)} %get-tuple-element.100), channel_id=1, source_target_pairs={{0,4},{4,0},{2,6},{6,2},{8,12},{12,8},{10,14},{14,10},{16,20},{20,... | collective-permute-start | bytes 98312 | tf_op jit(solution)/shard_map/ppermute | solution.py:57
  27.7 5.1 %collective-permute-start.15 = (bf16[128,128]{1,0:T(8,128)(2,1)S(1)}, bf16[128,128]{1,0:T(8,128)(2,1)S(1)}, u32[]{:S(2)}, u32[]{:S(2)}) collective-permute-start(bf16[128,128]{1,0:T(8,128)(2,1)S(1)} %get-tuple-element.101), channel_id=1, source_target_pairs={{0,16},{16,0},{2,18},{18,2},{4,20},{20,4},{6,22},{22,6},{8,24},{24... | collective-permute-start | bytes 98312 | tf_op jit(solution)/shard_map/ppermute | solution.py:57
  28.2 4.6 %collective-permute-start.16 = (bf16[128,128]{1,0:T(8,128)(2,1)S(1)}, bf16[128,128]{1,0:T(8,128)(2,1)S(1)}, u32[]{:S(2)}, u32[]{:S(2)}) collective-permute-start(bf16[128,128]{1,0:T(8,128)(2,1)S(1)} %get-tuple-element.102), channel_id=1, source_target_pairs={{0,2},{2,0},{4,6},{6,4},{8,10},{10,8},{12,14},{14,12},{16,18},{18,... | collective-permute-start | bytes 98312 | tf_op jit(solution)/shard_map/ppermute | solution.py:57
  32.8 4.4 %copy-start.1 = (bf16[32,3,64,64]{3,2,1,0:T(8,128)(2,1)S(1)}, bf16[32,3,64,64]{3,2,1,0:T(8,128)(2,1)}, u32[]{:S(2)}) copy-start(bf16[32,3,64,64]{3,2,1,0:T(8,128)(2,1)} %tiles.3) | copy-start | bytes 2359300
  32.8 4.4 %copy-start.2 = (bf16[4,64,64]{2,1,0:T(8,128)(2,1)S(1)}, bf16[4,64,64]{2,1,0:T(8,128)(2,1)}, u32[]{:S(2)}) copy-start(bf16[4,64,64]{2,1,0:T(8,128)(2,1)} %couplings.1) | copy-start | bytes 98308
  32.8 4.4 %copy-start.3 = (f32[32,64]{1,0:T(8,128)S(1)}, f32[32,64]{1,0:T(8,128)}, u32[]{:S(2)}) copy-start(f32[32,64]{1,0:T(8,128)} %coefficient.1) | copy-start | bytes 24580
  32.8 4.4 %copy-start.4 = (f32[32,64]{1,0:T(8,128)S(1)}, f32[32,64]{1,0:T(8,128)}, u32[]{:S(2)}) copy-start(f32[32,64]{1,0:T(8,128)} %storage.1) | copy-start | bytes 24580
  32.8 4.4 %copy-start.5 = (s32[32,3]{0,1:T(4,128)S(1)}, s32[32,3]{0,1:T(4,128)}, u32[]{:S(2)}) copy-start(s32[32,3]{0,1:T(4,128)} %param.27) | copy-start | bytes 1156
  33.6 8.2 %collective-permute-start.21 = (bf16[1552,128]{1,0:T(8,128)(2,1)S(1)}, bf16[1552,128]{1,0:T(8,128)(2,1)S(1)}, u32[]{:S(2)}, u32[]{:S(2)}) collective-permute-start(bf16[1552,128]{1,0:T(8,128)(2,1)S(1)} %bitcast.12), channel_id=1, source_target_pairs={{0,1},{1,0},{2,3},{3,2},{4,5},{5,4},{6,7},{7,6},{8,9},{9,8},{10,11... | collective-permute-start | bytes 1191944 | tf_op jit(solution)/shard_map/ppermute | solution.py:559
  35.2 4.8 %collective-permute-start.17 = (bf16[128,128]{1,0:T(8,128)(2,1)S(1)}, bf16[128,128]{1,0:T(8,128)(2,1)S(1)}, u32[]{:S(2)}, u32[]{:S(2)}) collective-permute-start(bf16[128,128]{1,0:T(8,128)(2,1)S(1)} %get-tuple-element.106), channel_id=1, source_target_pairs={{0,16},{16,0},{2,18},{18,2},{4,20},{20,4},{6,22},{22,6},{8,24},{24... | collective-permute-start | bytes 98312 | tf_op jit(solution)/shard_map/ppermute | solution.py:57
  35.4 4.6 %collective-permute-start.18 = (bf16[128,128]{1,0:T(8,128)(2,1)S(1)}, bf16[128,128]{1,0:T(8,128)(2,1)S(1)}, u32[]{:S(2)}, u32[]{:S(2)}) collective-permute-start(bf16[128,128]{1,0:T(8,128)(2,1)S(1)} %get-tuple-element.107), channel_id=1, source_target_pairs={{0,8},{8,0},{2,10},{10,2},{4,12},{12,4},{6,14},{14,6},{16,24},{24,... | collective-permute-start | bytes 98312 | tf_op jit(solution)/shard_map/ppermute | solution.py:57
  36.1 3.9 %collective-permute-start.19 = (bf16[128,128]{1,0:T(8,128)(2,1)S(1)}, bf16[128,128]{1,0:T(8,128)(2,1)S(1)}, u32[]{:S(2)}, u32[]{:S(2)}) collective-permute-start(bf16[128,128]{1,0:T(8,128)(2,1)S(1)} %get-tuple-element.108), channel_id=1, source_target_pairs={{0,4},{4,0},{2,6},{6,2},{8,12},{12,8},{10,14},{14,10},{16,20},{20,... | collective-permute-start | bytes 98312 | tf_op jit(solution)/shard_map/ppermute | solution.py:57
  37.2 2.9 %collective-permute-start.20 = (bf16[128,128]{1,0:T(8,128)(2,1)S(1)}, bf16[128,128]{1,0:T(8,128)(2,1)S(1)}, u32[]{:S(2)}, u32[]{:S(2)}) collective-permute-start(bf16[128,128]{1,0:T(8,128)(2,1)S(1)} %get-tuple-element.109), channel_id=1, source_target_pairs={{0,2},{2,0},{4,6},{6,4},{8,10},{10,8},{12,14},{14,12},{16,18},{18,... | collective-permute-start | bytes 98312 | tf_op jit(solution)/shard_map/ppermute | solution.py:57
  40.3 5.1 %collective-permute-start.22 = (bf16[8,64,128]{2,1,0:T(8,128)(2,1)S(1)}, bf16[8,64,128]{2,1,0:T(8,128)(2,1)S(1)}, u32[]{:S(2)}, u32[]{:S(2)}) collective-permute-start(bf16[8,64,128]{2,1,0:T(8,128)(2,1)S(1)} %bitcast.13), channel_id=1, source_target_pairs={{0,1},{1,0},{2,3},{3,2},{4,5},{5,4},{6,7},{7,6},{8,9},{9,8},{10,11... | collective-permute-start | bytes 393224 | tf_op jit(solution)/shard_map/ppermute | solution.py:596
where the time goes:
time: 46.4 us; the launch traced here: 46.2 us
  starting transfers between devices  23 us (50%)
  Pallas kernels  13.3 us (29%)
  waiting for transfers between devices  8.17 us (18%)
  between operations  0.89 us (2%)
  local copies, waits for them, and re-layouts  0.84 us (2%)
    ppermute x20, starting transfers between devices, from_partner(): return lax.ppermute(block, axis, route)  19.4 us
    pallas_call x14, Pallas kernels, call(): pl.pallas_call(kernel, out_shape=[SPACES[id(spec)](shape, dtype) for shap...  13.3 us
    ppermute x20, waiting for transfers between devices, from_partner(): return lax.ppermute(block, axis, route)  6.26 us
    ppermute x1, starting transfers between devices, body(): soon = [lax.ppermute(soon[s], 'therm', routes[s]) for s in range(shifts)]  1.58 us
    ppermute x1, starting transfers between devices, body(): below = above = lax.ppermute(edges[0], 'therm', [(0, 1), (1, 0)])  1.52 us
    ppermute x1, waiting for transfers between devices, body(): late = [lax.ppermute(late[s], 'therm', routes[s]) for s in range(shifts)]  0.97 us
    ppermute x1, waiting for transfers between devices, body(): soon = [lax.ppermute(soon[s], 'therm', routes[s]) for s in range(shifts)]  0.93 us
  transfers between devices with their start and end apart: 23, of which 7 were waited for; matrix products, arithmetic and copies ran while one was open for 2% of the time, Pallas kernels for 21%

commit v1 on v0

--- a/solution.py
+++ b/solution.py
@@ -146,6 +146,15 @@
             behind = behind + (is_early & jnp.logical_not(fits)).astype(I32)
             return at, behind, row
 
+        def spare(j, c):
+            at, behind, row = c
+            free = flag[j] == 0
+            fits = at < early_slots
+            row = jnp.where((lane == jnp.where(fits, at, behind)) & free, j, row)
+            at = at + (free & fits).astype(I32)
+            behind = behind + (free & jnp.logical_not(fits)).astype(I32)
+            return at, behind, row
+
         def assign(i, c):
             slot[i] = jnp.where(away(i) == g, g * tiles + place[tile[i]], slot[i])
             return c
@@ -158,9 +167,8 @@
                 j = tile[i]
                 flag[j] = jnp.where(away(i) == g, 2, flag[j])
         behind = lax.fori_loop(0, tiles, late, early_slots)
-        _, _, row = lax.fori_loop(
-            0, tiles, early, (0, behind, jnp.zeros(rows.shape[1:], I32))
-        )
+        filled = lax.fori_loop(0, tiles, early, (0, behind, jnp.zeros(rows.shape[1:], I32)))
+        _, _, row = lax.fori_loop(0, tiles, spare, filled)
         lax.fori_loop(0, blocks, assign, 0)
         rows[g - 1] = row.astype(F32).astype(BF16)
 
@@ -306,43 +314,37 @@
     return (kappa * (1.0 + 0.4 * jnp.tanh(w)) * w).astype(BF16)
 
 
-def edge_kernel(token, kappas, kind, warmth, *edges):
+def flux_kernel(token, kappas, kind, warmth, flux, *edges):
     turned = kappa_columns(kappas, kind)
     tiles, points, width = warmth.shape
+    for i in range(tiles):
+        flux[i] = block_flux(column(turned, i, width), warmth[i])
     sends_top = lax.axis_index("therm") == 0
     for z in range(ZB):
         top = tiles - ZB + z
-        low = block_flux(column(turned, z, width), warmth[z])
-        high = block_flux(column(turned, top, width), warmth[top])
         if len(edges) == 1:
-            both = jnp.where(sends_top, high.astype(F32), low.astype(F32))
-            edges[0][z] = both.astype(BF16)
+            edges[0][z] = flux[jnp.where(sends_top, top, z)]
         else:
-            edges[0][z], edges[1][z] = low, high
+            edges[0][z], edges[1][z] = flux[z], flux[top]
 
 
 def conduction_kernel(
     groups,
     ids,
-    kappas,
     tiles,
-    kind,
     coefficient,
     storage,
     couplings,
     warmth,
+    flux,
     below,
     above,
     heat,
     rest,
     gain,
-    flux,
 ):
     count = tiles.shape[0]
     width = flux.shape[2]
-    turned = kappa_columns(kappas, kind)
-    for i in range(count):
-        flux[i] = block_flux(column(turned, i, width), warmth[i])
     own = lax.axis_index("therm")
     lowest = (own > 0).astype(F32)
     highest = (own < groups - 1).astype(F32)
@@ -385,19 +387,27 @@
 
 def late_kernel(shifts, gain, *refs):
     maps, late = refs[:shifts], refs[shifts : 2 * shifts]
-    rest, out, sems = refs[2 * shifts], refs[2 * shifts + 2], refs[2 * shifts + 3]
+    rest, out = refs[2 * shifts], refs[2 * shifts + 2]
+    ready, sems = refs[2 * shifts + 3 :]
     spots = late[0].shape[0]
-    for g in range(shifts):
+    copies = []
+    if shifts == 1:
         for p in range(spots):
-            j = maps[g][p]
-            rest[j] = rest[j] + gain[j] * late[g][p].astype(F32)
-    copies = []
-    for g in range(shifts):
-        for p in range(spots):
-            j = maps[g][p]
-            copies.append(pltpu.make_async_copy(rest.at[j], out.at[j], sems.at[g * spots + p]))
-    for c in copies:
-        c.start()
+            j = maps[0][p]
+            ready[p] = rest[j] + gain[j] * late[0][p].astype(F32)
+            copies.append(pltpu.make_async_copy(ready.at[p], out.at[j], sems.at[p]))
+            copies[-1].start()
+    else:
+        for g in range(shifts):
+            for p in range(spots):
+                j = maps[g][p]
+                rest[j] = rest[j] + gain[j] * late[g][p].astype(F32)
+        for g in range(shifts):
+            for p in range(spots):
+                j = maps[g][p]
+                copy = pltpu.make_async_copy(rest.at[j], out.at[j], sems.at[g * spots + p])
+                copy.start()
+                copies.append(copy)
     for c in copies:
         c.wait()
 
@@ -509,11 +519,11 @@
             )
         token = scale
         if sweep_index == 1:
-            edges = call(
-                edge_kernel,
-                [((ZB, points, regimes), BF16, VM)] * min(2, shifts),
+            flux, *edges = call(
+                flux_kernel,
+                [(warm, BF16, VM)] + [((ZB, points, regimes), BF16, VM)] * min(2, shifts),
                 on(ANY, field) + on(SM, reference_material_kappas) + on(VM, kind, warmth),
-                "edge",
+                "flux",
             )
             token = edges[0]
         if sweep_index < SWEEPS - 2:
@@ -564,21 +574,20 @@
     rest, gain = call(
         functools.partial(conduction_kernel, groups),
         [(warm, F32, VM), (warm, F32, VM)],
-        on(SM, warmth_partner_tile_ids.T, reference_material_kappas)
+        on(SM, warmth_partner_tile_ids.T)
         + on(
             VM,
             warmth_coupling_tiles,
-            kind,
             warmth_self_coefficient,
             warmth_storage_per_point,
             layer_boundary_couplings,
             warmth,
+            flux,
             below,
             above,
         )
         + on(ANY, heat),
         "conduction",
-        scratch=[pltpu.VMEM(warm, BF16)],
         flops=near_flops,
     )
     heat, field, late = call(
@@ -608,7 +617,10 @@
         on(VM, gain) + on(SM, *maps) + on(VM, *late, rest) + on(HB, out),
         "late",
         aliases={2 + 2 * shifts: 0},
-        scratch=[dma((shifts * late_spots,))],
+        scratch=[
+            pltpu.VMEM((late_spots, points, regimes), F32),
+            dma((shifts * late_spots,)),
+        ],
     )
     return (voltage_solution, advanced_warmth_values)
 

time: 46.4 us -> 46.5 us (level)
  waiting for transfers between devices: 8.17 us -> 8.81 us
  starting transfers between devices: 23 us -> 22.4 us
    ppermute x20, waiting for transfers between devices: 6.26 us -> 6.95 us  [from_partner(): return lax.ppermute(block, axis, route)]
    ppermute x20, starting transfers between devices: 19.4 us -> 18.7 us  [from_partner(): return lax.ppermute(block, axis, route)]
  transfers between devices with their start and end apart: 23 -> 23, of which waited for: 7 -> 7; matrix products, arithmetic and copies ran while one was open for 2% -> 2% of each run, Pallas kernels for 21% -> 22%
where the time goes in v1:
time: 46.5 us; the launch traced here: 46.4 us
  starting transfers between devices  22.4 us (48%)
  Pallas kernels  13.5 us (29%)
  waiting for transfers between devices  8.81 us (19%)
  between operations  0.88 us (2%)
  local copies, waits for them, and re-layouts  0.84 us (2%)
    ppermute x20, starting transfers between devices, from_partner(): return lax.ppermute(block, axis, route)  18.7 us
    pallas_call x14, Pallas kernels, call(): pl.pallas_call(kernel, out_shape=[SPACES[id(spec)](shape, dtype) for shap...  13.5 us
    ppermute x20, waiting for transfers between devices, from_partner(): return lax.ppermute(block, axis, route)  6.95 us
    ppermute x1, starting transfers between devices, body(): soon = [lax.ppermute(soon[s], 'therm', routes[s]) for s in range(shifts)]  1.58 us
    ppermute x1, starting transfers between devices, body(): below = above = lax.ppermute(edges[0], 'therm', [(0, 1), (1, 0)])  1.52 us
    ppermute x1, waiting for transfers between devices, body(): soon = [lax.ppermute(soon[s], 'therm', routes[s]) for s in range(shifts)]  0.96 us
  transfers between devices with their start and end apart: 23, of which 7 were waited for; matrix products, arithmetic and copies ran while one was open for 2% of the time, Pallas kernels for 22%

profile of v1, /device:TPU:0, one launch (start us, length us, event | category | flops | bytes accessed | tf_op | source)
XLA Modules:
  0.0 46.4 jit_solution(4420809062000491422)
XLA Ops:
  0.6 1.3 %start.1 = (bf16[32,64,128]{2,1,0:T(8,128)(2,1)S(1)}, f32[32,64]{1,0:T(8,128)S(1)}, s32[2,4]{1,0:T(2,128)S(4)}, s32[4,32]{1,0:T(4,128)S(4)}, s32[1,32]{1,0:T(1,1...) custom-call(bf16[32,64,128]{2,1,0:T(8,128)(2,1)} %amps.1, ...), custom_call_target="tpu_custom_call" | custom-call | tf_op jit(solution)/shard_map/start/pallas_call | solution.py:33
  2.0 4.1 %collective-permute-start = (bf16[128,128]{1,0:T(8,128)(2,1)S(1)}, bf16[128,128]{1,0:T(8,128)(2,1)S(1)}, u32[]{:S(2)}, u32[]{:S(2)}) collective-permute-start(bf16[128,128]{1,0:T(8,128)(2,1)S(1)} %get-tuple-element.73), channel_id=1, source_target_pairs={{0,16},{16,0},{2,18},{18,2},{4,20},{20,4},{6,22},{22,6},{8,24},{24... | collective-permute-start | bytes 98312 | tf_op jit(solution)/shard_map/ppermute | solution.py:57
  6.1 1.6 %collective-permute-start.1 = (bf16[128,128]{1,0:T(8,128)(2,1)S(1)}, bf16[128,128]{1,0:T(8,128)(2,1)S(1)}, u32[]{:S(2)}, u32[]{:S(2)}) collective-permute-start(bf16[128,128]{1,0:T(8,128)(2,1)S(1)} %get-tuple-element.74), channel_id=1, source_target_pairs={{0,8},{8,0},{2,10},{10,2},{4,12},{12,4},{6,14},{14,6},{16,24},{24,... | collective-permute-start | bytes 98312 | tf_op jit(solution)/shard_map/ppermute | solution.py:57
  7.6 1.5 %collective-permute-start.2 = (bf16[128,128]{1,0:T(8,128)(2,1)S(1)}, bf16[128,128]{1,0:T(8,128)(2,1)S(1)}, u32[]{:S(2)}, u32[]{:S(2)}) collective-permute-start(bf16[128,128]{1,0:T(8,128)(2,1)S(1)} %get-tuple-element.75), channel_id=1, source_target_pairs={{0,4},{4,0},{2,6},{6,2},{8,12},{12,8},{10,14},{14,10},{16,20},{20,... | collective-permute-start | bytes 98312 | tf_op jit(solution)/shard_map/ppermute | solution.py:57
  9.1 3.2 %first.1 = (bf16[32,64,256]{2,1,0:T(8,128)(2,1)S(1)}, f32[32,64,128]{2,1,0:T(8,128)S(1)}, bf16[32,64,128]{2,1,0:T(8,128)(2,1)S(1)}, f32[32,64,128]{2,1,0:T(8,128...) custom-call(s32[4,32]{1,0:T(4,128)S(4)} %get-tuple-element.64.ids, ...), custom_call_target="tpu_custom_call" | custom-call | flops 134217728 | tf_op jit(solution)/shard_map/first/pallas_call | solution.py:33
  12.6 0.4 collective-permute-start.5
  13.4 1.1 %collective-permute-start.7 = (bf16[128,128]{1,0:T(8,128)(2,1)S(1)}, bf16[128,128]{1,0:T(8,128)(2,1)S(1)}, u32[]{:S(2)}, u32[]{:S(2)}) collective-permute-start(bf16[128,128]{1,0:T(8,128)(2,1)S(1)} %get-tuple-element.87), channel_id=1, source_target_pairs={{0,4},{4,0},{2,6},{6,2},{8,12},{12,8},{10,14},{14,10},{16,20},{20,... | collective-permute-start | bytes 98312 | tf_op jit(solution)/shard_map/ppermute | solution.py:57
  14.5 0.6 %near.3 = (f32[32,64,128]{2,1,0:T(8,128)S(1)}, bf16[32,64,128]{2,1,0:T(8,128)(2,1)S(1)}) custom-call(s32[4,32]{1,0:T(4,128)S(4)} %get-tuple-element.64.ids, bf16[32,64,256]{2,1,0:T(8,128)(2,1)S(1)} %get-tuple-element.71.packed, bf16[32,64,128]{2,1,0:T(8,128)(2,1)S(1)} %get-tuple-element.79.field, f32[32,64,128]{2,1,0:T(8,128)S(1)} %get-tuple-element.80.state, ...), custom_call_target="tpu_custom_call" | custom-call | flops 134217728 | tf_op jit(solution)/shard_map/near/pallas_call | solution.py:33
  15.2 1.0 %flux.1 = (bf16[32,64,128]{2,1,0:T(8,128)(2,1)S(1)}, bf16[2,64,128]{2,1,0:T(8,128)(2,1)S(1)}) custom-call(bf16[32,64,128]{2,1,0:T(8,128)(2,1)S(1)} %get-tuple-element.81.token.refs_5_, f32[8]{0:T(128)S(1)} %copy-done.6, s32[32,64]{1,0:T(8,128)S(1)} %get-tuple-element.82.kind, bf16[32,64,128]{2,1,0:T(8,128)(2,1)S(1)} %get-tuple-element.83.warmth), custom_call_target="tpu_custom_call" | custom-call | tf_op jit(solution)/shard_map/flux/pallas_call | solution.py:33
  16.2 1.5 %collective-permute-done.5.refs_0_ = bf16[128,128]{1,0:T(8,128)(2,1)S(1)} collective-permute-done((bf16[128,128]{1,0:T(8,128)(2,1)S(1)}, bf16[128,128]{1,0:T(8,128)(2,1)S(1)}, u32[]{:S(2)}, u32[]{:S(2)}) %collective-permute-start.5) | collective-permute-done | bytes 32800 | tf_op jit(solution)/shard_map/ppermute | solution.py:57
  17.9 2.3 %collective-permute-start.9 = (bf16[128,128]{1,0:T(8,128)(2,1)S(1)}, bf16[128,128]{1,0:T(8,128)(2,1)S(1)}, u32[]{:S(2)}, u32[]{:S(2)}) collective-permute-start(bf16[128,128]{1,0:T(8,128)(2,1)S(1)} %get-tuple-element.90), channel_id=1, source_target_pairs={{0,16},{16,0},{2,18},{18,2},{4,20},{20,4},{6,22},{22,6},{8,24},{24... | collective-permute-start | bytes 98312 | tf_op jit(solution)/shard_map/ppermute | solution.py:57
  20.2 0.8 %collective-permute-start.10 = (bf16[128,128]{1,0:T(8,128)(2,1)S(1)}, bf16[128,128]{1,0:T(8,128)(2,1)S(1)}, u32[]{:S(2)}, u32[]{:S(2)}) collective-permute-start(bf16[128,128]{1,0:T(8,128)(2,1)S(1)} %get-tuple-element.91), channel_id=1, source_target_pairs={{0,4},{4,0},{2,6},{6,2},{8,12},{12,8},{10,14},{14,10},{16,20},{20,... | collective-permute-start | bytes 98312 | tf_op jit(solution)/shard_map/ppermute | solution.py:57
  21.0 1.6 %collective-permute-start.11 = (bf16[128,128]{1,0:T(8,128)(2,1)S(1)}, bf16[128,128]{1,0:T(8,128)(2,1)S(1)}, u32[]{:S(2)}, u32[]{:S(2)}) collective-permute-start(bf16[128,128]{1,0:T(8,128)(2,1)S(1)} %get-tuple-element.92), channel_id=1, source_target_pairs={{0,8},{8,0},{2,10},{10,2},{4,12},{12,4},{6,14},{14,6},{16,24},{24,... | collective-permute-start | bytes 98312 | tf_op jit(solution)/shard_map/ppermute | solution.py:57
  22.6 1.5 %collective-permute-start.4 = (bf16[2,64,128]{2,1,0:T(8,128)(2,1)S(1)}, bf16[2,64,128]{2,1,0:T(8,128)(2,1)S(1)}, u32[]{:S(2)}, u32[]{:S(2)}) collective-permute-start(bf16[2,64,128]{2,1,0:T(8,128)(2,1)S(1)} %get-tuple-element.84.token), channel_id=1, source_target_pairs={{0,1},{1,0},{2,3},{3,2},{4,5},{5,4},{6,7},{7,6},{8,9},{9,8},{10,11... | collective-permute-start | bytes 98312 | tf_op jit(solution)/shard_map/ppermute | solution.py:544
  24.1 0.6 %near.4 = (f32[32,64,128]{2,1,0:T(8,128)S(1)}, bf16[32,64,128]{2,1,0:T(8,128)(2,1)S(1)}) custom-call(s32[4,32]{1,0:T(4,128)S(4)} %get-tuple-element.64.ids, bf16[32,64,256]{2,1,0:T(8,128)(2,1)S(1)} %get-tuple-element.71.packed, bf16[32,64,128]{2,1,0:T(8,128)(2,1)S(1)} %get-tuple-element.94.field, f32[32,64,128]{2,1,0:T(8,128)S(1)} %get-tuple-element.95.state, ...), custom_call_target="tpu_custom_call" | custom-call | flops 134217728 | tf_op jit(solution)/shard_map/near/pallas_call | solution.py:33
  25.1 1.6 %collective-permute-start.13 = (bf16[128,128]{1,0:T(8,128)(2,1)S(1)}, bf16[128,128]{1,0:T(8,128)(2,1)S(1)}, u32[]{:S(2)}, u32[]{:S(2)}) collective-permute-start(bf16[128,128]{1,0:T(8,128)(2,1)S(1)} %get-tuple-element.102), channel_id=1, source_target_pairs={{0,8},{8,0},{2,10},{10,2},{4,12},{12,4},{6,14},{14,6},{16,24},{24,... | collective-permute-start | bytes 98312 | tf_op jit(solution)/shard_map/ppermute | solution.py:57
  26.8 1.2 %collective-permute-start.14 = (bf16[128,128]{1,0:T(8,128)(2,1)S(1)}, bf16[128,128]{1,0:T(8,128)(2,1)S(1)}, u32[]{:S(2)}, u32[]{:S(2)}) collective-permute-start(bf16[128,128]{1,0:T(8,128)(2,1)S(1)} %get-tuple-element.103), channel_id=1, source_target_pairs={{0,4},{4,0},{2,6},{6,2},{8,12},{12,8},{10,14},{14,10},{16,20},{20,... | collective-permute-start | bytes 98312 | tf_op jit(solution)/shard_map/ppermute | solution.py:57
  28.4 0.9 %near.5 = (f32[32,64,128]{2,1,0:T(8,128)S(1)}, bf16[32,64,128]{2,1,0:T(8,128)(2,1)S(1)}, f32[64,64,128]{2,1,0:T(8,128)S(1)}, f32[32,64,128]{2,1,0:T(8,128)S(1)}) custom-call(s32[4,32]{1,0:T(4,128)S(4)} %get-tuple-element.64.ids, bf16[32,64,256]{2,1,0:T(8,128)(2,1)S(1)} %get-tuple-element.71.packed, bf16[32,64,128]{2,1,0:T(8,128)(2,1)S(1)} %get-tuple-element.98.field, ...), custom_call_target="tpu_custom_call" | custom-call | flops 134217728 | tf_op jit(solution)/shard_map/near/pallas_call | solution.py:33
  29.3 1.4 %collective-permute-done.14.refs_1_ = bf16[128,128]{1,0:T(8,128)(2,1)S(1)} collective-permute-done((bf16[128,128]{1,0:T(8,128)(2,1)S(1)}, bf16[128,128]{1,0:T(8,128)(2,1)S(1)}, u32[]{:S(2)}, u32[]{:S(2)}) %collective-permute-start.14) | collective-permute-done | bytes 32800 | tf_op jit(solution)/shard_map/ppermute | solution.py:57
  30.7 2.4 %collective-permute-done.15.refs_2_ = bf16[128,128]{1,0:T(8,128)(2,1)S(1)} collective-permute-done((bf16[128,128]{1,0:T(8,128)(2,1)S(1)}, bf16[128,128]{1,0:T(8,128)(2,1)S(1)}, u32[]{:S(2)}, u32[]{:S(2)}) %collective-permute-start.15) | collective-permute-done | bytes 32800 | tf_op jit(solution)/shard_map/ppermute | solution.py:57
  33.1 0.8 %heat.1 = (f32[32,64,128]{2,1,0:T(8,128)S(1)}, bf16[32,64,128]{2,1,0:T(8,128)(2,1)S(1)}, f32[64,64,128]{2,1,0:T(8,128)S(1)}, bf16[1,1552,128]{2,1,0:T(8,128)(2,1...) custom-call(bf16[2,64,128]{2,1,0:T(8,128)(2,1)S(1)} %collective-perm, ...), custom_call_target="tpu_custom_call", output_to_operand_aliasing={{0}: (13, {}), {1}: (14, {}), {2}: (15, {})} | custom-call | flops 134217728 | tf_op jit(solution)/shard_map/heat/pallas_call | solution.py:33
  33.9 1.6 %collective-permute-start.21 = (bf16[1552,128]{1,0:T(8,128)(2,1)S(1)}, bf16[1552,128]{1,0:T(8,128)(2,1)S(1)}, u32[]{:S(2)}, u32[]{:S(2)}) collective-permute-start(bf16[1552,128]{1,0:T(8,128)(2,1)S(1)} %bitcast.12), channel_id=1, source_target_pairs={{0,1},{1,0},{2,3},{3,2},{4,5},{5,4},{6,7},{7,6},{8,9},{9,8},{10,11... | collective-permute-start | bytes 1191944 | tf_op jit(solution)/shard_map/ppermute | solution.py:569
  35.6 0.8 %collective-permute-start.18 = (bf16[128,128]{1,0:T(8,128)(2,1)S(1)}, bf16[128,128]{1,0:T(8,128)(2,1)S(1)}, u32[]{:S(2)}, u32[]{:S(2)}) collective-permute-start(bf16[128,128]{1,0:T(8,128)(2,1)S(1)} %get-tuple-element.110), channel_id=1, source_target_pairs={{0,8},{8,0},{2,10},{10,2},{4,12},{12,4},{6,14},{14,6},{16,24},{24,... | collective-permute-start | bytes 98312 | tf_op jit(solution)/shard_map/ppermute | solution.py:57
  36.4 0.8 %collective-permute-start.19 = (bf16[128,128]{1,0:T(8,128)(2,1)S(1)}, bf16[128,128]{1,0:T(8,128)(2,1)S(1)}, u32[]{:S(2)}, u32[]{:S(2)}) collective-permute-start(bf16[128,128]{1,0:T(8,128)(2,1)S(1)} %get-tuple-element.111), channel_id=1, source_target_pairs={{0,4},{4,0},{2,6},{6,2},{8,12},{12,8},{10,14},{14,10},{16,20},{20,... | collective-permute-start | bytes 98312 | tf_op jit(solution)/shard_map/ppermute | solution.py:57
  37.3 1.6 %conduction.1 = (f32[32,64,128]{2,1,0:T(8,128)S(1)}, f32[32,64,128]{2,1,0:T(8,128)S(1)}) custom-call(s32[3,32]{1,0:T(4,128)S(1)} %bitcast.11, bf16[32,3,64,64]{3,2,1,0:T(8,128)(2,1)S(1)} %copy-done.1, f32[32,64]{1,0:T(8,128)S(1)} %copy-done.3, f32[32,64]{1,0:T(8,128)S(1)} %copy-done.4, bf16[4,64,64]{2,1,0:T(8,128)(2,1)S(1)} %copy-done.2, ...), custom_call_target="tpu_custom_call" | custom-call | flops 134217728 | tf_op jit(solution)/shard_map/conduction/pallas_call | solution.py:33
  38.9 1.4 %collective-permute-done.17.refs_0_ = bf16[128,128]{1,0:T(8,128)(2,1)S(1)} collective-permute-done((bf16[128,128]{1,0:T(8,128)(2,1)S(1)}, bf16[128,128]{1,0:T(8,128)(2,1)S(1)}, u32[]{:S(2)}, u32[]{:S(2)}) %collective-permute-start.17) | collective-permute-done | bytes 32800 | tf_op jit(solution)/shard_map/ppermute | solution.py:57
  40.6 0.6 %collective-permute-start.22 = (bf16[8,64,128]{2,1,0:T(8,128)(2,1)S(1)}, bf16[8,64,128]{2,1,0:T(8,128)(2,1)S(1)}, u32[]{:S(2)}, u32[]{:S(2)}) collective-permute-start(bf16[8,64,128]{2,1,0:T(8,128)(2,1)S(1)} %bitcast.13), channel_id=1, source_target_pairs={{0,1},{1,0},{2,3},{3,2},{4,5},{5,4},{6,7},{7,6},{8,9},{9,8},{10,11... | collective-permute-start | bytes 393224 | tf_op jit(solution)/shard_map/ppermute | solution.py:605
  41.2 1.0 %collective-permute-done.21.refs_1_ = bf16[1552,128]{1,0:T(8,128)(2,1)S(1)} collective-permute-done((bf16[1552,128]{1,0:T(8,128)(2,1)S(1)}, bf16[1552,128]{1,0:T(8,128)(2,1)S(1)}, u32[]{:S(2)}, u32[]{:S(2)}) %collective-permute-start.21) | collective-permute-done | bytes 397344 | tf_op jit(solution)/shard_map/ppermute | solution.py:569
  42.1 1.8 %early.1 = (f32[32,64,128]{2,1,0:T(8,128)S(1)}, bf16[32,64,128]{2,1,0:T(8,128)(2,1)S(1)}, f32[32,64,128]{2,1,0:T(8,128)}, s32[8]{0:T(128)S(4)}) custom-call(f32[64,64,128]{2,1,0:T(8,128)S(1)} %get-tuple-element.115.heat, f32[32,64,128]{2,1,0:T(8,128)S(1)} %get-tuple-element.117.gain, ...), custom_call_target="tpu_custom_call", output_to_operand_aliasing={{0}: (4, {}), {1}: (5, {})} | custom-call | tf_op jit(solution)/shard_map/early/pallas_call | solution.py:33
  43.9 0.8 %copy.46 = bf16[32,64,128]{2,1,0:T(8,128)(2,1)} copy(bf16[32,64,128]{2,1,0:T(8,128)(2,1)S(1)} %get-tuple-element.126) | data formatting | bytes 1048576
  44.7 0.9 %collective-permute-done.22.refs_1_ = bf16[8,64,128]{2,1,0:T(8,128)(2,1)S(1)} collective-permute-done((bf16[8,64,128]{2,1,0:T(8,128)(2,1)S(1)}, bf16[8,64,128]{2,1,0:T(8,128)(2,1)S(1)}, u32[]{:S(2)}, u32[]{:S(2)}) %collective-permute-start.22) | collective-permute-done | bytes 131104 | tf_op jit(solution)/shard_map/ppermute | solution.py:605
  45.6 0.8 %late.1 = f32[32,64,128]{2,1,0:T(8,128)} custom-call(f32[32,64,128]{2,1,0:T(8,128)S(1)} %get-tuple-element.117.gain, s32[8]{0:T(128)S(4)} %get-tuple-element.122.refs_0_, bf16[8,64,128]{2,1,0:T(8,128)(2,1)S(1)} %collective-permute-done.22.refs_1_, f32[32,64,128]{2,1,0:T(8,128)S(1)} %get-tuple-element.124.refs_2_, ...), custom_call_target="tpu_custom_call", output_to_operand_aliasing={{}: (4, {})} | custom-call | tf_op jit(solution)/shard_map/late/pallas_call | solution.py:33
  (44 shorter events, 1.9 us)
Async XLA Ops:
  0.6 11.7 %copy-start = (bf16[8,64,64]{2,1,0:T(8,128)(2,1)S(1)}, bf16[8,64,64]{2,1,0:T(8,128)(2,1)}, u32[]{:S(2)}) copy-start(bf16[8,64,64]{2,1,0:T(8,128)(2,1)} %admittance.9) | copy-start | bytes 196612
  2.0 10.3 %collective-permute-start = (bf16[128,128]{1,0:T(8,128)(2,1)S(1)}, bf16[128,128]{1,0:T(8,128)(2,1)S(1)}, u32[]{:S(2)}, u32[]{:S(2)}) collective-permute-start(bf16[128,128]{1,0:T(8,128)(2,1)S(1)} %get-tuple-element.73), channel_id=1, source_target_pairs={{0,16},{16,0},{2,18},{18,2},{4,20},{20,4},{6,22},{22,6},{8,24},{24... | collective-permute-start | bytes 98312 | tf_op jit(solution)/shard_map/ppermute | solution.py:57
  6.1 6.3 %collective-permute-start.1 = (bf16[128,128]{1,0:T(8,128)(2,1)S(1)}, bf16[128,128]{1,0:T(8,128)(2,1)S(1)}, u32[]{:S(2)}, u32[]{:S(2)}) collective-permute-start(bf16[128,128]{1,0:T(8,128)(2,1)S(1)} %get-tuple-element.74), channel_id=1, source_target_pairs={{0,8},{8,0},{2,10},{10,2},{4,12},{12,4},{6,14},{14,6},{16,24},{24,... | collective-permute-start | bytes 98312 | tf_op jit(solution)/shard_map/ppermute | solution.py:57
  7.6 4.7 %collective-permute-start.2 = (bf16[128,128]{1,0:T(8,128)(2,1)S(1)}, bf16[128,128]{1,0:T(8,128)(2,1)S(1)}, u32[]{:S(2)}, u32[]{:S(2)}) collective-permute-start(bf16[128,128]{1,0:T(8,128)(2,1)S(1)} %get-tuple-element.75), channel_id=1, source_target_pairs={{0,4},{4,0},{2,6},{6,2},{8,12},{12,8},{10,14},{14,10},{16,20},{20,... | collective-permute-start | bytes 98312 | tf_op jit(solution)/shard_map/ppermute | solution.py:57
  9.1 3.2 %collective-permute-start.3 = (bf16[128,128]{1,0:T(8,128)(2,1)S(1)}, bf16[128,128]{1,0:T(8,128)(2,1)S(1)}, u32[]{:S(2)}, u32[]{:S(2)}) collective-permute-start(bf16[128,128]{1,0:T(8,128)(2,1)S(1)} %get-tuple-element.76), channel_id=1, source_target_pairs={{0,2},{2,0},{4,6},{6,4},{8,10},{10,8},{12,14},{14,12},{16,18},{18,... | collective-permute-start | bytes 98312 | tf_op jit(solution)/shard_map/ppermute | solution.py:57
  12.6 5.1 %collective-permute-start.5 = (bf16[128,128]{1,0:T(8,128)(2,1)S(1)}, bf16[128,128]{1,0:T(8,128)(2,1)S(1)}, u32[]{:S(2)}, u32[]{:S(2)}) collective-permute-start(bf16[128,128]{1,0:T(8,128)(2,1)S(1)} %get-tuple-element.85), channel_id=1, source_target_pairs={{0,16},{16,0},{2,18},{18,2},{4,20},{20,4},{6,22},{22,6},{8,24},{24... | collective-permute-start | bytes 98312 | tf_op jit(solution)/shard_map/ppermute | solution.py:57
  13.0 4.7 %collective-permute-start.6 = (bf16[128,128]{1,0:T(8,128)(2,1)S(1)}, bf16[128,128]{1,0:T(8,128)(2,1)S(1)}, u32[]{:S(2)}, u32[]{:S(2)}) collective-permute-start(bf16[128,128]{1,0:T(8,128)(2,1)S(1)} %get-tuple-element.86), channel_id=1, source_target_pairs={{0,8},{8,0},{2,10},{10,2},{4,12},{12,4},{6,14},{14,6},{16,24},{24,... | collective-permute-start | bytes 98312 | tf_op jit(solution)/shard_map/ppermute | solution.py:57
  13.4 4.3 %collective-permute-start.7 = (bf16[128,128]{1,0:T(8,128)(2,1)S(1)}, bf16[128,128]{1,0:T(8,128)(2,1)S(1)}, u32[]{:S(2)}, u32[]{:S(2)}) collective-permute-start(bf16[128,128]{1,0:T(8,128)(2,1)S(1)} %get-tuple-element.87), channel_id=1, source_target_pairs={{0,4},{4,0},{2,6},{6,2},{8,12},{12,8},{10,14},{14,10},{16,20},{20,... | collective-permute-start | bytes 98312 | tf_op jit(solution)/shard_map/ppermute | solution.py:57
  14.5 3.2 %collective-permute-start.8 = (bf16[128,128]{1,0:T(8,128)(2,1)S(1)}, bf16[128,128]{1,0:T(8,128)(2,1)S(1)}, u32[]{:S(2)}, u32[]{:S(2)}) collective-permute-start(bf16[128,128]{1,0:T(8,128)(2,1)S(1)} %get-tuple-element.88), channel_id=1, source_target_pairs={{0,2},{2,0},{4,6},{6,4},{8,10},{10,8},{12,14},{14,12},{16,18},{18,... | collective-permute-start | bytes 98312 | tf_op jit(solution)/shard_map/ppermute | solution.py:57
  14.5 0.7 %copy-start.6 = (f32[8]{0:T(128)S(1)}, f32[8]{0:T(128)}, u32[]{:S(2)}) copy-start(f32[8]{0:T(128)} %kappas.1) | copy-start | bytes 100
  17.9 6.8 %collective-permute-start.9 = (bf16[128,128]{1,0:T(8,128)(2,1)S(1)}, bf16[128,128]{1,0:T(8,128)(2,1)S(1)}, u32[]{:S(2)}, u32[]{:S(2)}) collective-permute-start(bf16[128,128]{1,0:T(8,128)(2,1)S(1)} %get-tuple-element.90), channel_id=1, source_target_pairs={{0,16},{16,0},{2,18},{18,2},{4,20},{20,4},{6,22},{22,6},{8,24},{24... | collective-permute-start | bytes 98312 | tf_op jit(solution)/shard_map/ppermute | solution.py:57
  20.2 4.5 %collective-permute-start.10 = (bf16[128,128]{1,0:T(8,128)(2,1)S(1)}, bf16[128,128]{1,0:T(8,128)(2,1)S(1)}, u32[]{:S(2)}, u32[]{:S(2)}) collective-permute-start(bf16[128,128]{1,0:T(8,128)(2,1)S(1)} %get-tuple-element.91), channel_id=1, source_target_pairs={{0,4},{4,0},{2,6},{6,2},{8,12},{12,8},{10,14},{14,10},{16,20},{20,... | collective-permute-start | bytes 98312 | tf_op jit(solution)/shard_map/ppermute | solution.py:57
  21.0 3.9 %collective-permute-start.11 = (bf16[128,128]{1,0:T(8,128)(2,1)S(1)}, bf16[128,128]{1,0:T(8,128)(2,1)S(1)}, u32[]{:S(2)}, u32[]{:S(2)}) collective-permute-start(bf16[128,128]{1,0:T(8,128)(2,1)S(1)} %get-tuple-element.92), channel_id=1, source_target_pairs={{0,8},{8,0},{2,10},{10,2},{4,12},{12,4},{6,14},{14,6},{16,24},{24,... | collective-permute-start | bytes 98312 | tf_op jit(solution)/shard_map/ppermute | solution.py:57
  22.6 2.3 %collective-permute-start.12 = (bf16[128,128]{1,0:T(8,128)(2,1)S(1)}, bf16[128,128]{1,0:T(8,128)(2,1)S(1)}, u32[]{:S(2)}, u32[]{:S(2)}) collective-permute-start(bf16[128,128]{1,0:T(8,128)(2,1)S(1)} %get-tuple-element.93), channel_id=1, source_target_pairs={{0,2},{2,0},{4,6},{6,4},{8,10},{10,8},{12,14},{14,12},{16,18},{18,... | collective-permute-start | bytes 98312 | tf_op jit(solution)/shard_map/ppermute | solution.py:57
  22.6 6.7 %collective-permute-start.4 = (bf16[2,64,128]{2,1,0:T(8,128)(2,1)S(1)}, bf16[2,64,128]{2,1,0:T(8,128)(2,1)S(1)}, u32[]{:S(2)}, u32[]{:S(2)}) collective-permute-start(bf16[2,64,128]{2,1,0:T(8,128)(2,1)S(1)} %get-tuple-element.84.token), channel_id=1, source_target_pairs={{0,1},{1,0},{2,3},{3,2},{4,5},{5,4},{6,7},{7,6},{8,9},{9,8},{10,11... | collective-permute-start | bytes 98312 | tf_op jit(solution)/shard_map/ppermute | solution.py:544
  25.1 4.1 %collective-permute-start.13 = (bf16[128,128]{1,0:T(8,128)(2,1)S(1)}, bf16[128,128]{1,0:T(8,128)(2,1)S(1)}, u32[]{:S(2)}, u32[]{:S(2)}) collective-permute-start(bf16[128,128]{1,0:T(8,128)(2,1)S(1)} %get-tuple-element.102), channel_id=1, source_target_pairs={{0,8},{8,0},{2,10},{10,2},{4,12},{12,4},{6,14},{14,6},{16,24},{24,... | collective-permute-start | bytes 98312 | tf_op jit(solution)/shard_map/ppermute | solution.py:57
  26.8 3.9 %collective-permute-start.14 = (bf16[128,128]{1,0:T(8,128)(2,1)S(1)}, bf16[128,128]{1,0:T(8,128)(2,1)S(1)}, u32[]{:S(2)}, u32[]{:S(2)}) collective-permute-start(bf16[128,128]{1,0:T(8,128)(2,1)S(1)} %get-tuple-element.103), channel_id=1, source_target_pairs={{0,4},{4,0},{2,6},{6,2},{8,12},{12,8},{10,14},{14,10},{16,20},{20,... | collective-permute-start | bytes 98312 | tf_op jit(solution)/shard_map/ppermute | solution.py:57
  28.0 5.1 %collective-permute-start.15 = (bf16[128,128]{1,0:T(8,128)(2,1)S(1)}, bf16[128,128]{1,0:T(8,128)(2,1)S(1)}, u32[]{:S(2)}, u32[]{:S(2)}) collective-permute-start(bf16[128,128]{1,0:T(8,128)(2,1)S(1)} %get-tuple-element.104), channel_id=1, source_target_pairs={{0,16},{16,0},{2,18},{18,2},{4,20},{20,4},{6,22},{22,6},{8,24},{24... | collective-permute-start | bytes 98312 | tf_op jit(solution)/shard_map/ppermute | solution.py:57
  28.4 4.7 %collective-permute-start.16 = (bf16[128,128]{1,0:T(8,128)(2,1)S(1)}, bf16[128,128]{1,0:T(8,128)(2,1)S(1)}, u32[]{:S(2)}, u32[]{:S(2)}) collective-permute-start(bf16[128,128]{1,0:T(8,128)(2,1)S(1)} %get-tuple-element.105), channel_id=1, source_target_pairs={{0,2},{2,0},{4,6},{6,4},{8,10},{10,8},{12,14},{14,12},{16,18},{18,... | collective-permute-start | bytes 98312 | tf_op jit(solution)/shard_map/ppermute | solution.py:57
  33.1 4.2 %copy-start.1 = (bf16[32,3,64,64]{3,2,1,0:T(8,128)(2,1)S(1)}, bf16[32,3,64,64]{3,2,1,0:T(8,128)(2,1)}, u32[]{:S(2)}) copy-start(bf16[32,3,64,64]{3,2,1,0:T(8,128)(2,1)} %tiles.3) | copy-start | bytes 2359300
  33.1 4.2 %copy-start.2 = (bf16[4,64,64]{2,1,0:T(8,128)(2,1)S(1)}, bf16[4,64,64]{2,1,0:T(8,128)(2,1)}, u32[]{:S(2)}) copy-start(bf16[4,64,64]{2,1,0:T(8,128)(2,1)} %couplings.1) | copy-start | bytes 98308
  33.1 4.2 %copy-start.3 = (f32[32,64]{1,0:T(8,128)S(1)}, f32[32,64]{1,0:T(8,128)}, u32[]{:S(2)}) copy-start(f32[32,64]{1,0:T(8,128)} %coefficient.1) | copy-start | bytes 24580
  33.1 4.2 %copy-start.4 = (f32[32,64]{1,0:T(8,128)S(1)}, f32[32,64]{1,0:T(8,128)}, u32[]{:S(2)}) copy-start(f32[32,64]{1,0:T(8,128)} %storage.1) | copy-start | bytes 24580
  33.1 4.2 %copy-start.5 = (s32[32,3]{0,1:T(4,128)S(1)}, s32[32,3]{0,1:T(4,128)}, u32[]{:S(2)}) copy-start(s32[32,3]{0,1:T(4,128)} %param.27) | copy-start | bytes 1156
  33.9 8.2 %collective-permute-start.21 = (bf16[1552,128]{1,0:T(8,128)(2,1)S(1)}, bf16[1552,128]{1,0:T(8,128)(2,1)S(1)}, u32[]{:S(2)}, u32[]{:S(2)}) collective-permute-start(bf16[1552,128]{1,0:T(8,128)(2,1)S(1)} %bitcast.12), channel_id=1, source_target_pairs={{0,1},{1,0},{2,3},{3,2},{4,5},{5,4},{6,7},{7,6},{8,9},{9,8},{10,11... | collective-permute-start | bytes 1191944 | tf_op jit(solution)/shard_map/ppermute | solution.py:569
  35.5 4.8 %collective-permute-start.17 = (bf16[128,128]{1,0:T(8,128)(2,1)S(1)}, bf16[128,128]{1,0:T(8,128)(2,1)S(1)}, u32[]{:S(2)}, u32[]{:S(2)}) collective-permute-start(bf16[128,128]{1,0:T(8,128)(2,1)S(1)} %get-tuple-element.109), channel_id=1, source_target_pairs={{0,16},{16,0},{2,18},{18,2},{4,20},{20,4},{6,22},{22,6},{8,24},{24... | collective-permute-start | bytes 98312 | tf_op jit(solution)/shard_map/ppermute | solution.py:57
  35.6 4.7 %collective-permute-start.18 = (bf16[128,128]{1,0:T(8,128)(2,1)S(1)}, bf16[128,128]{1,0:T(8,128)(2,1)S(1)}, u32[]{:S(2)}, u32[]{:S(2)}) collective-permute-start(bf16[128,128]{1,0:T(8,128)(2,1)S(1)} %get-tuple-element.110), channel_id=1, source_target_pairs={{0,8},{8,0},{2,10},{10,2},{4,12},{12,4},{6,14},{14,6},{16,24},{24,... | collective-permute-start | bytes 98312 | tf_op jit(solution)/shard_map/ppermute | solution.py:57
  36.4 3.9 %collective-permute-start.19 = (bf16[128,128]{1,0:T(8,128)(2,1)S(1)}, bf16[128,128]{1,0:T(8,128)(2,1)S(1)}, u32[]{:S(2)}, u32[]{:S(2)}) collective-permute-start(bf16[128,128]{1,0:T(8,128)(2,1)S(1)} %get-tuple-element.111), channel_id=1, source_target_pairs={{0,4},{4,0},{2,6},{6,2},{8,12},{12,8},{10,14},{14,10},{16,20},{20,... | collective-permute-start | bytes 98312 | tf_op jit(solution)/shard_map/ppermute | solution.py:57
  37.3 3.1 %collective-permute-start.20 = (bf16[128,128]{1,0:T(8,128)(2,1)S(1)}, bf16[128,128]{1,0:T(8,128)(2,1)S(1)}, u32[]{:S(2)}, u32[]{:S(2)}) collective-permute-start(bf16[128,128]{1,0:T(8,128)(2,1)S(1)} %get-tuple-element.112), channel_id=1, source_target_pairs={{0,2},{2,0},{4,6},{6,4},{8,10},{10,8},{12,14},{14,12},{16,18},{18,... | collective-permute-start | bytes 98312 | tf_op jit(solution)/shard_map/ppermute | solution.py:57
  40.6 5.0 %collective-permute-start.22 = (bf16[8,64,128]{2,1,0:T(8,128)(2,1)S(1)}, bf16[8,64,128]{2,1,0:T(8,128)(2,1)S(1)}, u32[]{:S(2)}, u32[]{:S(2)}) collective-permute-start(bf16[8,64,128]{2,1,0:T(8,128)(2,1)S(1)} %bitcast.13), channel_id=1, source_target_pairs={{0,1},{1,0},{2,3},{3,2},{4,5},{5,4},{6,7},{7,6},{8,9},{9,8},{10,11... | collective-permute-start | bytes 393224 | tf_op jit(solution)/shard_map/ppermute | solution.py:605

commit v2 on v0

--- a/solution.py
+++ b/solution.py
@@ -306,43 +306,37 @@
     return (kappa * (1.0 + 0.4 * jnp.tanh(w)) * w).astype(BF16)
 
 
-def edge_kernel(token, kappas, kind, warmth, *edges):
+def flux_kernel(token, kappas, kind, warmth, flux, *edges):
     turned = kappa_columns(kappas, kind)
     tiles, points, width = warmth.shape
+    for i in range(tiles):
+        flux[i] = block_flux(column(turned, i, width), warmth[i])
     sends_top = lax.axis_index("therm") == 0
     for z in range(ZB):
         top = tiles - ZB + z
-        low = block_flux(column(turned, z, width), warmth[z])
-        high = block_flux(column(turned, top, width), warmth[top])
         if len(edges) == 1:
-            both = jnp.where(sends_top, high.astype(F32), low.astype(F32))
-            edges[0][z] = both.astype(BF16)
+            edges[0][z] = flux[jnp.where(sends_top, top, z)]
         else:
-            edges[0][z], edges[1][z] = low, high
+            edges[0][z], edges[1][z] = flux[z], flux[top]
 
 
 def conduction_kernel(
     groups,
     ids,
-    kappas,
     tiles,
-    kind,
     coefficient,
     storage,
     couplings,
     warmth,
+    flux,
     below,
     above,
     heat,
     rest,
     gain,
-    flux,
 ):
     count = tiles.shape[0]
     width = flux.shape[2]
-    turned = kappa_columns(kappas, kind)
-    for i in range(count):
-        flux[i] = block_flux(column(turned, i, width), warmth[i])
     own = lax.axis_index("therm")
     lowest = (own > 0).astype(F32)
     highest = (own < groups - 1).astype(F32)
@@ -441,7 +435,7 @@
 
     far_first = list(range(levels))[::-1]
     near, *middle, far = range(levels)
-    orders = [far_first, [far] + middle + [near], middle[::-1] + [far, near]]
+    first_order, last_order = [far] + middle + [near], [near] + middle[::-1] + [far]
 
     amps, diag, face_ids, ids, layer, tile, *faces = call(
         functools.partial(start_kernel, levels),
@@ -466,7 +460,7 @@
         "start",
         scratch=[dma((6,))],
     )
-    order = far_first
+    order = first_order
     incoming = exchange(faces, order)
 
     packed, state, field, scale, warmth, kind, slot, rows = call(
@@ -509,11 +503,11 @@
             )
         token = scale
         if sweep_index == 1:
-            edges = call(
-                edge_kernel,
-                [((ZB, points, regimes), BF16, VM)] * min(2, shifts),
+            flux, *edges = call(
+                flux_kernel,
+                [(warm, BF16, VM)] + [((ZB, points, regimes), BF16, VM)] * min(2, shifts),
                 on(ANY, field) + on(SM, reference_material_kappas) + on(VM, kind, warmth),
-                "edge",
+                "flux",
             )
             token = edges[0]
         if sweep_index < SWEEPS - 2:
@@ -527,7 +521,7 @@
                 aliases={levels + 4: 0, levels + 5: 1},
                 scratch=[terms],
             )
-            order = orders[sweep_index]
+            order = far_first
             incoming = exchange(faces, order)
 
     if groups == 2:
@@ -558,27 +552,26 @@
     routes = [[(i, (i + s) % groups) for i in range(groups)] for s in range(1, groups)]
     soon = [lax.ppermute(soon[s], "therm", routes[s]) for s in range(shifts)]
     maps = [x[sent_rows, :tiles].astype(I32) for x in soon]
-    order = far_first
+    order = last_order
     incoming = exchange(faces, order)
 
     rest, gain = call(
         functools.partial(conduction_kernel, groups),
         [(warm, F32, VM), (warm, F32, VM)],
-        on(SM, warmth_partner_tile_ids.T, reference_material_kappas)
+        on(SM, warmth_partner_tile_ids.T)
         + on(
             VM,
             warmth_coupling_tiles,
-            kind,
             warmth_self_coefficient,
             warmth_storage_per_point,
             layer_boundary_couplings,
             warmth,
+            flux,
             below,
             above,
         )
         + on(ANY, heat),
         "conduction",
-        scratch=[pltpu.VMEM(warm, BF16)],
         flops=near_flops,
     )
     heat, field, late = call(

time: 46.4 us -> 46.2 us (level)
  waiting for transfers between devices: 8.17 us -> 7.34 us
  starting transfers between devices: 23 us -> 23.8 us
    ppermute x20, starting transfers between devices: 19.4 us -> 20.2 us  [from_partner(): return lax.ppermute(block, axis, route)]
    ppermute x20, waiting for transfers between devices: 6.26 us -> 5.48 us  [from_partner(): return lax.ppermute(block, axis, route)]
  transfers between devices with their start and end apart: 23 -> 23, of which waited for: 7 -> 9; matrix products, arithmetic and copies ran while one was open for 2% -> 2% of each run, Pallas kernels for 21% -> 21%
where the time goes in v2:
time: 46.2 us; the launch traced here: 46.1 us
  starting transfers between devices  23.8 us (52%)
  Pallas kernels  13.2 us (29%)
  waiting for transfers between devices  7.34 us (16%)
  between operations  0.87 us (2%)
  local copies, waits for them, and re-layouts  0.83 us (2%)
    ppermute x20, starting transfers between devices, from_partner(): return lax.ppermute(block, axis, route)  20.2 us
    pallas_call x14, Pallas kernels, call(): pl.pallas_call(kernel, out_shape=[SPACES[id(spec)](shape, dtype) for shap...  13.2 us
    ppermute x20, waiting for transfers between devices, from_partner(): return lax.ppermute(block, axis, route)  5.48 us
    ppermute x1, starting transfers between devices, body(): soon = [lax.ppermute(soon[s], 'therm', routes[s]) for s in range(shifts)]  1.59 us
    ppermute x1, starting transfers between devices, body(): below = above = lax.ppermute(edges[0], 'therm', [(0, 1), (1, 0)])  1.52 us
    ppermute x1, waiting for transfers between devices, body(): late = [lax.ppermute(late[s], 'therm', routes[s]) for s in range(shifts)]  1.15 us
  transfers between devices with their start and end apart: 23, of which 9 were waited for; matrix products, arithmetic and copies ran while one was open for 2% of the time, Pallas kernels for 21%

profile of v2, /device:TPU:0, one launch (start us, length us, event | category | flops | bytes accessed | tf_op | source)
XLA Modules:
  0.0 46.1 jit_solution(12896409670480896621)
XLA Ops:
  0.6 1.3 %start.1 = (bf16[32,64,128]{2,1,0:T(8,128)(2,1)S(1)}, f32[32,64]{1,0:T(8,128)S(1)}, s32[2,4]{1,0:T(2,128)S(4)}, s32[4,32]{1,0:T(4,128)S(4)}, s32[1,32]{1,0:T(1,1...) custom-call(bf16[32,64,128]{2,1,0:T(8,128)(2,1)} %amps.1, ...), custom_call_target="tpu_custom_call" | custom-call | tf_op jit(solution)/shard_map/start/pallas_call | solution.py:33
  2.0 4.1 %collective-permute-start = (bf16[128,128]{1,0:T(8,128)(2,1)S(1)}, bf16[128,128]{1,0:T(8,128)(2,1)S(1)}, u32[]{:S(2)}, u32[]{:S(2)}) collective-permute-start(bf16[128,128]{1,0:T(8,128)(2,1)S(1)} %get-tuple-element.73), channel_id=1, source_target_pairs={{0,16},{16,0},{2,18},{18,2},{4,20},{20,4},{6,22},{22,6},{8,24},{24... | collective-permute-start | bytes 98312 | tf_op jit(solution)/shard_map/ppermute | solution.py:57
  6.1 1.5 %collective-permute-start.1 = (bf16[128,128]{1,0:T(8,128)(2,1)S(1)}, bf16[128,128]{1,0:T(8,128)(2,1)S(1)}, u32[]{:S(2)}, u32[]{:S(2)}) collective-permute-start(bf16[128,128]{1,0:T(8,128)(2,1)S(1)} %get-tuple-element.74), channel_id=1, source_target_pairs={{0,4},{4,0},{2,6},{6,2},{8,12},{12,8},{10,14},{14,10},{16,20},{20,... | collective-permute-start | bytes 98312 | tf_op jit(solution)/shard_map/ppermute | solution.py:57
  7.6 1.6 %collective-permute-start.2 = (bf16[128,128]{1,0:T(8,128)(2,1)S(1)}, bf16[128,128]{1,0:T(8,128)(2,1)S(1)}, u32[]{:S(2)}, u32[]{:S(2)}) collective-permute-start(bf16[128,128]{1,0:T(8,128)(2,1)S(1)} %get-tuple-element.75), channel_id=1, source_target_pairs={{0,8},{8,0},{2,10},{10,2},{4,12},{12,4},{6,14},{14,6},{16,24},{24,... | collective-permute-start | bytes 98312 | tf_op jit(solution)/shard_map/ppermute | solution.py:57
  9.1 2.8 %first.1 = (bf16[32,64,256]{2,1,0:T(8,128)(2,1)S(1)}, f32[32,64,128]{2,1,0:T(8,128)S(1)}, bf16[32,64,128]{2,1,0:T(8,128)(2,1)S(1)}, f32[32,64,128]{2,1,0:T(8,128...) custom-call(s32[4,32]{1,0:T(4,128)S(4)} %get-tuple-element.64.ids, ...), custom_call_target="tpu_custom_call" | custom-call | flops 134217728 | tf_op jit(solution)/shard_map/first/pallas_call | solution.py:33
  12.7 1.0 %collective-permute-start.6 = (bf16[128,128]{1,0:T(8,128)(2,1)S(1)}, bf16[128,128]{1,0:T(8,128)(2,1)S(1)}, u32[]{:S(2)}, u32[]{:S(2)}) collective-permute-start(bf16[128,128]{1,0:T(8,128)(2,1)S(1)} %get-tuple-element.86), channel_id=1, source_target_pairs={{0,8},{8,0},{2,10},{10,2},{4,12},{12,4},{6,14},{14,6},{16,24},{24,... | collective-permute-start | bytes 98312 | tf_op jit(solution)/shard_map/ppermute | solution.py:57
  13.7 0.9 %collective-permute-start.7 = (bf16[128,128]{1,0:T(8,128)(2,1)S(1)}, bf16[128,128]{1,0:T(8,128)(2,1)S(1)}, u32[]{:S(2)}, u32[]{:S(2)}) collective-permute-start(bf16[128,128]{1,0:T(8,128)(2,1)S(1)} %get-tuple-element.87), channel_id=1, source_target_pairs={{0,4},{4,0},{2,6},{6,2},{8,12},{12,8},{10,14},{14,10},{16,20},{20,... | collective-permute-start | bytes 98312 | tf_op jit(solution)/shard_map/ppermute | solution.py:57
  14.6 0.6 %near.3 = (f32[32,64,128]{2,1,0:T(8,128)S(1)}, bf16[32,64,128]{2,1,0:T(8,128)(2,1)S(1)}) custom-call(s32[4,32]{1,0:T(4,128)S(4)} %get-tuple-element.64.ids, bf16[32,64,256]{2,1,0:T(8,128)(2,1)S(1)} %get-tuple-element.71.packed, bf16[32,64,128]{2,1,0:T(8,128)(2,1)S(1)} %get-tuple-element.79.field, f32[32,64,128]{2,1,0:T(8,128)S(1)} %get-tuple-element.80.state, ...), custom_call_target="tpu_custom_call" | custom-call | flops 134217728 | tf_op jit(solution)/shard_map/near/pallas_call | solution.py:33
  15.2 1.0 %flux.1 = (bf16[32,64,128]{2,1,0:T(8,128)(2,1)S(1)}, bf16[2,64,128]{2,1,0:T(8,128)(2,1)S(1)}) custom-call(bf16[32,64,128]{2,1,0:T(8,128)(2,1)S(1)} %get-tuple-element.81.token.refs_5_, f32[8]{0:T(128)S(1)} %copy-done.6, s32[32,64]{1,0:T(8,128)S(1)} %get-tuple-element.82.kind, bf16[32,64,128]{2,1,0:T(8,128)(2,1)S(1)} %get-tuple-element.83.warmth), custom_call_target="tpu_custom_call" | custom-call | tf_op jit(solution)/shard_map/flux/pallas_call | solution.py:33
  16.3 0.8 %collective-permute-done.5.refs_0_ = bf16[128,128]{1,0:T(8,128)(2,1)S(1)} collective-permute-done((bf16[128,128]{1,0:T(8,128)(2,1)S(1)}, bf16[128,128]{1,0:T(8,128)(2,1)S(1)}, u32[]{:S(2)}, u32[]{:S(2)}) %collective-permute-start.5) | collective-permute-done | bytes 32800 | tf_op jit(solution)/shard_map/ppermute | solution.py:57
  17.8 2.7 %collective-permute-start.9 = (bf16[128,128]{1,0:T(8,128)(2,1)S(1)}, bf16[128,128]{1,0:T(8,128)(2,1)S(1)}, u32[]{:S(2)}, u32[]{:S(2)}) collective-permute-start(bf16[128,128]{1,0:T(8,128)(2,1)S(1)} %get-tuple-element.90), channel_id=1, source_target_pairs={{0,16},{16,0},{2,18},{18,2},{4,20},{20,4},{6,22},{22,6},{8,24},{24... | collective-permute-start | bytes 98312 | tf_op jit(solution)/shard_map/ppermute | solution.py:57
  20.5 1.0 %collective-permute-start.10 = (bf16[128,128]{1,0:T(8,128)(2,1)S(1)}, bf16[128,128]{1,0:T(8,128)(2,1)S(1)}, u32[]{:S(2)}, u32[]{:S(2)}) collective-permute-start(bf16[128,128]{1,0:T(8,128)(2,1)S(1)} %get-tuple-element.91), channel_id=1, source_target_pairs={{0,8},{8,0},{2,10},{10,2},{4,12},{12,4},{6,14},{14,6},{16,24},{24,... | collective-permute-start | bytes 98312 | tf_op jit(solution)/shard_map/ppermute | solution.py:57
  21.5 0.5 %collective-permute-start.11 = (bf16[128,128]{1,0:T(8,128)(2,1)S(1)}, bf16[128,128]{1,0:T(8,128)(2,1)S(1)}, u32[]{:S(2)}, u32[]{:S(2)}) collective-permute-start(bf16[128,128]{1,0:T(8,128)(2,1)S(1)} %get-tuple-element.92), channel_id=1, source_target_pairs={{0,4},{4,0},{2,6},{6,2},{8,12},{12,8},{10,14},{14,10},{16,20},{20,... | collective-permute-start | bytes 98312 | tf_op jit(solution)/shard_map/ppermute | solution.py:57
  22.0 1.5 %collective-permute-start.4 = (bf16[2,64,128]{2,1,0:T(8,128)(2,1)S(1)}, bf16[2,64,128]{2,1,0:T(8,128)(2,1)S(1)}, u32[]{:S(2)}, u32[]{:S(2)}) collective-permute-start(bf16[2,64,128]{2,1,0:T(8,128)(2,1)S(1)} %get-tuple-element.84.token), channel_id=1, source_target_pairs={{0,1},{1,0},{2,3},{3,2},{4,5},{5,4},{6,7},{7,6},{8,9},{9,8},{10,11... | collective-permute-start | bytes 98312 | tf_op jit(solution)/shard_map/ppermute | solution.py:528
  23.5 0.6 %near.4 = (f32[32,64,128]{2,1,0:T(8,128)S(1)}, bf16[32,64,128]{2,1,0:T(8,128)(2,1)S(1)}) custom-call(s32[4,32]{1,0:T(4,128)S(4)} %get-tuple-element.64.ids, bf16[32,64,256]{2,1,0:T(8,128)(2,1)S(1)} %get-tuple-element.71.packed, bf16[32,64,128]{2,1,0:T(8,128)(2,1)S(1)} %get-tuple-element.94.field, f32[32,64,128]{2,1,0:T(8,128)S(1)} %get-tuple-element.95.state, ...), custom_call_target="tpu_custom_call" | custom-call | flops 134217728 | tf_op jit(solution)/shard_map/near/pallas_call | solution.py:33
  24.4 1.0 %collective-permute-done.11.refs_2_ = bf16[128,128]{1,0:T(8,128)(2,1)S(1)} collective-permute-done((bf16[128,128]{1,0:T(8,128)(2,1)S(1)}, bf16[128,128]{1,0:T(8,128)(2,1)S(1)}, u32[]{:S(2)}, u32[]{:S(2)}) %collective-permute-start.11) | collective-permute-done | bytes 32800 | tf_op jit(solution)/shard_map/ppermute | solution.py:57
  26.0 1.0 %collective-permute-start.14 = (bf16[128,128]{1,0:T(8,128)(2,1)S(1)}, bf16[128,128]{1,0:T(8,128)(2,1)S(1)}, u32[]{:S(2)}, u32[]{:S(2)}) collective-permute-start(bf16[128,128]{1,0:T(8,128)(2,1)S(1)} %get-tuple-element.103), channel_id=1, source_target_pairs={{0,8},{8,0},{2,10},{10,2},{4,12},{12,4},{6,14},{14,6},{16,24},{24,... | collective-permute-start | bytes 98312 | tf_op jit(solution)/shard_map/ppermute | solution.py:57
  27.0 0.9 %collective-permute-start.15 = (bf16[128,128]{1,0:T(8,128)(2,1)S(1)}, bf16[128,128]{1,0:T(8,128)(2,1)S(1)}, u32[]{:S(2)}, u32[]{:S(2)}) collective-permute-start(bf16[128,128]{1,0:T(8,128)(2,1)S(1)} %get-tuple-element.104), channel_id=1, source_target_pairs={{0,4},{4,0},{2,6},{6,2},{8,12},{12,8},{10,14},{14,10},{16,20},{20,... | collective-permute-start | bytes 98312 | tf_op jit(solution)/shard_map/ppermute | solution.py:57
  27.9 0.9 %near.5 = (f32[32,64,128]{2,1,0:T(8,128)S(1)}, bf16[32,64,128]{2,1,0:T(8,128)(2,1)S(1)}, f32[64,64,128]{2,1,0:T(8,128)S(1)}, f32[32,64,128]{2,1,0:T(8,128)S(1)}) custom-call(s32[4,32]{1,0:T(4,128)S(4)} %get-tuple-element.64.ids, bf16[32,64,256]{2,1,0:T(8,128)(2,1)S(1)} %get-tuple-element.71.packed, bf16[32,64,128]{2,1,0:T(8,128)(2,1)S(1)} %get-tuple-element.98.field, ...), custom_call_target="tpu_custom_call" | custom-call | flops 134217728 | tf_op jit(solution)/shard_map/near/pallas_call | solution.py:33
  28.9 1.6 %collective-permute-done.13.refs_0_ = bf16[128,128]{1,0:T(8,128)(2,1)S(1)} collective-permute-done((bf16[128,128]{1,0:T(8,128)(2,1)S(1)}, bf16[128,128]{1,0:T(8,128)(2,1)S(1)}, u32[]{:S(2)}, u32[]{:S(2)}) %collective-permute-start.13) | collective-permute-done | bytes 32800 | tf_op jit(solution)/shard_map/ppermute | solution.py:57
  31.0 0.8 %heat.1 = (f32[32,64,128]{2,1,0:T(8,128)S(1)}, bf16[32,64,128]{2,1,0:T(8,128)(2,1)S(1)}, f32[64,64,128]{2,1,0:T(8,128)S(1)}, bf16[1,1552,128]{2,1,0:T(8,128)(2,1...) custom-call(bf16[2,64,128]{2,1,0:T(8,128)(2,1)S(1)} %collective-perm, ...), custom_call_target="tpu_custom_call", output_to_operand_aliasing={{0}: (13, {}), {1}: (14, {}), {2}: (15, {})} | custom-call | flops 134217728 | tf_op jit(solution)/shard_map/heat/pallas_call | solution.py:33
  31.8 1.6 %collective-permute-start.21 = (bf16[1552,128]{1,0:T(8,128)(2,1)S(1)}, bf16[1552,128]{1,0:T(8,128)(2,1)S(1)}, u32[]{:S(2)}, u32[]{:S(2)}) collective-permute-start(bf16[1552,128]{1,0:T(8,128)(2,1)S(1)} %bitcast.12), channel_id=1, source_target_pairs={{0,1},{1,0},{2,3},{3,2},{4,5},{5,4},{6,7},{7,6},{8,9},{9,8},{10,11... | collective-permute-start | bytes 1191944 | tf_op jit(solution)/shard_map/ppermute | solution.py:553
  33.4 1.0 %collective-permute-start.18 = (bf16[128,128]{1,0:T(8,128)(2,1)S(1)}, bf16[128,128]{1,0:T(8,128)(2,1)S(1)}, u32[]{:S(2)}, u32[]{:S(2)}) collective-permute-start(bf16[128,128]{1,0:T(8,128)(2,1)S(1)} %get-tuple-element.110), channel_id=1, source_target_pairs={{0,8},{8,0},{2,10},{10,2},{4,12},{12,4},{6,14},{14,6},{16,24},{24,... | collective-permute-start | bytes 98312 | tf_op jit(solution)/shard_map/ppermute | solution.py:57
  34.9 2.6 %collective-permute-start.20 = (bf16[128,128]{1,0:T(8,128)(2,1)S(1)}, bf16[128,128]{1,0:T(8,128)(2,1)S(1)}, u32[]{:S(2)}, u32[]{:S(2)}) collective-permute-start(bf16[128,128]{1,0:T(8,128)(2,1)S(1)} %get-tuple-element.112), channel_id=1, source_target_pairs={{0,16},{16,0},{2,18},{18,2},{4,20},{20,4},{6,22},{22,6},{8,24},{24... | collective-permute-start | bytes 98312 | tf_op jit(solution)/shard_map/ppermute | solution.py:57
  37.6 1.6 %conduction.1 = (f32[32,64,128]{2,1,0:T(8,128)S(1)}, f32[32,64,128]{2,1,0:T(8,128)S(1)}) custom-call(s32[3,32]{1,0:T(4,128)S(1)} %bitcast.11, bf16[32,3,64,64]{3,2,1,0:T(8,128)(2,1)S(1)} %copy-done.1, f32[32,64]{1,0:T(8,128)S(1)} %copy-done.3, f32[32,64]{1,0:T(8,128)S(1)} %copy-done.4, bf16[4,64,64]{2,1,0:T(8,128)(2,1)S(1)} %copy-done.2, ...), custom_call_target="tpu_custom_call" | custom-call | flops 134217728 | tf_op jit(solution)/shard_map/conduction/pallas_call | solution.py:33
  39.2 0.8 %collective-permute-done.20.refs_3_ = bf16[128,128]{1,0:T(8,128)(2,1)S(1)} collective-permute-done((bf16[128,128]{1,0:T(8,128)(2,1)S(1)}, bf16[128,128]{1,0:T(8,128)(2,1)S(1)}, u32[]{:S(2)}, u32[]{:S(2)}) %collective-permute-start.20) | collective-permute-done | bytes 32800 | tf_op jit(solution)/shard_map/ppermute | solution.py:57
  40.2 0.5 %collective-permute-start.22 = (bf16[8,64,128]{2,1,0:T(8,128)(2,1)S(1)}, bf16[8,64,128]{2,1,0:T(8,128)(2,1)S(1)}, u32[]{:S(2)}, u32[]{:S(2)}) collective-permute-start(bf16[8,64,128]{2,1,0:T(8,128)(2,1)S(1)} %bitcast.13), channel_id=1, source_target_pairs={{0,1},{1,0},{2,3},{3,2},{4,5},{5,4},{6,7},{7,6},{8,9},{9,8},{10,11... | collective-permute-start | bytes 393224 | tf_op jit(solution)/shard_map/ppermute | solution.py:589
  40.8 0.7 %collective-permute-done.21.refs_1_ = bf16[1552,128]{1,0:T(8,128)(2,1)S(1)} collective-permute-done((bf16[1552,128]{1,0:T(8,128)(2,1)S(1)}, bf16[1552,128]{1,0:T(8,128)(2,1)S(1)}, u32[]{:S(2)}, u32[]{:S(2)}) %collective-permute-start.21) | collective-permute-done | bytes 397344 | tf_op jit(solution)/shard_map/ppermute | solution.py:553
  41.5 1.8 %early.1 = (f32[32,64,128]{2,1,0:T(8,128)S(1)}, bf16[32,64,128]{2,1,0:T(8,128)(2,1)S(1)}, f32[32,64,128]{2,1,0:T(8,128)}, s32[8]{0:T(128)S(4)}) custom-call(f32[64,64,128]{2,1,0:T(8,128)S(1)} %get-tuple-element.115.heat, f32[32,64,128]{2,1,0:T(8,128)S(1)} %get-tuple-element.117.gain, ...), custom_call_target="tpu_custom_call", output_to_operand_aliasing={{0}: (4, {}), {1}: (5, {})} | custom-call | tf_op jit(solution)/shard_map/early/pallas_call | solution.py:33
  43.3 0.8 %copy.46 = bf16[32,64,128]{2,1,0:T(8,128)(2,1)} copy(bf16[32,64,128]{2,1,0:T(8,128)(2,1)S(1)} %get-tuple-element.126) | data formatting | bytes 1048576
  44.1 1.1 %collective-permute-done.22.refs_1_ = bf16[8,64,128]{2,1,0:T(8,128)(2,1)S(1)} collective-permute-done((bf16[8,64,128]{2,1,0:T(8,128)(2,1)S(1)}, bf16[8,64,128]{2,1,0:T(8,128)(2,1)S(1)}, u32[]{:S(2)}, u32[]{:S(2)}) %collective-permute-start.22) | collective-permute-done | bytes 131104 | tf_op jit(solution)/shard_map/ppermute | solution.py:589
  45.2 0.8 %late.1 = f32[32,64,128]{2,1,0:T(8,128)} custom-call(f32[32,64,128]{2,1,0:T(8,128)S(1)} %get-tuple-element.117.gain, s32[8]{0:T(128)S(4)} %get-tuple-element.122.refs_0_, bf16[8,64,128]{2,1,0:T(8,128)(2,1)S(1)} %collective-permute-done.22.refs_1_, f32[32,64,128]{2,1,0:T(8,128)S(1)} %get-tuple-element.124.refs_2_, ...), custom_call_target="tpu_custom_call", output_to_operand_aliasing={{}: (4, {})} | custom-call | tf_op jit(solution)/shard_map/late/pallas_call | solution.py:33
  (44 shorter events, 3.4 us)
Async XLA Ops:
  0.6 11.4 %copy-start = (bf16[8,64,64]{2,1,0:T(8,128)(2,1)S(1)}, bf16[8,64,64]{2,1,0:T(8,128)(2,1)}, u32[]{:S(2)}) copy-start(bf16[8,64,64]{2,1,0:T(8,128)(2,1)} %admittance.9) | copy-start | bytes 196612
  2.0 10.0 %collective-permute-start = (bf16[128,128]{1,0:T(8,128)(2,1)S(1)}, bf16[128,128]{1,0:T(8,128)(2,1)S(1)}, u32[]{:S(2)}, u32[]{:S(2)}) collective-permute-start(bf16[128,128]{1,0:T(8,128)(2,1)S(1)} %get-tuple-element.73), channel_id=1, source_target_pairs={{0,16},{16,0},{2,18},{18,2},{4,20},{20,4},{6,22},{22,6},{8,24},{24... | collective-permute-start | bytes 98312 | tf_op jit(solution)/shard_map/ppermute | solution.py:57
  6.1 5.9 %collective-permute-start.1 = (bf16[128,128]{1,0:T(8,128)(2,1)S(1)}, bf16[128,128]{1,0:T(8,128)(2,1)S(1)}, u32[]{:S(2)}, u32[]{:S(2)}) collective-permute-start(bf16[128,128]{1,0:T(8,128)(2,1)S(1)} %get-tuple-element.74), channel_id=1, source_target_pairs={{0,4},{4,0},{2,6},{6,2},{8,12},{12,8},{10,14},{14,10},{16,20},{20,... | collective-permute-start | bytes 98312 | tf_op jit(solution)/shard_map/ppermute | solution.py:57
  7.6 4.4 %collective-permute-start.2 = (bf16[128,128]{1,0:T(8,128)(2,1)S(1)}, bf16[128,128]{1,0:T(8,128)(2,1)S(1)}, u32[]{:S(2)}, u32[]{:S(2)}) collective-permute-start(bf16[128,128]{1,0:T(8,128)(2,1)S(1)} %get-tuple-element.75), channel_id=1, source_target_pairs={{0,8},{8,0},{2,10},{10,2},{4,12},{12,4},{6,14},{14,6},{16,24},{24,... | collective-permute-start | bytes 98312 | tf_op jit(solution)/shard_map/ppermute | solution.py:57
  9.1 2.9 %collective-permute-start.3 = (bf16[128,128]{1,0:T(8,128)(2,1)S(1)}, bf16[128,128]{1,0:T(8,128)(2,1)S(1)}, u32[]{:S(2)}, u32[]{:S(2)}) collective-permute-start(bf16[128,128]{1,0:T(8,128)(2,1)S(1)} %get-tuple-element.76), channel_id=1, source_target_pairs={{0,2},{2,0},{4,6},{6,4},{8,10},{10,8},{12,14},{14,12},{16,18},{18,... | collective-permute-start | bytes 98312 | tf_op jit(solution)/shard_map/ppermute | solution.py:57
  12.3 4.9 %collective-permute-start.5 = (bf16[128,128]{1,0:T(8,128)(2,1)S(1)}, bf16[128,128]{1,0:T(8,128)(2,1)S(1)}, u32[]{:S(2)}, u32[]{:S(2)}) collective-permute-start(bf16[128,128]{1,0:T(8,128)(2,1)S(1)} %get-tuple-element.85), channel_id=1, source_target_pairs={{0,16},{16,0},{2,18},{18,2},{4,20},{20,4},{6,22},{22,6},{8,24},{24... | collective-permute-start | bytes 98312 | tf_op jit(solution)/shard_map/ppermute | solution.py:57
  12.7 4.5 %collective-permute-start.6 = (bf16[128,128]{1,0:T(8,128)(2,1)S(1)}, bf16[128,128]{1,0:T(8,128)(2,1)S(1)}, u32[]{:S(2)}, u32[]{:S(2)}) collective-permute-start(bf16[128,128]{1,0:T(8,128)(2,1)S(1)} %get-tuple-element.86), channel_id=1, source_target_pairs={{0,8},{8,0},{2,10},{10,2},{4,12},{12,4},{6,14},{14,6},{16,24},{24,... | collective-permute-start | bytes 98312 | tf_op jit(solution)/shard_map/ppermute | solution.py:57
  13.7 3.9 %collective-permute-start.7 = (bf16[128,128]{1,0:T(8,128)(2,1)S(1)}, bf16[128,128]{1,0:T(8,128)(2,1)S(1)}, u32[]{:S(2)}, u32[]{:S(2)}) collective-permute-start(bf16[128,128]{1,0:T(8,128)(2,1)S(1)} %get-tuple-element.87), channel_id=1, source_target_pairs={{0,4},{4,0},{2,6},{6,2},{8,12},{12,8},{10,14},{14,10},{16,20},{20,... | collective-permute-start | bytes 98312 | tf_op jit(solution)/shard_map/ppermute | solution.py:57
  14.6 3.0 %collective-permute-start.8 = (bf16[128,128]{1,0:T(8,128)(2,1)S(1)}, bf16[128,128]{1,0:T(8,128)(2,1)S(1)}, u32[]{:S(2)}, u32[]{:S(2)}) collective-permute-start(bf16[128,128]{1,0:T(8,128)(2,1)S(1)} %get-tuple-element.88), channel_id=1, source_target_pairs={{0,2},{2,0},{4,6},{6,4},{8,10},{10,8},{12,14},{14,12},{16,18},{18,... | collective-permute-start | bytes 98312 | tf_op jit(solution)/shard_map/ppermute | solution.py:57
  14.6 0.7 %copy-start.6 = (f32[8]{0:T(128)S(1)}, f32[8]{0:T(128)}, u32[]{:S(2)}) copy-start(f32[8]{0:T(128)} %kappas.1) | copy-start | bytes 100
  17.8 6.3 %collective-permute-start.9 = (bf16[128,128]{1,0:T(8,128)(2,1)S(1)}, bf16[128,128]{1,0:T(8,128)(2,1)S(1)}, u32[]{:S(2)}, u32[]{:S(2)}) collective-permute-start(bf16[128,128]{1,0:T(8,128)(2,1)S(1)} %get-tuple-element.90), channel_id=1, source_target_pairs={{0,16},{16,0},{2,18},{18,2},{4,20},{20,4},{6,22},{22,6},{8,24},{24... | collective-permute-start | bytes 98312 | tf_op jit(solution)/shard_map/ppermute | solution.py:57
  20.5 3.9 %collective-permute-start.10 = (bf16[128,128]{1,0:T(8,128)(2,1)S(1)}, bf16[128,128]{1,0:T(8,128)(2,1)S(1)}, u32[]{:S(2)}, u32[]{:S(2)}) collective-permute-start(bf16[128,128]{1,0:T(8,128)(2,1)S(1)} %get-tuple-element.91), channel_id=1, source_target_pairs={{0,8},{8,0},{2,10},{10,2},{4,12},{12,4},{6,14},{14,6},{16,24},{24,... | collective-permute-start | bytes 98312 | tf_op jit(solution)/shard_map/ppermute | solution.py:57
  21.5 3.9 %collective-permute-start.11 = (bf16[128,128]{1,0:T(8,128)(2,1)S(1)}, bf16[128,128]{1,0:T(8,128)(2,1)S(1)}, u32[]{:S(2)}, u32[]{:S(2)}) collective-permute-start(bf16[128,128]{1,0:T(8,128)(2,1)S(1)} %get-tuple-element.92), channel_id=1, source_target_pairs={{0,4},{4,0},{2,6},{6,2},{8,12},{12,8},{10,14},{14,10},{16,20},{20,... | collective-permute-start | bytes 98312 | tf_op jit(solution)/shard_map/ppermute | solution.py:57
  22.0 3.4 %collective-permute-start.12 = (bf16[128,128]{1,0:T(8,128)(2,1)S(1)}, bf16[128,128]{1,0:T(8,128)(2,1)S(1)}, u32[]{:S(2)}, u32[]{:S(2)}) collective-permute-start(bf16[128,128]{1,0:T(8,128)(2,1)S(1)} %get-tuple-element.93), channel_id=1, source_target_pairs={{0,2},{2,0},{4,6},{6,4},{8,10},{10,8},{12,14},{14,12},{16,18},{18,... | collective-permute-start | bytes 98312 | tf_op jit(solution)/shard_map/ppermute | solution.py:57
  22.0 6.8 %collective-permute-start.4 = (bf16[2,64,128]{2,1,0:T(8,128)(2,1)S(1)}, bf16[2,64,128]{2,1,0:T(8,128)(2,1)S(1)}, u32[]{:S(2)}, u32[]{:S(2)}) collective-permute-start(bf16[2,64,128]{2,1,0:T(8,128)(2,1)S(1)} %get-tuple-element.84.token), channel_id=1, source_target_pairs={{0,1},{1,0},{2,3},{3,2},{4,5},{5,4},{6,7},{7,6},{8,9},{9,8},{10,11... | collective-permute-start | bytes 98312 | tf_op jit(solution)/shard_map/ppermute | solution.py:528
  25.6 4.9 %collective-permute-start.13 = (bf16[128,128]{1,0:T(8,128)(2,1)S(1)}, bf16[128,128]{1,0:T(8,128)(2,1)S(1)}, u32[]{:S(2)}, u32[]{:S(2)}) collective-permute-start(bf16[128,128]{1,0:T(8,128)(2,1)S(1)} %get-tuple-element.102), channel_id=1, source_target_pairs={{0,16},{16,0},{2,18},{18,2},{4,20},{20,4},{6,22},{22,6},{8,24},{24... | collective-permute-start | bytes 98312 | tf_op jit(solution)/shard_map/ppermute | solution.py:57
  26.0 4.5 %collective-permute-start.14 = (bf16[128,128]{1,0:T(8,128)(2,1)S(1)}, bf16[128,128]{1,0:T(8,128)(2,1)S(1)}, u32[]{:S(2)}, u32[]{:S(2)}) collective-permute-start(bf16[128,128]{1,0:T(8,128)(2,1)S(1)} %get-tuple-element.103), channel_id=1, source_target_pairs={{0,8},{8,0},{2,10},{10,2},{4,12},{12,4},{6,14},{14,6},{16,24},{24,... | collective-permute-start | bytes 98312 | tf_op jit(solution)/shard_map/ppermute | solution.py:57
  27.0 3.9 %collective-permute-start.15 = (bf16[128,128]{1,0:T(8,128)(2,1)S(1)}, bf16[128,128]{1,0:T(8,128)(2,1)S(1)}, u32[]{:S(2)}, u32[]{:S(2)}) collective-permute-start(bf16[128,128]{1,0:T(8,128)(2,1)S(1)} %get-tuple-element.104), channel_id=1, source_target_pairs={{0,4},{4,0},{2,6},{6,2},{8,12},{12,8},{10,14},{14,10},{16,20},{20,... | collective-permute-start | bytes 98312 | tf_op jit(solution)/shard_map/ppermute | solution.py:57
  27.9 3.0 %collective-permute-start.16 = (bf16[128,128]{1,0:T(8,128)(2,1)S(1)}, bf16[128,128]{1,0:T(8,128)(2,1)S(1)}, u32[]{:S(2)}, u32[]{:S(2)}) collective-permute-start(bf16[128,128]{1,0:T(8,128)(2,1)S(1)} %get-tuple-element.105), channel_id=1, source_target_pairs={{0,2},{2,0},{4,6},{6,4},{8,10},{10,8},{12,14},{14,12},{16,18},{18,... | collective-permute-start | bytes 98312 | tf_op jit(solution)/shard_map/ppermute | solution.py:57
  30.9 6.6 %copy-start.1 = (bf16[32,3,64,64]{3,2,1,0:T(8,128)(2,1)S(1)}, bf16[32,3,64,64]{3,2,1,0:T(8,128)(2,1)}, u32[]{:S(2)}) copy-start(bf16[32,3,64,64]{3,2,1,0:T(8,128)(2,1)} %tiles.3) | copy-start | bytes 2359300
  30.9 6.6 %copy-start.2 = (bf16[4,64,64]{2,1,0:T(8,128)(2,1)S(1)}, bf16[4,64,64]{2,1,0:T(8,128)(2,1)}, u32[]{:S(2)}) copy-start(bf16[4,64,64]{2,1,0:T(8,128)(2,1)} %couplings.1) | copy-start | bytes 98308
  30.9 6.6 %copy-start.3 = (f32[32,64]{1,0:T(8,128)S(1)}, f32[32,64]{1,0:T(8,128)}, u32[]{:S(2)}) copy-start(f32[32,64]{1,0:T(8,128)} %coefficient.1) | copy-start | bytes 24580
  31.0 6.6 %copy-start.4 = (f32[32,64]{1,0:T(8,128)S(1)}, f32[32,64]{1,0:T(8,128)}, u32[]{:S(2)}) copy-start(f32[32,64]{1,0:T(8,128)} %storage.1) | copy-start | bytes 24580
  31.0 6.6 %copy-start.5 = (s32[32,3]{0,1:T(4,128)S(1)}, s32[32,3]{0,1:T(4,128)}, u32[]{:S(2)}) copy-start(s32[32,3]{0,1:T(4,128)} %param.27) | copy-start | bytes 1156
  31.8 9.7 %collective-permute-start.21 = (bf16[1552,128]{1,0:T(8,128)(2,1)S(1)}, bf16[1552,128]{1,0:T(8,128)(2,1)S(1)}, u32[]{:S(2)}, u32[]{:S(2)}) collective-permute-start(bf16[1552,128]{1,0:T(8,128)(2,1)S(1)} %bitcast.12), channel_id=1, source_target_pairs={{0,1},{1,0},{2,3},{3,2},{4,5},{5,4},{6,7},{7,6},{8,9},{9,8},{10,11... | collective-permute-start | bytes 1191944 | tf_op jit(solution)/shard_map/ppermute | solution.py:553
  33.4 5.8 %collective-permute-start.17 = (bf16[128,128]{1,0:T(8,128)(2,1)S(1)}, bf16[128,128]{1,0:T(8,128)(2,1)S(1)}, u32[]{:S(2)}, u32[]{:S(2)}) collective-permute-start(bf16[128,128]{1,0:T(8,128)(2,1)S(1)} %get-tuple-element.109), channel_id=1, source_target_pairs={{0,2},{2,0},{4,6},{6,4},{8,10},{10,8},{12,14},{14,12},{16,18},{18,... | collective-permute-start | bytes 98312 | tf_op jit(solution)/shard_map/ppermute | solution.py:57
  33.4 5.8 %collective-permute-start.18 = (bf16[128,128]{1,0:T(8,128)(2,1)S(1)}, bf16[128,128]{1,0:T(8,128)(2,1)S(1)}, u32[]{:S(2)}, u32[]{:S(2)}) collective-permute-start(bf16[128,128]{1,0:T(8,128)(2,1)S(1)} %get-tuple-element.110), channel_id=1, source_target_pairs={{0,8},{8,0},{2,10},{10,2},{4,12},{12,4},{6,14},{14,6},{16,24},{24,... | collective-permute-start | bytes 98312 | tf_op jit(solution)/shard_map/ppermute | solution.py:57
  34.4 4.8 %collective-permute-start.19 = (bf16[128,128]{1,0:T(8,128)(2,1)S(1)}, bf16[128,128]{1,0:T(8,128)(2,1)S(1)}, u32[]{:S(2)}, u32[]{:S(2)}) collective-permute-start(bf16[128,128]{1,0:T(8,128)(2,1)S(1)} %get-tuple-element.111), channel_id=1, source_target_pairs={{0,4},{4,0},{2,6},{6,2},{8,12},{12,8},{10,14},{14,10},{16,20},{20,... | collective-permute-start | bytes 98312 | tf_op jit(solution)/shard_map/ppermute | solution.py:57
  34.9 5.1 %collective-permute-start.20 = (bf16[128,128]{1,0:T(8,128)(2,1)S(1)}, bf16[128,128]{1,0:T(8,128)(2,1)S(1)}, u32[]{:S(2)}, u32[]{:S(2)}) collective-permute-start(bf16[128,128]{1,0:T(8,128)(2,1)S(1)} %get-tuple-element.112), channel_id=1, source_target_pairs={{0,16},{16,0},{2,18},{18,2},{4,20},{20,4},{6,22},{22,6},{8,24},{24... | collective-permute-start | bytes 98312 | tf_op jit(solution)/shard_map/ppermute | solution.py:57
  40.2 5.0 %collective-permute-start.22 = (bf16[8,64,128]{2,1,0:T(8,128)(2,1)S(1)}, bf16[8,64,128]{2,1,0:T(8,128)(2,1)S(1)}, u32[]{:S(2)}, u32[]{:S(2)}) collective-permute-start(bf16[8,64,128]{2,1,0:T(8,128)(2,1)S(1)} %bitcast.13), channel_id=1, source_target_pairs={{0,1},{1,0},{2,3},{3,2},{4,5},{5,4},{6,7},{7,6},{8,9},{9,8},{10,11... | collective-permute-start | bytes 393224 | tf_op jit(solution)/shard_map/ppermute | solution.py:589

commit v3 on v2

--- a/solution.py
+++ b/solution.py
@@ -82,14 +82,12 @@
         c.start()
     copies[0].wait()
     copies[1].wait()
-    scale = relax_factor / diag_v[...]
-    rows = lax.broadcasted_iota(I32, scale.shape, 0)
-    chosen = []
-    for b in range(levels):
-        for f in range(face_ids.shape[0]):
-            mine = jnp.where(rows == face_ids_s[f, b], scale, 0.0)
-            chosen.append(jnp.sum(mine, axis=0, keepdims=True))
-    turned = jnp.concatenate(chosen, axis=0).T
+    chosen = [
+        diag_v[pl.ds(face_ids_s[f, b], 1), :]
+        for b in range(levels)
+        for f in range(face_ids.shape[0])
+    ]
+    turned = (relax_factor / jnp.concatenate(chosen, axis=0)).T
     copies[2].wait()
     for b in range(levels):
         for f in range(face_ids.shape[0]):

time: 46.2 us -> 46.2 us (level)
  no operation moved by 1% of the time
where the time goes in v3:
time: 46.2 us; the launch traced here: 46 us
  starting transfers between devices  23.8 us (52%)
  Pallas kernels  13.2 us (29%)
  waiting for transfers between devices  7.35 us (16%)
  between operations  0.87 us (2%)
  local copies, waits for them, and re-layouts  0.83 us (2%)
    ppermute x20, starting transfers between devices, from_partner(): return lax.ppermute(block, axis, route)  20.2 us
    pallas_call x14, Pallas kernels, call(): pl.pallas_call(kernel, out_shape=[SPACES[id(spec)](shape, dtype) for shap...  13.2 us
    ppermute x20, waiting for transfers between devices, from_partner(): return lax.ppermute(block, axis, route)  5.49 us
    ppermute x1, starting transfers between devices, body(): soon = [lax.ppermute(soon[s], 'therm', routes[s]) for s in range(shifts)]  1.59 us
    ppermute x1, starting transfers between devices, body(): below = above = lax.ppermute(edges[0], 'therm', [(0, 1), (1, 0)])  1.52 us
    ppermute x1, waiting for transfers between devices, body(): late = [lax.ppermute(late[s], 'therm', routes[s]) for s in range(shifts)]  1.15 us
  transfers between devices with their start and end apart: 23, of which 9 were waited for; matrix products, arithmetic and copies ran while one was open for 2% of the time, Pallas kernels for 21%

profile of v3, /device:TPU:0, one launch (start us, length us, event | category | flops | bytes accessed | tf_op | source)
XLA Modules:
  0.0 46.0 jit_solution(6439766242683623590)
XLA Ops:
  0.6 1.3 %start.1 = (bf16[32,64,128]{2,1,0:T(8,128)(2,1)S(1)}, f32[32,64]{1,0:T(8,128)S(1)}, s32[2,4]{1,0:T(2,128)S(4)}, s32[4,32]{1,0:T(4,128)S(4)}, s32[1,32]{1,0:T(1,1...) custom-call(bf16[32,64,128]{2,1,0:T(8,128)(2,1)} %amps.1, ...), custom_call_target="tpu_custom_call" | custom-call | tf_op jit(solution)/shard_map/start/pallas_call | solution.py:33
  2.0 4.1 %collective-permute-start = (bf16[128,128]{1,0:T(8,128)(2,1)S(1)}, bf16[128,128]{1,0:T(8,128)(2,1)S(1)}, u32[]{:S(2)}, u32[]{:S(2)}) collective-permute-start(bf16[128,128]{1,0:T(8,128)(2,1)S(1)} %get-tuple-element.73), channel_id=1, source_target_pairs={{0,16},{16,0},{2,18},{18,2},{4,20},{20,4},{6,22},{22,6},{8,24},{24... | collective-permute-start | bytes 98312 | tf_op jit(solution)/shard_map/ppermute | solution.py:57
  6.1 1.5 %collective-permute-start.1 = (bf16[128,128]{1,0:T(8,128)(2,1)S(1)}, bf16[128,128]{1,0:T(8,128)(2,1)S(1)}, u32[]{:S(2)}, u32[]{:S(2)}) collective-permute-start(bf16[128,128]{1,0:T(8,128)(2,1)S(1)} %get-tuple-element.74), channel_id=1, source_target_pairs={{0,4},{4,0},{2,6},{6,2},{8,12},{12,8},{10,14},{14,10},{16,20},{20,... | collective-permute-start | bytes 98312 | tf_op jit(solution)/shard_map/ppermute | solution.py:57
  7.6 1.6 %collective-permute-start.2 = (bf16[128,128]{1,0:T(8,128)(2,1)S(1)}, bf16[128,128]{1,0:T(8,128)(2,1)S(1)}, u32[]{:S(2)}, u32[]{:S(2)}) collective-permute-start(bf16[128,128]{1,0:T(8,128)(2,1)S(1)} %get-tuple-element.75), channel_id=1, source_target_pairs={{0,8},{8,0},{2,10},{10,2},{4,12},{12,4},{6,14},{14,6},{16,24},{24,... | collective-permute-start | bytes 98312 | tf_op jit(solution)/shard_map/ppermute | solution.py:57
  9.1 2.8 %first.1 = (bf16[32,64,256]{2,1,0:T(8,128)(2,1)S(1)}, f32[32,64,128]{2,1,0:T(8,128)S(1)}, bf16[32,64,128]{2,1,0:T(8,128)(2,1)S(1)}, f32[32,64,128]{2,1,0:T(8,128...) custom-call(s32[4,32]{1,0:T(4,128)S(4)} %get-tuple-element.64.ids, ...), custom_call_target="tpu_custom_call" | custom-call | flops 134217728 | tf_op jit(solution)/shard_map/first/pallas_call | solution.py:33
  12.7 1.0 %collective-permute-start.6 = (bf16[128,128]{1,0:T(8,128)(2,1)S(1)}, bf16[128,128]{1,0:T(8,128)(2,1)S(1)}, u32[]{:S(2)}, u32[]{:S(2)}) collective-permute-start(bf16[128,128]{1,0:T(8,128)(2,1)S(1)} %get-tuple-element.86), channel_id=1, source_target_pairs={{0,8},{8,0},{2,10},{10,2},{4,12},{12,4},{6,14},{14,6},{16,24},{24,... | collective-permute-start | bytes 98312 | tf_op jit(solution)/shard_map/ppermute | solution.py:57
  13.7 0.9 %collective-permute-start.7 = (bf16[128,128]{1,0:T(8,128)(2,1)S(1)}, bf16[128,128]{1,0:T(8,128)(2,1)S(1)}, u32[]{:S(2)}, u32[]{:S(2)}) collective-permute-start(bf16[128,128]{1,0:T(8,128)(2,1)S(1)} %get-tuple-element.87), channel_id=1, source_target_pairs={{0,4},{4,0},{2,6},{6,2},{8,12},{12,8},{10,14},{14,10},{16,20},{20,... | collective-permute-start | bytes 98312 | tf_op jit(solution)/shard_map/ppermute | solution.py:57
  14.6 0.6 %near.3 = (f32[32,64,128]{2,1,0:T(8,128)S(1)}, bf16[32,64,128]{2,1,0:T(8,128)(2,1)S(1)}) custom-call(s32[4,32]{1,0:T(4,128)S(4)} %get-tuple-element.64.ids, bf16[32,64,256]{2,1,0:T(8,128)(2,1)S(1)} %get-tuple-element.71.packed, bf16[32,64,128]{2,1,0:T(8,128)(2,1)S(1)} %get-tuple-element.79.field, f32[32,64,128]{2,1,0:T(8,128)S(1)} %get-tuple-element.80.state, ...), custom_call_target="tpu_custom_call" | custom-call | flops 134217728 | tf_op jit(solution)/shard_map/near/pallas_call | solution.py:33
  15.2 1.0 %flux.1 = (bf16[32,64,128]{2,1,0:T(8,128)(2,1)S(1)}, bf16[2,64,128]{2,1,0:T(8,128)(2,1)S(1)}) custom-call(bf16[32,64,128]{2,1,0:T(8,128)(2,1)S(1)} %get-tuple-element.81.token.refs_5_, f32[8]{0:T(128)S(1)} %copy-done.6, s32[32,64]{1,0:T(8,128)S(1)} %get-tuple-element.82.kind, bf16[32,64,128]{2,1,0:T(8,128)(2,1)S(1)} %get-tuple-element.83.warmth), custom_call_target="tpu_custom_call" | custom-call | tf_op jit(solution)/shard_map/flux/pallas_call | solution.py:33
  16.3 0.8 %collective-permute-done.5.refs_0_ = bf16[128,128]{1,0:T(8,128)(2,1)S(1)} collective-permute-done((bf16[128,128]{1,0:T(8,128)(2,1)S(1)}, bf16[128,128]{1,0:T(8,128)(2,1)S(1)}, u32[]{:S(2)}, u32[]{:S(2)}) %collective-permute-start.5) | collective-permute-done | bytes 32800 | tf_op jit(solution)/shard_map/ppermute | solution.py:57
  17.8 2.7 %collective-permute-start.9 = (bf16[128,128]{1,0:T(8,128)(2,1)S(1)}, bf16[128,128]{1,0:T(8,128)(2,1)S(1)}, u32[]{:S(2)}, u32[]{:S(2)}) collective-permute-start(bf16[128,128]{1,0:T(8,128)(2,1)S(1)} %get-tuple-element.90), channel_id=1, source_target_pairs={{0,16},{16,0},{2,18},{18,2},{4,20},{20,4},{6,22},{22,6},{8,24},{24... | collective-permute-start | bytes 98312 | tf_op jit(solution)/shard_map/ppermute | solution.py:57
  20.5 1.0 %collective-permute-start.10 = (bf16[128,128]{1,0:T(8,128)(2,1)S(1)}, bf16[128,128]{1,0:T(8,128)(2,1)S(1)}, u32[]{:S(2)}, u32[]{:S(2)}) collective-permute-start(bf16[128,128]{1,0:T(8,128)(2,1)S(1)} %get-tuple-element.91), channel_id=1, source_target_pairs={{0,8},{8,0},{2,10},{10,2},{4,12},{12,4},{6,14},{14,6},{16,24},{24,... | collective-permute-start | bytes 98312 | tf_op jit(solution)/shard_map/ppermute | solution.py:57
  21.5 0.5 %collective-permute-start.11 = (bf16[128,128]{1,0:T(8,128)(2,1)S(1)}, bf16[128,128]{1,0:T(8,128)(2,1)S(1)}, u32[]{:S(2)}, u32[]{:S(2)}) collective-permute-start(bf16[128,128]{1,0:T(8,128)(2,1)S(1)} %get-tuple-element.92), channel_id=1, source_target_pairs={{0,4},{4,0},{2,6},{6,2},{8,12},{12,8},{10,14},{14,10},{16,20},{20,... | collective-permute-start | bytes 98312 | tf_op jit(solution)/shard_map/ppermute | solution.py:57
  22.0 1.5 %collective-permute-start.4 = (bf16[2,64,128]{2,1,0:T(8,128)(2,1)S(1)}, bf16[2,64,128]{2,1,0:T(8,128)(2,1)S(1)}, u32[]{:S(2)}, u32[]{:S(2)}) collective-permute-start(bf16[2,64,128]{2,1,0:T(8,128)(2,1)S(1)} %get-tuple-element.84.token), channel_id=1, source_target_pairs={{0,1},{1,0},{2,3},{3,2},{4,5},{5,4},{6,7},{7,6},{8,9},{9,8},{10,11... | collective-permute-start | bytes 98312 | tf_op jit(solution)/shard_map/ppermute | solution.py:526
  23.5 0.6 %near.4 = (f32[32,64,128]{2,1,0:T(8,128)S(1)}, bf16[32,64,128]{2,1,0:T(8,128)(2,1)S(1)}) custom-call(s32[4,32]{1,0:T(4,128)S(4)} %get-tuple-element.64.ids, bf16[32,64,256]{2,1,0:T(8,128)(2,1)S(1)} %get-tuple-element.71.packed, bf16[32,64,128]{2,1,0:T(8,128)(2,1)S(1)} %get-tuple-element.94.field, f32[32,64,128]{2,1,0:T(8,128)S(1)} %get-tuple-element.95.state, ...), custom_call_target="tpu_custom_call" | custom-call | flops 134217728 | tf_op jit(solution)/shard_map/near/pallas_call | solution.py:33
  24.4 1.0 %collective-permute-done.11.refs_2_ = bf16[128,128]{1,0:T(8,128)(2,1)S(1)} collective-permute-done((bf16[128,128]{1,0:T(8,128)(2,1)S(1)}, bf16[128,128]{1,0:T(8,128)(2,1)S(1)}, u32[]{:S(2)}, u32[]{:S(2)}) %collective-permute-start.11) | collective-permute-done | bytes 32800 | tf_op jit(solution)/shard_map/ppermute | solution.py:57
  26.0 1.0 %collective-permute-start.14 = (bf16[128,128]{1,0:T(8,128)(2,1)S(1)}, bf16[128,128]{1,0:T(8,128)(2,1)S(1)}, u32[]{:S(2)}, u32[]{:S(2)}) collective-permute-start(bf16[128,128]{1,0:T(8,128)(2,1)S(1)} %get-tuple-element.103), channel_id=1, source_target_pairs={{0,8},{8,0},{2,10},{10,2},{4,12},{12,4},{6,14},{14,6},{16,24},{24,... | collective-permute-start | bytes 98312 | tf_op jit(solution)/shard_map/ppermute | solution.py:57
  27.0 0.9 %collective-permute-start.15 = (bf16[128,128]{1,0:T(8,128)(2,1)S(1)}, bf16[128,128]{1,0:T(8,128)(2,1)S(1)}, u32[]{:S(2)}, u32[]{:S(2)}) collective-permute-start(bf16[128,128]{1,0:T(8,128)(2,1)S(1)} %get-tuple-element.104), channel_id=1, source_target_pairs={{0,4},{4,0},{2,6},{6,2},{8,12},{12,8},{10,14},{14,10},{16,20},{20,... | collective-permute-start | bytes 98312 | tf_op jit(solution)/shard_map/ppermute | solution.py:57
  27.9 0.9 %near.5 = (f32[32,64,128]{2,1,0:T(8,128)S(1)}, bf16[32,64,128]{2,1,0:T(8,128)(2,1)S(1)}, f32[64,64,128]{2,1,0:T(8,128)S(1)}, f32[32,64,128]{2,1,0:T(8,128)S(1)}) custom-call(s32[4,32]{1,0:T(4,128)S(4)} %get-tuple-element.64.ids, bf16[32,64,256]{2,1,0:T(8,128)(2,1)S(1)} %get-tuple-element.71.packed, bf16[32,64,128]{2,1,0:T(8,128)(2,1)S(1)} %get-tuple-element.98.field, ...), custom_call_target="tpu_custom_call" | custom-call | flops 134217728 | tf_op jit(solution)/shard_map/near/pallas_call | solution.py:33
  28.8 1.6 %collective-permute-done.13.refs_0_ = bf16[128,128]{1,0:T(8,128)(2,1)S(1)} collective-permute-done((bf16[128,128]{1,0:T(8,128)(2,1)S(1)}, bf16[128,128]{1,0:T(8,128)(2,1)S(1)}, u32[]{:S(2)}, u32[]{:S(2)}) %collective-permute-start.13) | collective-permute-done | bytes 32800 | tf_op jit(solution)/shard_map/ppermute | solution.py:57
  31.0 0.8 %heat.1 = (f32[32,64,128]{2,1,0:T(8,128)S(1)}, bf16[32,64,128]{2,1,0:T(8,128)(2,1)S(1)}, f32[64,64,128]{2,1,0:T(8,128)S(1)}, bf16[1,1552,128]{2,1,0:T(8,128)(2,1...) custom-call(bf16[2,64,128]{2,1,0:T(8,128)(2,1)S(1)} %collective-perm, ...), custom_call_target="tpu_custom_call", output_to_operand_aliasing={{0}: (13, {}), {1}: (14, {}), {2}: (15, {})} | custom-call | flops 134217728 | tf_op jit(solution)/shard_map/heat/pallas_call | solution.py:33
  31.8 1.6 %collective-permute-start.21 = (bf16[1552,128]{1,0:T(8,128)(2,1)S(1)}, bf16[1552,128]{1,0:T(8,128)(2,1)S(1)}, u32[]{:S(2)}, u32[]{:S(2)}) collective-permute-start(bf16[1552,128]{1,0:T(8,128)(2,1)S(1)} %bitcast.12), channel_id=1, source_target_pairs={{0,1},{1,0},{2,3},{3,2},{4,5},{5,4},{6,7},{7,6},{8,9},{9,8},{10,11... | collective-permute-start | bytes 1191944 | tf_op jit(solution)/shard_map/ppermute | solution.py:551
  33.4 1.0 %collective-permute-start.18 = (bf16[128,128]{1,0:T(8,128)(2,1)S(1)}, bf16[128,128]{1,0:T(8,128)(2,1)S(1)}, u32[]{:S(2)}, u32[]{:S(2)}) collective-permute-start(bf16[128,128]{1,0:T(8,128)(2,1)S(1)} %get-tuple-element.110), channel_id=1, source_target_pairs={{0,8},{8,0},{2,10},{10,2},{4,12},{12,4},{6,14},{14,6},{16,24},{24,... | collective-permute-start | bytes 98312 | tf_op jit(solution)/shard_map/ppermute | solution.py:57
  34.9 2.6 %collective-permute-start.20 = (bf16[128,128]{1,0:T(8,128)(2,1)S(1)}, bf16[128,128]{1,0:T(8,128)(2,1)S(1)}, u32[]{:S(2)}, u32[]{:S(2)}) collective-permute-start(bf16[128,128]{1,0:T(8,128)(2,1)S(1)} %get-tuple-element.112), channel_id=1, source_target_pairs={{0,16},{16,0},{2,18},{18,2},{4,20},{20,4},{6,22},{22,6},{8,24},{24... | collective-permute-start | bytes 98312 | tf_op jit(solution)/shard_map/ppermute | solution.py:57
  37.6 1.6 %conduction.1 = (f32[32,64,128]{2,1,0:T(8,128)S(1)}, f32[32,64,128]{2,1,0:T(8,128)S(1)}) custom-call(s32[3,32]{1,0:T(4,128)S(1)} %bitcast.11, bf16[32,3,64,64]{3,2,1,0:T(8,128)(2,1)S(1)} %copy-done.1, f32[32,64]{1,0:T(8,128)S(1)} %copy-done.3, f32[32,64]{1,0:T(8,128)S(1)} %copy-done.4, bf16[4,64,64]{2,1,0:T(8,128)(2,1)S(1)} %copy-done.2, ...), custom_call_target="tpu_custom_call" | custom-call | flops 134217728 | tf_op jit(solution)/shard_map/conduction/pallas_call | solution.py:33
  39.2 0.8 %collective-permute-done.20.refs_3_ = bf16[128,128]{1,0:T(8,128)(2,1)S(1)} collective-permute-done((bf16[128,128]{1,0:T(8,128)(2,1)S(1)}, bf16[128,128]{1,0:T(8,128)(2,1)S(1)}, u32[]{:S(2)}, u32[]{:S(2)}) %collective-permute-start.20) | collective-permute-done | bytes 32800 | tf_op jit(solution)/shard_map/ppermute | solution.py:57
  40.2 0.5 %collective-permute-start.22 = (bf16[8,64,128]{2,1,0:T(8,128)(2,1)S(1)}, bf16[8,64,128]{2,1,0:T(8,128)(2,1)S(1)}, u32[]{:S(2)}, u32[]{:S(2)}) collective-permute-start(bf16[8,64,128]{2,1,0:T(8,128)(2,1)S(1)} %bitcast.13), channel_id=1, source_target_pairs={{0,1},{1,0},{2,3},{3,2},{4,5},{5,4},{6,7},{7,6},{8,9},{9,8},{10,11... | collective-permute-start | bytes 393224 | tf_op jit(solution)/shard_map/ppermute | solution.py:587
  40.8 0.7 %collective-permute-done.21.refs_1_ = bf16[1552,128]{1,0:T(8,128)(2,1)S(1)} collective-permute-done((bf16[1552,128]{1,0:T(8,128)(2,1)S(1)}, bf16[1552,128]{1,0:T(8,128)(2,1)S(1)}, u32[]{:S(2)}, u32[]{:S(2)}) %collective-permute-start.21) | collective-permute-done | bytes 397344 | tf_op jit(solution)/shard_map/ppermute | solution.py:551
  41.5 1.8 %early.1 = (f32[32,64,128]{2,1,0:T(8,128)S(1)}, bf16[32,64,128]{2,1,0:T(8,128)(2,1)S(1)}, f32[32,64,128]{2,1,0:T(8,128)}, s32[8]{0:T(128)S(4)}) custom-call(f32[64,64,128]{2,1,0:T(8,128)S(1)} %get-tuple-element.115.heat, f32[32,64,128]{2,1,0:T(8,128)S(1)} %get-tuple-element.117.gain, ...), custom_call_target="tpu_custom_call", output_to_operand_aliasing={{0}: (4, {}), {1}: (5, {})} | custom-call | tf_op jit(solution)/shard_map/early/pallas_call | solution.py:33
  43.3 0.8 %copy.46 = bf16[32,64,128]{2,1,0:T(8,128)(2,1)} copy(bf16[32,64,128]{2,1,0:T(8,128)(2,1)S(1)} %get-tuple-element.126) | data formatting | bytes 1048576
  44.1 1.1 %collective-permute-done.22.refs_1_ = bf16[8,64,128]{2,1,0:T(8,128)(2,1)S(1)} collective-permute-done((bf16[8,64,128]{2,1,0:T(8,128)(2,1)S(1)}, bf16[8,64,128]{2,1,0:T(8,128)(2,1)S(1)}, u32[]{:S(2)}, u32[]{:S(2)}) %collective-permute-start.22) | collective-permute-done | bytes 131104 | tf_op jit(solution)/shard_map/ppermute | solution.py:587
  45.2 0.8 %late.1 = f32[32,64,128]{2,1,0:T(8,128)} custom-call(f32[32,64,128]{2,1,0:T(8,128)S(1)} %get-tuple-element.117.gain, s32[8]{0:T(128)S(4)} %get-tuple-element.122.refs_0_, bf16[8,64,128]{2,1,0:T(8,128)(2,1)S(1)} %collective-permute-done.22.refs_1_, f32[32,64,128]{2,1,0:T(8,128)S(1)} %get-tuple-element.124.refs_2_, ...), custom_call_target="tpu_custom_call", output_to_operand_aliasing={{}: (4, {})} | custom-call | tf_op jit(solution)/shard_map/late/pallas_call | solution.py:33
  (44 shorter events, 3.4 us)
Async XLA Ops:
  0.6 11.4 %copy-start = (bf16[8,64,64]{2,1,0:T(8,128)(2,1)S(1)}, bf16[8,64,64]{2,1,0:T(8,128)(2,1)}, u32[]{:S(2)}) copy-start(bf16[8,64,64]{2,1,0:T(8,128)(2,1)} %admittance.9) | copy-start | bytes 196612
  2.0 10.0 %collective-permute-start = (bf16[128,128]{1,0:T(8,128)(2,1)S(1)}, bf16[128,128]{1,0:T(8,128)(2,1)S(1)}, u32[]{:S(2)}, u32[]{:S(2)}) collective-permute-start(bf16[128,128]{1,0:T(8,128)(2,1)S(1)} %get-tuple-element.73), channel_id=1, source_target_pairs={{0,16},{16,0},{2,18},{18,2},{4,20},{20,4},{6,22},{22,6},{8,24},{24... | collective-permute-start | bytes 98312 | tf_op jit(solution)/shard_map/ppermute | solution.py:57
  6.1 5.9 %collective-permute-start.1 = (bf16[128,128]{1,0:T(8,128)(2,1)S(1)}, bf16[128,128]{1,0:T(8,128)(2,1)S(1)}, u32[]{:S(2)}, u32[]{:S(2)}) collective-permute-start(bf16[128,128]{1,0:T(8,128)(2,1)S(1)} %get-tuple-element.74), channel_id=1, source_target_pairs={{0,4},{4,0},{2,6},{6,2},{8,12},{12,8},{10,14},{14,10},{16,20},{20,... | collective-permute-start | bytes 98312 | tf_op jit(solution)/shard_map/ppermute | solution.py:57
  7.6 4.4 %collective-permute-start.2 = (bf16[128,128]{1,0:T(8,128)(2,1)S(1)}, bf16[128,128]{1,0:T(8,128)(2,1)S(1)}, u32[]{:S(2)}, u32[]{:S(2)}) collective-permute-start(bf16[128,128]{1,0:T(8,128)(2,1)S(1)} %get-tuple-element.75), channel_id=1, source_target_pairs={{0,8},{8,0},{2,10},{10,2},{4,12},{12,4},{6,14},{14,6},{16,24},{24,... | collective-permute-start | bytes 98312 | tf_op jit(solution)/shard_map/ppermute | solution.py:57
  9.1 2.9 %collective-permute-start.3 = (bf16[128,128]{1,0:T(8,128)(2,1)S(1)}, bf16[128,128]{1,0:T(8,128)(2,1)S(1)}, u32[]{:S(2)}, u32[]{:S(2)}) collective-permute-start(bf16[128,128]{1,0:T(8,128)(2,1)S(1)} %get-tuple-element.76), channel_id=1, source_target_pairs={{0,2},{2,0},{4,6},{6,4},{8,10},{10,8},{12,14},{14,12},{16,18},{18,... | collective-permute-start | bytes 98312 | tf_op jit(solution)/shard_map/ppermute | solution.py:57
  12.3 4.9 %collective-permute-start.5 = (bf16[128,128]{1,0:T(8,128)(2,1)S(1)}, bf16[128,128]{1,0:T(8,128)(2,1)S(1)}, u32[]{:S(2)}, u32[]{:S(2)}) collective-permute-start(bf16[128,128]{1,0:T(8,128)(2,1)S(1)} %get-tuple-element.85), channel_id=1, source_target_pairs={{0,16},{16,0},{2,18},{18,2},{4,20},{20,4},{6,22},{22,6},{8,24},{24... | collective-permute-start | bytes 98312 | tf_op jit(solution)/shard_map/ppermute | solution.py:57
  12.7 4.5 %collective-permute-start.6 = (bf16[128,128]{1,0:T(8,128)(2,1)S(1)}, bf16[128,128]{1,0:T(8,128)(2,1)S(1)}, u32[]{:S(2)}, u32[]{:S(2)}) collective-permute-start(bf16[128,128]{1,0:T(8,128)(2,1)S(1)} %get-tuple-element.86), channel_id=1, source_target_pairs={{0,8},{8,0},{2,10},{10,2},{4,12},{12,4},{6,14},{14,6},{16,24},{24,... | collective-permute-start | bytes 98312 | tf_op jit(solution)/shard_map/ppermute | solution.py:57
  13.7 3.9 %collective-permute-start.7 = (bf16[128,128]{1,0:T(8,128)(2,1)S(1)}, bf16[128,128]{1,0:T(8,128)(2,1)S(1)}, u32[]{:S(2)}, u32[]{:S(2)}) collective-permute-start(bf16[128,128]{1,0:T(8,128)(2,1)S(1)} %get-tuple-element.87), channel_id=1, source_target_pairs={{0,4},{4,0},{2,6},{6,2},{8,12},{12,8},{10,14},{14,10},{16,20},{20,... | collective-permute-start | bytes 98312 | tf_op jit(solution)/shard_map/ppermute | solution.py:57
  14.6 3.0 %collective-permute-start.8 = (bf16[128,128]{1,0:T(8,128)(2,1)S(1)}, bf16[128,128]{1,0:T(8,128)(2,1)S(1)}, u32[]{:S(2)}, u32[]{:S(2)}) collective-permute-start(bf16[128,128]{1,0:T(8,128)(2,1)S(1)} %get-tuple-element.88), channel_id=1, source_target_pairs={{0,2},{2,0},{4,6},{6,4},{8,10},{10,8},{12,14},{14,12},{16,18},{18,... | collective-permute-start | bytes 98312 | tf_op jit(solution)/shard_map/ppermute | solution.py:57
  14.6 0.7 %copy-start.6 = (f32[8]{0:T(128)S(1)}, f32[8]{0:T(128)}, u32[]{:S(2)}) copy-start(f32[8]{0:T(128)} %kappas.1) | copy-start | bytes 100
  17.8 6.3 %collective-permute-start.9 = (bf16[128,128]{1,0:T(8,128)(2,1)S(1)}, bf16[128,128]{1,0:T(8,128)(2,1)S(1)}, u32[]{:S(2)}, u32[]{:S(2)}) collective-permute-start(bf16[128,128]{1,0:T(8,128)(2,1)S(1)} %get-tuple-element.90), channel_id=1, source_target_pairs={{0,16},{16,0},{2,18},{18,2},{4,20},{20,4},{6,22},{22,6},{8,24},{24... | collective-permute-start | bytes 98312 | tf_op jit(solution)/shard_map/ppermute | solution.py:57
  20.5 3.9 %collective-permute-start.10 = (bf16[128,128]{1,0:T(8,128)(2,1)S(1)}, bf16[128,128]{1,0:T(8,128)(2,1)S(1)}, u32[]{:S(2)}, u32[]{:S(2)}) collective-permute-start(bf16[128,128]{1,0:T(8,128)(2,1)S(1)} %get-tuple-element.91), channel_id=1, source_target_pairs={{0,8},{8,0},{2,10},{10,2},{4,12},{12,4},{6,14},{14,6},{16,24},{24,... | collective-permute-start | bytes 98312 | tf_op jit(solution)/shard_map/ppermute | solution.py:57
  21.5 3.9 %collective-permute-start.11 = (bf16[128,128]{1,0:T(8,128)(2,1)S(1)}, bf16[128,128]{1,0:T(8,128)(2,1)S(1)}, u32[]{:S(2)}, u32[]{:S(2)}) collective-permute-start(bf16[128,128]{1,0:T(8,128)(2,1)S(1)} %get-tuple-element.92), channel_id=1, source_target_pairs={{0,4},{4,0},{2,6},{6,2},{8,12},{12,8},{10,14},{14,10},{16,20},{20,... | collective-permute-start | bytes 98312 | tf_op jit(solution)/shard_map/ppermute | solution.py:57
  22.0 3.4 %collective-permute-start.12 = (bf16[128,128]{1,0:T(8,128)(2,1)S(1)}, bf16[128,128]{1,0:T(8,128)(2,1)S(1)}, u32[]{:S(2)}, u32[]{:S(2)}) collective-permute-start(bf16[128,128]{1,0:T(8,128)(2,1)S(1)} %get-tuple-element.93), channel_id=1, source_target_pairs={{0,2},{2,0},{4,6},{6,4},{8,10},{10,8},{12,14},{14,12},{16,18},{18,... | collective-permute-start | bytes 98312 | tf_op jit(solution)/shard_map/ppermute | solution.py:57
  22.0 6.8 %collective-permute-start.4 = (bf16[2,64,128]{2,1,0:T(8,128)(2,1)S(1)}, bf16[2,64,128]{2,1,0:T(8,128)(2,1)S(1)}, u32[]{:S(2)}, u32[]{:S(2)}) collective-permute-start(bf16[2,64,128]{2,1,0:T(8,128)(2,1)S(1)} %get-tuple-element.84.token), channel_id=1, source_target_pairs={{0,1},{1,0},{2,3},{3,2},{4,5},{5,4},{6,7},{7,6},{8,9},{9,8},{10,11... | collective-permute-start | bytes 98312 | tf_op jit(solution)/shard_map/ppermute | solution.py:526
  25.6 4.9 %collective-permute-start.13 = (bf16[128,128]{1,0:T(8,128)(2,1)S(1)}, bf16[128,128]{1,0:T(8,128)(2,1)S(1)}, u32[]{:S(2)}, u32[]{:S(2)}) collective-permute-start(bf16[128,128]{1,0:T(8,128)(2,1)S(1)} %get-tuple-element.102), channel_id=1, source_target_pairs={{0,16},{16,0},{2,18},{18,2},{4,20},{20,4},{6,22},{22,6},{8,24},{24... | collective-permute-start | bytes 98312 | tf_op jit(solution)/shard_map/ppermute | solution.py:57
  26.0 4.5 %collective-permute-start.14 = (bf16[128,128]{1,0:T(8,128)(2,1)S(1)}, bf16[128,128]{1,0:T(8,128)(2,1)S(1)}, u32[]{:S(2)}, u32[]{:S(2)}) collective-permute-start(bf16[128,128]{1,0:T(8,128)(2,1)S(1)} %get-tuple-element.103), channel_id=1, source_target_pairs={{0,8},{8,0},{2,10},{10,2},{4,12},{12,4},{6,14},{14,6},{16,24},{24,... | collective-permute-start | bytes 98312 | tf_op jit(solution)/shard_map/ppermute | solution.py:57
  27.0 3.9 %collective-permute-start.15 = (bf16[128,128]{1,0:T(8,128)(2,1)S(1)}, bf16[128,128]{1,0:T(8,128)(2,1)S(1)}, u32[]{:S(2)}, u32[]{:S(2)}) collective-permute-start(bf16[128,128]{1,0:T(8,128)(2,1)S(1)} %get-tuple-element.104), channel_id=1, source_target_pairs={{0,4},{4,0},{2,6},{6,2},{8,12},{12,8},{10,14},{14,10},{16,20},{20,... | collective-permute-start | bytes 98312 | tf_op jit(solution)/shard_map/ppermute | solution.py:57
  27.9 3.0 %collective-permute-start.16 = (bf16[128,128]{1,0:T(8,128)(2,1)S(1)}, bf16[128,128]{1,0:T(8,128)(2,1)S(1)}, u32[]{:S(2)}, u32[]{:S(2)}) collective-permute-start(bf16[128,128]{1,0:T(8,128)(2,1)S(1)} %get-tuple-element.105), channel_id=1, source_target_pairs={{0,2},{2,0},{4,6},{6,4},{8,10},{10,8},{12,14},{14,12},{16,18},{18,... | collective-permute-start | bytes 98312 | tf_op jit(solution)/shard_map/ppermute | solution.py:57
  30.9 6.6 %copy-start.1 = (bf16[32,3,64,64]{3,2,1,0:T(8,128)(2,1)S(1)}, bf16[32,3,64,64]{3,2,1,0:T(8,128)(2,1)}, u32[]{:S(2)}) copy-start(bf16[32,3,64,64]{3,2,1,0:T(8,128)(2,1)} %tiles.3) | copy-start | bytes 2359300
  30.9 6.6 %copy-start.2 = (bf16[4,64,64]{2,1,0:T(8,128)(2,1)S(1)}, bf16[4,64,64]{2,1,0:T(8,128)(2,1)}, u32[]{:S(2)}) copy-start(bf16[4,64,64]{2,1,0:T(8,128)(2,1)} %couplings.1) | copy-start | bytes 98308
  30.9 6.6 %copy-start.3 = (f32[32,64]{1,0:T(8,128)S(1)}, f32[32,64]{1,0:T(8,128)}, u32[]{:S(2)}) copy-start(f32[32,64]{1,0:T(8,128)} %coefficient.1) | copy-start | bytes 24580
  31.0 6.6 %copy-start.4 = (f32[32,64]{1,0:T(8,128)S(1)}, f32[32,64]{1,0:T(8,128)}, u32[]{:S(2)}) copy-start(f32[32,64]{1,0:T(8,128)} %storage.1) | copy-start | bytes 24580
  31.0 6.6 %copy-start.5 = (s32[32,3]{0,1:T(4,128)S(1)}, s32[32,3]{0,1:T(4,128)}, u32[]{:S(2)}) copy-start(s32[32,3]{0,1:T(4,128)} %param.27) | copy-start | bytes 1156
  31.8 9.7 %collective-permute-start.21 = (bf16[1552,128]{1,0:T(8,128)(2,1)S(1)}, bf16[1552,128]{1,0:T(8,128)(2,1)S(1)}, u32[]{:S(2)}, u32[]{:S(2)}) collective-permute-start(bf16[1552,128]{1,0:T(8,128)(2,1)S(1)} %bitcast.12), channel_id=1, source_target_pairs={{0,1},{1,0},{2,3},{3,2},{4,5},{5,4},{6,7},{7,6},{8,9},{9,8},{10,11... | collective-permute-start | bytes 1191944 | tf_op jit(solution)/shard_map/ppermute | solution.py:551
  33.4 5.8 %collective-permute-start.17 = (bf16[128,128]{1,0:T(8,128)(2,1)S(1)}, bf16[128,128]{1,0:T(8,128)(2,1)S(1)}, u32[]{:S(2)}, u32[]{:S(2)}) collective-permute-start(bf16[128,128]{1,0:T(8,128)(2,1)S(1)} %get-tuple-element.109), channel_id=1, source_target_pairs={{0,2},{2,0},{4,6},{6,4},{8,10},{10,8},{12,14},{14,12},{16,18},{18,... | collective-permute-start | bytes 98312 | tf_op jit(solution)/shard_map/ppermute | solution.py:57
  33.4 5.8 %collective-permute-start.18 = (bf16[128,128]{1,0:T(8,128)(2,1)S(1)}, bf16[128,128]{1,0:T(8,128)(2,1)S(1)}, u32[]{:S(2)}, u32[]{:S(2)}) collective-permute-start(bf16[128,128]{1,0:T(8,128)(2,1)S(1)} %get-tuple-element.110), channel_id=1, source_target_pairs={{0,8},{8,0},{2,10},{10,2},{4,12},{12,4},{6,14},{14,6},{16,24},{24,... | collective-permute-start | bytes 98312 | tf_op jit(solution)/shard_map/ppermute | solution.py:57
  34.4 4.8 %collective-permute-start.19 = (bf16[128,128]{1,0:T(8,128)(2,1)S(1)}, bf16[128,128]{1,0:T(8,128)(2,1)S(1)}, u32[]{:S(2)}, u32[]{:S(2)}) collective-permute-start(bf16[128,128]{1,0:T(8,128)(2,1)S(1)} %get-tuple-element.111), channel_id=1, source_target_pairs={{0,4},{4,0},{2,6},{6,2},{8,12},{12,8},{10,14},{14,10},{16,20},{20,... | collective-permute-start | bytes 98312 | tf_op jit(solution)/shard_map/ppermute | solution.py:57
  34.9 5.1 %collective-permute-start.20 = (bf16[128,128]{1,0:T(8,128)(2,1)S(1)}, bf16[128,128]{1,0:T(8,128)(2,1)S(1)}, u32[]{:S(2)}, u32[]{:S(2)}) collective-permute-start(bf16[128,128]{1,0:T(8,128)(2,1)S(1)} %get-tuple-element.112), channel_id=1, source_target_pairs={{0,16},{16,0},{2,18},{18,2},{4,20},{20,4},{6,22},{22,6},{8,24},{24... | collective-permute-start | bytes 98312 | tf_op jit(solution)/shard_map/ppermute | solution.py:57
  40.2 5.0 %collective-permute-start.22 = (bf16[8,64,128]{2,1,0:T(8,128)(2,1)S(1)}, bf16[8,64,128]{2,1,0:T(8,128)(2,1)S(1)}, u32[]{:S(2)}, u32[]{:S(2)}) collective-permute-start(bf16[8,64,128]{2,1,0:T(8,128)(2,1)S(1)} %bitcast.13), channel_id=1, source_target_pairs={{0,1},{1,0},{2,3},{3,2},{4,5},{5,4},{6,7},{7,6},{8,9},{9,8},{10,11... | collective-permute-start | bytes 393224 | tf_op jit(solution)/shard_map/ppermute | solution.py:587

commit v4 on v2

--- a/solution.py
+++ b/solution.py
@@ -260,15 +260,17 @@
     levels = len(order)
     incoming = in_level_order(refs[:levels], order)
     state, field, heat, soon = refs[levels + 3 : levels + 7]
-    faces, terms = refs[levels + 7 : 2 * levels + 7], refs[-1]
+    faces, terms, made = refs[levels + 7 : 2 * levels + 7], refs[-2], refs[-1]
     groups, points = soon.shape[0] + 1, heat.shape[1]
     tiles = heat.shape[0] // groups
     update_faces(face_ids, admittance, scale, incoming, state, field, faces, terms)
     for i in range(packed.shape[0]):
         image = jnp.dot(packed[i], picked(field, ids, i), preferred_element_type=F32)
         v = field[i].astype(F32)
+        made[i] = v * (diag[i] * v + image)
+    for i in range(packed.shape[0]):
         s = slot[i]
-        heat[s] = heat[s] + v * (diag[i] * v + image)
+        heat[s] = heat[s] + made[i]
     for g in range(1, groups):
         blocks = [heat[g * tiles + p].astype(BF16) for p in range(spots)]
         for p, block in enumerate(blocks):
@@ -546,7 +548,7 @@
         + on(VM, state, field, heat),
         "heat",
         aliases={9 + levels + n: n for n in range(3)},
-        scratch=[terms],
+        scratch=[terms, pltpu.VMEM(whole, F32)],
         flops=near_flops,
     )
     routes = [[(i, (i + s) % groups) for i in range(groups)] for s in range(1, groups)]

time: 46.2 us -> 46.2 us (level)
  no operation moved by 1% of the time
where the time goes in v4:
time: 46.2 us; the launch traced here: 46.1 us
  starting transfers between devices  23.8 us (52%)
  Pallas kernels  13.2 us (29%)
  waiting for transfers between devices  7.36 us (16%)
  between operations  0.87 us (2%)
  local copies, waits for them, and re-layouts  0.83 us (2%)
    ppermute x20, starting transfers between devices, from_partner(): return lax.ppermute(block, axis, route)  20.2 us
    pallas_call x14, Pallas kernels, call(): pl.pallas_call(kernel, out_shape=[SPACES[id(spec)](shape, dtype) for shap...  13.2 us
    ppermute x20, waiting for transfers between devices, from_partner(): return lax.ppermute(block, axis, route)  5.49 us
    ppermute x1, starting transfers between devices, body(): soon = [lax.ppermute(soon[s], 'therm', routes[s]) for s in range(shifts)]  1.58 us
    ppermute x1, starting transfers between devices, body(): below = above = lax.ppermute(edges[0], 'therm', [(0, 1), (1, 0)])  1.52 us
    ppermute x1, waiting for transfers between devices, body(): late = [lax.ppermute(late[s], 'therm', routes[s]) for s in range(shifts)]  1.15 us
  transfers between devices with their start and end apart: 23, of which 9 were waited for; matrix products, arithmetic and copies ran while one was open for 2% of the time, Pallas kernels for 21%

profile of v4, /device:TPU:0, one launch (start us, length us, event | category | flops | bytes accessed | tf_op | source)
XLA Modules:
  0.0 46.1 jit_solution(5093899177961129239)
XLA Ops:
  0.6 1.3 %start.1 = (bf16[32,64,128]{2,1,0:T(8,128)(2,1)S(1)}, f32[32,64]{1,0:T(8,128)S(1)}, s32[2,4]{1,0:T(2,128)S(4)}, s32[4,32]{1,0:T(4,128)S(4)}, s32[1,32]{1,0:T(1,1...) custom-call(bf16[32,64,128]{2,1,0:T(8,128)(2,1)} %amps.1, ...), custom_call_target="tpu_custom_call" | custom-call | tf_op jit(solution)/shard_map/start/pallas_call | solution.py:33
  2.0 4.1 %collective-permute-start = (bf16[128,128]{1,0:T(8,128)(2,1)S(1)}, bf16[128,128]{1,0:T(8,128)(2,1)S(1)}, u32[]{:S(2)}, u32[]{:S(2)}) collective-permute-start(bf16[128,128]{1,0:T(8,128)(2,1)S(1)} %get-tuple-element.73), channel_id=1, source_target_pairs={{0,16},{16,0},{2,18},{18,2},{4,20},{20,4},{6,22},{22,6},{8,24},{24... | collective-permute-start | bytes 98312 | tf_op jit(solution)/shard_map/ppermute | solution.py:57
  6.1 1.5 %collective-permute-start.1 = (bf16[128,128]{1,0:T(8,128)(2,1)S(1)}, bf16[128,128]{1,0:T(8,128)(2,1)S(1)}, u32[]{:S(2)}, u32[]{:S(2)}) collective-permute-start(bf16[128,128]{1,0:T(8,128)(2,1)S(1)} %get-tuple-element.74), channel_id=1, source_target_pairs={{0,4},{4,0},{2,6},{6,2},{8,12},{12,8},{10,14},{14,10},{16,20},{20,... | collective-permute-start | bytes 98312 | tf_op jit(solution)/shard_map/ppermute | solution.py:57
  7.6 1.6 %collective-permute-start.2 = (bf16[128,128]{1,0:T(8,128)(2,1)S(1)}, bf16[128,128]{1,0:T(8,128)(2,1)S(1)}, u32[]{:S(2)}, u32[]{:S(2)}) collective-permute-start(bf16[128,128]{1,0:T(8,128)(2,1)S(1)} %get-tuple-element.75), channel_id=1, source_target_pairs={{0,8},{8,0},{2,10},{10,2},{4,12},{12,4},{6,14},{14,6},{16,24},{24,... | collective-permute-start | bytes 98312 | tf_op jit(solution)/shard_map/ppermute | solution.py:57
  9.1 2.8 %first.1 = (bf16[32,64,256]{2,1,0:T(8,128)(2,1)S(1)}, f32[32,64,128]{2,1,0:T(8,128)S(1)}, bf16[32,64,128]{2,1,0:T(8,128)(2,1)S(1)}, f32[32,64,128]{2,1,0:T(8,128...) custom-call(s32[4,32]{1,0:T(4,128)S(4)} %get-tuple-element.64.ids, ...), custom_call_target="tpu_custom_call" | custom-call | flops 134217728 | tf_op jit(solution)/shard_map/first/pallas_call | solution.py:33
  12.7 1.0 %collective-permute-start.6 = (bf16[128,128]{1,0:T(8,128)(2,1)S(1)}, bf16[128,128]{1,0:T(8,128)(2,1)S(1)}, u32[]{:S(2)}, u32[]{:S(2)}) collective-permute-start(bf16[128,128]{1,0:T(8,128)(2,1)S(1)} %get-tuple-element.86), channel_id=1, source_target_pairs={{0,8},{8,0},{2,10},{10,2},{4,12},{12,4},{6,14},{14,6},{16,24},{24,... | collective-permute-start | bytes 98312 | tf_op jit(solution)/shard_map/ppermute | solution.py:57
  13.7 0.9 %collective-permute-start.7 = (bf16[128,128]{1,0:T(8,128)(2,1)S(1)}, bf16[128,128]{1,0:T(8,128)(2,1)S(1)}, u32[]{:S(2)}, u32[]{:S(2)}) collective-permute-start(bf16[128,128]{1,0:T(8,128)(2,1)S(1)} %get-tuple-element.87), channel_id=1, source_target_pairs={{0,4},{4,0},{2,6},{6,2},{8,12},{12,8},{10,14},{14,10},{16,20},{20,... | collective-permute-start | bytes 98312 | tf_op jit(solution)/shard_map/ppermute | solution.py:57
  14.6 0.6 %near.3 = (f32[32,64,128]{2,1,0:T(8,128)S(1)}, bf16[32,64,128]{2,1,0:T(8,128)(2,1)S(1)}) custom-call(s32[4,32]{1,0:T(4,128)S(4)} %get-tuple-element.64.ids, bf16[32,64,256]{2,1,0:T(8,128)(2,1)S(1)} %get-tuple-element.71.packed, bf16[32,64,128]{2,1,0:T(8,128)(2,1)S(1)} %get-tuple-element.79.field, f32[32,64,128]{2,1,0:T(8,128)S(1)} %get-tuple-element.80.state, ...), custom_call_target="tpu_custom_call" | custom-call | flops 134217728 | tf_op jit(solution)/shard_map/near/pallas_call | solution.py:33
  15.2 1.0 %flux.1 = (bf16[32,64,128]{2,1,0:T(8,128)(2,1)S(1)}, bf16[2,64,128]{2,1,0:T(8,128)(2,1)S(1)}) custom-call(bf16[32,64,128]{2,1,0:T(8,128)(2,1)S(1)} %get-tuple-element.81.token.refs_5_, f32[8]{0:T(128)S(1)} %copy-done.6, s32[32,64]{1,0:T(8,128)S(1)} %get-tuple-element.82.kind, bf16[32,64,128]{2,1,0:T(8,128)(2,1)S(1)} %get-tuple-element.83.warmth), custom_call_target="tpu_custom_call" | custom-call | tf_op jit(solution)/shard_map/flux/pallas_call | solution.py:33
  16.3 0.8 %collective-permute-done.5.refs_0_ = bf16[128,128]{1,0:T(8,128)(2,1)S(1)} collective-permute-done((bf16[128,128]{1,0:T(8,128)(2,1)S(1)}, bf16[128,128]{1,0:T(8,128)(2,1)S(1)}, u32[]{:S(2)}, u32[]{:S(2)}) %collective-permute-start.5) | collective-permute-done | bytes 32800 | tf_op jit(solution)/shard_map/ppermute | solution.py:57
  17.8 2.7 %collective-permute-start.9 = (bf16[128,128]{1,0:T(8,128)(2,1)S(1)}, bf16[128,128]{1,0:T(8,128)(2,1)S(1)}, u32[]{:S(2)}, u32[]{:S(2)}) collective-permute-start(bf16[128,128]{1,0:T(8,128)(2,1)S(1)} %get-tuple-element.90), channel_id=1, source_target_pairs={{0,16},{16,0},{2,18},{18,2},{4,20},{20,4},{6,22},{22,6},{8,24},{24... | collective-permute-start | bytes 98312 | tf_op jit(solution)/shard_map/ppermute | solution.py:57
  20.5 1.0 %collective-permute-start.10 = (bf16[128,128]{1,0:T(8,128)(2,1)S(1)}, bf16[128,128]{1,0:T(8,128)(2,1)S(1)}, u32[]{:S(2)}, u32[]{:S(2)}) collective-permute-start(bf16[128,128]{1,0:T(8,128)(2,1)S(1)} %get-tuple-element.91), channel_id=1, source_target_pairs={{0,8},{8,0},{2,10},{10,2},{4,12},{12,4},{6,14},{14,6},{16,24},{24,... | collective-permute-start | bytes 98312 | tf_op jit(solution)/shard_map/ppermute | solution.py:57
  21.5 0.5 %collective-permute-start.11 = (bf16[128,128]{1,0:T(8,128)(2,1)S(1)}, bf16[128,128]{1,0:T(8,128)(2,1)S(1)}, u32[]{:S(2)}, u32[]{:S(2)}) collective-permute-start(bf16[128,128]{1,0:T(8,128)(2,1)S(1)} %get-tuple-element.92), channel_id=1, source_target_pairs={{0,4},{4,0},{2,6},{6,2},{8,12},{12,8},{10,14},{14,10},{16,20},{20,... | collective-permute-start | bytes 98312 | tf_op jit(solution)/shard_map/ppermute | solution.py:57
  22.0 1.5 %collective-permute-start.4 = (bf16[2,64,128]{2,1,0:T(8,128)(2,1)S(1)}, bf16[2,64,128]{2,1,0:T(8,128)(2,1)S(1)}, u32[]{:S(2)}, u32[]{:S(2)}) collective-permute-start(bf16[2,64,128]{2,1,0:T(8,128)(2,1)S(1)} %get-tuple-element.84.token), channel_id=1, source_target_pairs={{0,1},{1,0},{2,3},{3,2},{4,5},{5,4},{6,7},{7,6},{8,9},{9,8},{10,11... | collective-permute-start | bytes 98312 | tf_op jit(solution)/shard_map/ppermute | solution.py:530
  23.5 0.6 %near.4 = (f32[32,64,128]{2,1,0:T(8,128)S(1)}, bf16[32,64,128]{2,1,0:T(8,128)(2,1)S(1)}) custom-call(s32[4,32]{1,0:T(4,128)S(4)} %get-tuple-element.64.ids, bf16[32,64,256]{2,1,0:T(8,128)(2,1)S(1)} %get-tuple-element.71.packed, bf16[32,64,128]{2,1,0:T(8,128)(2,1)S(1)} %get-tuple-element.94.field, f32[32,64,128]{2,1,0:T(8,128)S(1)} %get-tuple-element.95.state, ...), custom_call_target="tpu_custom_call" | custom-call | flops 134217728 | tf_op jit(solution)/shard_map/near/pallas_call | solution.py:33
  24.4 1.0 %collective-permute-done.11.refs_2_ = bf16[128,128]{1,0:T(8,128)(2,1)S(1)} collective-permute-done((bf16[128,128]{1,0:T(8,128)(2,1)S(1)}, bf16[128,128]{1,0:T(8,128)(2,1)S(1)}, u32[]{:S(2)}, u32[]{:S(2)}) %collective-permute-start.11) | collective-permute-done | bytes 32800 | tf_op jit(solution)/shard_map/ppermute | solution.py:57
  26.0 1.0 %collective-permute-start.14 = (bf16[128,128]{1,0:T(8,128)(2,1)S(1)}, bf16[128,128]{1,0:T(8,128)(2,1)S(1)}, u32[]{:S(2)}, u32[]{:S(2)}) collective-permute-start(bf16[128,128]{1,0:T(8,128)(2,1)S(1)} %get-tuple-element.103), channel_id=1, source_target_pairs={{0,8},{8,0},{2,10},{10,2},{4,12},{12,4},{6,14},{14,6},{16,24},{24,... | collective-permute-start | bytes 98312 | tf_op jit(solution)/shard_map/ppermute | solution.py:57
  27.0 0.9 %collective-permute-start.15 = (bf16[128,128]{1,0:T(8,128)(2,1)S(1)}, bf16[128,128]{1,0:T(8,128)(2,1)S(1)}, u32[]{:S(2)}, u32[]{:S(2)}) collective-permute-start(bf16[128,128]{1,0:T(8,128)(2,1)S(1)} %get-tuple-element.104), channel_id=1, source_target_pairs={{0,4},{4,0},{2,6},{6,2},{8,12},{12,8},{10,14},{14,10},{16,20},{20,... | collective-permute-start | bytes 98312 | tf_op jit(solution)/shard_map/ppermute | solution.py:57
  27.9 0.9 %near.5 = (f32[32,64,128]{2,1,0:T(8,128)S(1)}, bf16[32,64,128]{2,1,0:T(8,128)(2,1)S(1)}, f32[64,64,128]{2,1,0:T(8,128)S(1)}, f32[32,64,128]{2,1,0:T(8,128)S(1)}) custom-call(s32[4,32]{1,0:T(4,128)S(4)} %get-tuple-element.64.ids, bf16[32,64,256]{2,1,0:T(8,128)(2,1)S(1)} %get-tuple-element.71.packed, bf16[32,64,128]{2,1,0:T(8,128)(2,1)S(1)} %get-tuple-element.98.field, ...), custom_call_target="tpu_custom_call" | custom-call | flops 134217728 | tf_op jit(solution)/shard_map/near/pallas_call | solution.py:33
  28.8 1.6 %collective-permute-done.13.refs_0_ = bf16[128,128]{1,0:T(8,128)(2,1)S(1)} collective-permute-done((bf16[128,128]{1,0:T(8,128)(2,1)S(1)}, bf16[128,128]{1,0:T(8,128)(2,1)S(1)}, u32[]{:S(2)}, u32[]{:S(2)}) %collective-permute-start.13) | collective-permute-done | bytes 32800 | tf_op jit(solution)/shard_map/ppermute | solution.py:57
  31.0 0.8 %heat.1 = (f32[32,64,128]{2,1,0:T(8,128)S(1)}, bf16[32,64,128]{2,1,0:T(8,128)(2,1)S(1)}, f32[64,64,128]{2,1,0:T(8,128)S(1)}, bf16[1,1552,128]{2,1,0:T(8,128)(2,1...) custom-call(bf16[2,64,128]{2,1,0:T(8,128)(2,1)S(1)} %collective-perm, ...), custom_call_target="tpu_custom_call", output_to_operand_aliasing={{0}: (13, {}), {1}: (14, {}), {2}: (15, {})} | custom-call | flops 134217728 | tf_op jit(solution)/shard_map/heat/pallas_call | solution.py:33
  31.8 1.6 %collective-permute-start.21 = (bf16[1552,128]{1,0:T(8,128)(2,1)S(1)}, bf16[1552,128]{1,0:T(8,128)(2,1)S(1)}, u32[]{:S(2)}, u32[]{:S(2)}) collective-permute-start(bf16[1552,128]{1,0:T(8,128)(2,1)S(1)} %bitcast.12), channel_id=1, source_target_pairs={{0,1},{1,0},{2,3},{3,2},{4,5},{5,4},{6,7},{7,6},{8,9},{9,8},{10,11... | collective-permute-start | bytes 1191944 | tf_op jit(solution)/shard_map/ppermute | solution.py:555
  33.4 1.0 %collective-permute-start.18 = (bf16[128,128]{1,0:T(8,128)(2,1)S(1)}, bf16[128,128]{1,0:T(8,128)(2,1)S(1)}, u32[]{:S(2)}, u32[]{:S(2)}) collective-permute-start(bf16[128,128]{1,0:T(8,128)(2,1)S(1)} %get-tuple-element.110), channel_id=1, source_target_pairs={{0,8},{8,0},{2,10},{10,2},{4,12},{12,4},{6,14},{14,6},{16,24},{24,... | collective-permute-start | bytes 98312 | tf_op jit(solution)/shard_map/ppermute | solution.py:57
  35.0 2.6 %collective-permute-start.20 = (bf16[128,128]{1,0:T(8,128)(2,1)S(1)}, bf16[128,128]{1,0:T(8,128)(2,1)S(1)}, u32[]{:S(2)}, u32[]{:S(2)}) collective-permute-start(bf16[128,128]{1,0:T(8,128)(2,1)S(1)} %get-tuple-element.112), channel_id=1, source_target_pairs={{0,16},{16,0},{2,18},{18,2},{4,20},{20,4},{6,22},{22,6},{8,24},{24... | collective-permute-start | bytes 98312 | tf_op jit(solution)/shard_map/ppermute | solution.py:57
  37.6 1.6 %conduction.1 = (f32[32,64,128]{2,1,0:T(8,128)S(1)}, f32[32,64,128]{2,1,0:T(8,128)S(1)}) custom-call(s32[3,32]{1,0:T(4,128)S(1)} %bitcast.11, bf16[32,3,64,64]{3,2,1,0:T(8,128)(2,1)S(1)} %copy-done.1, f32[32,64]{1,0:T(8,128)S(1)} %copy-done.3, f32[32,64]{1,0:T(8,128)S(1)} %copy-done.4, bf16[4,64,64]{2,1,0:T(8,128)(2,1)S(1)} %copy-done.2, ...), custom_call_target="tpu_custom_call" | custom-call | flops 134217728 | tf_op jit(solution)/shard_map/conduction/pallas_call | solution.py:33
  39.2 0.8 %collective-permute-done.20.refs_3_ = bf16[128,128]{1,0:T(8,128)(2,1)S(1)} collective-permute-done((bf16[128,128]{1,0:T(8,128)(2,1)S(1)}, bf16[128,128]{1,0:T(8,128)(2,1)S(1)}, u32[]{:S(2)}, u32[]{:S(2)}) %collective-permute-start.20) | collective-permute-done | bytes 32800 | tf_op jit(solution)/shard_map/ppermute | solution.py:57
  40.2 0.5 %collective-permute-start.22 = (bf16[8,64,128]{2,1,0:T(8,128)(2,1)S(1)}, bf16[8,64,128]{2,1,0:T(8,128)(2,1)S(1)}, u32[]{:S(2)}, u32[]{:S(2)}) collective-permute-start(bf16[8,64,128]{2,1,0:T(8,128)(2,1)S(1)} %bitcast.13), channel_id=1, source_target_pairs={{0,1},{1,0},{2,3},{3,2},{4,5},{5,4},{6,7},{7,6},{8,9},{9,8},{10,11... | collective-permute-start | bytes 393224 | tf_op jit(solution)/shard_map/ppermute | solution.py:591
  40.8 0.7 %collective-permute-done.21.refs_1_ = bf16[1552,128]{1,0:T(8,128)(2,1)S(1)} collective-permute-done((bf16[1552,128]{1,0:T(8,128)(2,1)S(1)}, bf16[1552,128]{1,0:T(8,128)(2,1)S(1)}, u32[]{:S(2)}, u32[]{:S(2)}) %collective-permute-start.21) | collective-permute-done | bytes 397344 | tf_op jit(solution)/shard_map/ppermute | solution.py:555
  41.5 1.8 %early.1 = (f32[32,64,128]{2,1,0:T(8,128)S(1)}, bf16[32,64,128]{2,1,0:T(8,128)(2,1)S(1)}, f32[32,64,128]{2,1,0:T(8,128)}, s32[8]{0:T(128)S(4)}) custom-call(f32[64,64,128]{2,1,0:T(8,128)S(1)} %get-tuple-element.115.heat, f32[32,64,128]{2,1,0:T(8,128)S(1)} %get-tuple-element.117.gain, ...), custom_call_target="tpu_custom_call", output_to_operand_aliasing={{0}: (4, {}), {1}: (5, {})} | custom-call | tf_op jit(solution)/shard_map/early/pallas_call | solution.py:33
  43.3 0.8 %copy.46 = bf16[32,64,128]{2,1,0:T(8,128)(2,1)} copy(bf16[32,64,128]{2,1,0:T(8,128)(2,1)S(1)} %get-tuple-element.126) | data formatting | bytes 1048576
  44.1 1.1 %collective-permute-done.22.refs_1_ = bf16[8,64,128]{2,1,0:T(8,128)(2,1)S(1)} collective-permute-done((bf16[8,64,128]{2,1,0:T(8,128)(2,1)S(1)}, bf16[8,64,128]{2,1,0:T(8,128)(2,1)S(1)}, u32[]{:S(2)}, u32[]{:S(2)}) %collective-permute-start.22) | collective-permute-done | bytes 131104 | tf_op jit(solution)/shard_map/ppermute | solution.py:591
  45.3 0.8 %late.1 = f32[32,64,128]{2,1,0:T(8,128)} custom-call(f32[32,64,128]{2,1,0:T(8,128)S(1)} %get-tuple-element.117.gain, s32[8]{0:T(128)S(4)} %get-tuple-element.122.refs_0_, bf16[8,64,128]{2,1,0:T(8,128)(2,1)S(1)} %collective-permute-done.22.refs_1_, f32[32,64,128]{2,1,0:T(8,128)S(1)} %get-tuple-element.124.refs_2_, ...), custom_call_target="tpu_custom_call", output_to_operand_aliasing={{}: (4, {})} | custom-call | tf_op jit(solution)/shard_map/late/pallas_call | solution.py:33
  (44 shorter events, 3.4 us)
Async XLA Ops:
  0.6 11.4 %copy-start = (bf16[8,64,64]{2,1,0:T(8,128)(2,1)S(1)}, bf16[8,64,64]{2,1,0:T(8,128)(2,1)}, u32[]{:S(2)}) copy-start(bf16[8,64,64]{2,1,0:T(8,128)(2,1)} %admittance.9) | copy-start | bytes 196612
  2.0 10.0 %collective-permute-start = (bf16[128,128]{1,0:T(8,128)(2,1)S(1)}, bf16[128,128]{1,0:T(8,128)(2,1)S(1)}, u32[]{:S(2)}, u32[]{:S(2)}) collective-permute-start(bf16[128,128]{1,0:T(8,128)(2,1)S(1)} %get-tuple-element.73), channel_id=1, source_target_pairs={{0,16},{16,0},{2,18},{18,2},{4,20},{20,4},{6,22},{22,6},{8,24},{24... | collective-permute-start | bytes 98312 | tf_op jit(solution)/shard_map/ppermute | solution.py:57
  6.1 5.9 %collective-permute-start.1 = (bf16[128,128]{1,0:T(8,128)(2,1)S(1)}, bf16[128,128]{1,0:T(8,128)(2,1)S(1)}, u32[]{:S(2)}, u32[]{:S(2)}) collective-permute-start(bf16[128,128]{1,0:T(8,128)(2,1)S(1)} %get-tuple-element.74), channel_id=1, source_target_pairs={{0,4},{4,0},{2,6},{6,2},{8,12},{12,8},{10,14},{14,10},{16,20},{20,... | collective-permute-start | bytes 98312 | tf_op jit(solution)/shard_map/ppermute | solution.py:57
  7.6 4.4 %collective-permute-start.2 = (bf16[128,128]{1,0:T(8,128)(2,1)S(1)}, bf16[128,128]{1,0:T(8,128)(2,1)S(1)}, u32[]{:S(2)}, u32[]{:S(2)}) collective-permute-start(bf16[128,128]{1,0:T(8,128)(2,1)S(1)} %get-tuple-element.75), channel_id=1, source_target_pairs={{0,8},{8,0},{2,10},{10,2},{4,12},{12,4},{6,14},{14,6},{16,24},{24,... | collective-permute-start | bytes 98312 | tf_op jit(solution)/shard_map/ppermute | solution.py:57
  9.1 2.9 %collective-permute-start.3 = (bf16[128,128]{1,0:T(8,128)(2,1)S(1)}, bf16[128,128]{1,0:T(8,128)(2,1)S(1)}, u32[]{:S(2)}, u32[]{:S(2)}) collective-permute-start(bf16[128,128]{1,0:T(8,128)(2,1)S(1)} %get-tuple-element.76), channel_id=1, source_target_pairs={{0,2},{2,0},{4,6},{6,4},{8,10},{10,8},{12,14},{14,12},{16,18},{18,... | collective-permute-start | bytes 98312 | tf_op jit(solution)/shard_map/ppermute | solution.py:57
  12.3 4.9 %collective-permute-start.5 = (bf16[128,128]{1,0:T(8,128)(2,1)S(1)}, bf16[128,128]{1,0:T(8,128)(2,1)S(1)}, u32[]{:S(2)}, u32[]{:S(2)}) collective-permute-start(bf16[128,128]{1,0:T(8,128)(2,1)S(1)} %get-tuple-element.85), channel_id=1, source_target_pairs={{0,16},{16,0},{2,18},{18,2},{4,20},{20,4},{6,22},{22,6},{8,24},{24... | collective-permute-start | bytes 98312 | tf_op jit(solution)/shard_map/ppermute | solution.py:57
  12.7 4.5 %collective-permute-start.6 = (bf16[128,128]{1,0:T(8,128)(2,1)S(1)}, bf16[128,128]{1,0:T(8,128)(2,1)S(1)}, u32[]{:S(2)}, u32[]{:S(2)}) collective-permute-start(bf16[128,128]{1,0:T(8,128)(2,1)S(1)} %get-tuple-element.86), channel_id=1, source_target_pairs={{0,8},{8,0},{2,10},{10,2},{4,12},{12,4},{6,14},{14,6},{16,24},{24,... | collective-permute-start | bytes 98312 | tf_op jit(solution)/shard_map/ppermute | solution.py:57
  13.7 3.9 %collective-permute-start.7 = (bf16[128,128]{1,0:T(8,128)(2,1)S(1)}, bf16[128,128]{1,0:T(8,128)(2,1)S(1)}, u32[]{:S(2)}, u32[]{:S(2)}) collective-permute-start(bf16[128,128]{1,0:T(8,128)(2,1)S(1)} %get-tuple-element.87), channel_id=1, source_target_pairs={{0,4},{4,0},{2,6},{6,2},{8,12},{12,8},{10,14},{14,10},{16,20},{20,... | collective-permute-start | bytes 98312 | tf_op jit(solution)/shard_map/ppermute | solution.py:57
  14.6 3.0 %collective-permute-start.8 = (bf16[128,128]{1,0:T(8,128)(2,1)S(1)}, bf16[128,128]{1,0:T(8,128)(2,1)S(1)}, u32[]{:S(2)}, u32[]{:S(2)}) collective-permute-start(bf16[128,128]{1,0:T(8,128)(2,1)S(1)} %get-tuple-element.88), channel_id=1, source_target_pairs={{0,2},{2,0},{4,6},{6,4},{8,10},{10,8},{12,14},{14,12},{16,18},{18,... | collective-permute-start | bytes 98312 | tf_op jit(solution)/shard_map/ppermute | solution.py:57
  14.6 0.7 %copy-start.6 = (f32[8]{0:T(128)S(1)}, f32[8]{0:T(128)}, u32[]{:S(2)}) copy-start(f32[8]{0:T(128)} %kappas.1) | copy-start | bytes 100
  17.8 6.3 %collective-permute-start.9 = (bf16[128,128]{1,0:T(8,128)(2,1)S(1)}, bf16[128,128]{1,0:T(8,128)(2,1)S(1)}, u32[]{:S(2)}, u32[]{:S(2)}) collective-permute-start(bf16[128,128]{1,0:T(8,128)(2,1)S(1)} %get-tuple-element.90), channel_id=1, source_target_pairs={{0,16},{16,0},{2,18},{18,2},{4,20},{20,4},{6,22},{22,6},{8,24},{24... | collective-permute-start | bytes 98312 | tf_op jit(solution)/shard_map/ppermute | solution.py:57
  20.5 3.9 %collective-permute-start.10 = (bf16[128,128]{1,0:T(8,128)(2,1)S(1)}, bf16[128,128]{1,0:T(8,128)(2,1)S(1)}, u32[]{:S(2)}, u32[]{:S(2)}) collective-permute-start(bf16[128,128]{1,0:T(8,128)(2,1)S(1)} %get-tuple-element.91), channel_id=1, source_target_pairs={{0,8},{8,0},{2,10},{10,2},{4,12},{12,4},{6,14},{14,6},{16,24},{24,... | collective-permute-start | bytes 98312 | tf_op jit(solution)/shard_map/ppermute | solution.py:57
  21.5 3.9 %collective-permute-start.11 = (bf16[128,128]{1,0:T(8,128)(2,1)S(1)}, bf16[128,128]{1,0:T(8,128)(2,1)S(1)}, u32[]{:S(2)}, u32[]{:S(2)}) collective-permute-start(bf16[128,128]{1,0:T(8,128)(2,1)S(1)} %get-tuple-element.92), channel_id=1, source_target_pairs={{0,4},{4,0},{2,6},{6,2},{8,12},{12,8},{10,14},{14,10},{16,20},{20,... | collective-permute-start | bytes 98312 | tf_op jit(solution)/shard_map/ppermute | solution.py:57
  22.0 3.4 %collective-permute-start.12 = (bf16[128,128]{1,0:T(8,128)(2,1)S(1)}, bf16[128,128]{1,0:T(8,128)(2,1)S(1)}, u32[]{:S(2)}, u32[]{:S(2)}) collective-permute-start(bf16[128,128]{1,0:T(8,128)(2,1)S(1)} %get-tuple-element.93), channel_id=1, source_target_pairs={{0,2},{2,0},{4,6},{6,4},{8,10},{10,8},{12,14},{14,12},{16,18},{18,... | collective-permute-start | bytes 98312 | tf_op jit(solution)/shard_map/ppermute | solution.py:57
  22.0 6.8 %collective-permute-start.4 = (bf16[2,64,128]{2,1,0:T(8,128)(2,1)S(1)}, bf16[2,64,128]{2,1,0:T(8,128)(2,1)S(1)}, u32[]{:S(2)}, u32[]{:S(2)}) collective-permute-start(bf16[2,64,128]{2,1,0:T(8,128)(2,1)S(1)} %get-tuple-element.84.token), channel_id=1, source_target_pairs={{0,1},{1,0},{2,3},{3,2},{4,5},{5,4},{6,7},{7,6},{8,9},{9,8},{10,11... | collective-permute-start | bytes 98312 | tf_op jit(solution)/shard_map/ppermute | solution.py:530
  25.6 4.9 %collective-permute-start.13 = (bf16[128,128]{1,0:T(8,128)(2,1)S(1)}, bf16[128,128]{1,0:T(8,128)(2,1)S(1)}, u32[]{:S(2)}, u32[]{:S(2)}) collective-permute-start(bf16[128,128]{1,0:T(8,128)(2,1)S(1)} %get-tuple-element.102), channel_id=1, source_target_pairs={{0,16},{16,0},{2,18},{18,2},{4,20},{20,4},{6,22},{22,6},{8,24},{24... | collective-permute-start | bytes 98312 | tf_op jit(solution)/shard_map/ppermute | solution.py:57
  26.0 4.5 %collective-permute-start.14 = (bf16[128,128]{1,0:T(8,128)(2,1)S(1)}, bf16[128,128]{1,0:T(8,128)(2,1)S(1)}, u32[]{:S(2)}, u32[]{:S(2)}) collective-permute-start(bf16[128,128]{1,0:T(8,128)(2,1)S(1)} %get-tuple-element.103), channel_id=1, source_target_pairs={{0,8},{8,0},{2,10},{10,2},{4,12},{12,4},{6,14},{14,6},{16,24},{24,... | collective-permute-start | bytes 98312 | tf_op jit(solution)/shard_map/ppermute | solution.py:57
  27.0 3.9 %collective-permute-start.15 = (bf16[128,128]{1,0:T(8,128)(2,1)S(1)}, bf16[128,128]{1,0:T(8,128)(2,1)S(1)}, u32[]{:S(2)}, u32[]{:S(2)}) collective-permute-start(bf16[128,128]{1,0:T(8,128)(2,1)S(1)} %get-tuple-element.104), channel_id=1, source_target_pairs={{0,4},{4,0},{2,6},{6,2},{8,12},{12,8},{10,14},{14,10},{16,20},{20,... | collective-permute-start | bytes 98312 | tf_op jit(solution)/shard_map/ppermute | solution.py:57
  27.9 3.0 %collective-permute-start.16 = (bf16[128,128]{1,0:T(8,128)(2,1)S(1)}, bf16[128,128]{1,0:T(8,128)(2,1)S(1)}, u32[]{:S(2)}, u32[]{:S(2)}) collective-permute-start(bf16[128,128]{1,0:T(8,128)(2,1)S(1)} %get-tuple-element.105), channel_id=1, source_target_pairs={{0,2},{2,0},{4,6},{6,4},{8,10},{10,8},{12,14},{14,12},{16,18},{18,... | collective-permute-start | bytes 98312 | tf_op jit(solution)/shard_map/ppermute | solution.py:57
  30.9 6.6 %copy-start.1 = (bf16[32,3,64,64]{3,2,1,0:T(8,128)(2,1)S(1)}, bf16[32,3,64,64]{3,2,1,0:T(8,128)(2,1)}, u32[]{:S(2)}) copy-start(bf16[32,3,64,64]{3,2,1,0:T(8,128)(2,1)} %tiles.3) | copy-start | bytes 2359300
  30.9 6.6 %copy-start.2 = (bf16[4,64,64]{2,1,0:T(8,128)(2,1)S(1)}, bf16[4,64,64]{2,1,0:T(8,128)(2,1)}, u32[]{:S(2)}) copy-start(bf16[4,64,64]{2,1,0:T(8,128)(2,1)} %couplings.1) | copy-start | bytes 98308
  30.9 6.6 %copy-start.3 = (f32[32,64]{1,0:T(8,128)S(1)}, f32[32,64]{1,0:T(8,128)}, u32[]{:S(2)}) copy-start(f32[32,64]{1,0:T(8,128)} %coefficient.1) | copy-start | bytes 24580
  31.0 6.6 %copy-start.4 = (f32[32,64]{1,0:T(8,128)S(1)}, f32[32,64]{1,0:T(8,128)}, u32[]{:S(2)}) copy-start(f32[32,64]{1,0:T(8,128)} %storage.1) | copy-start | bytes 24580
  31.0 6.6 %copy-start.5 = (s32[32,3]{0,1:T(4,128)S(1)}, s32[32,3]{0,1:T(4,128)}, u32[]{:S(2)}) copy-start(s32[32,3]{0,1:T(4,128)} %param.27) | copy-start | bytes 1156
  31.8 9.7 %collective-permute-start.21 = (bf16[1552,128]{1,0:T(8,128)(2,1)S(1)}, bf16[1552,128]{1,0:T(8,128)(2,1)S(1)}, u32[]{:S(2)}, u32[]{:S(2)}) collective-permute-start(bf16[1552,128]{1,0:T(8,128)(2,1)S(1)} %bitcast.12), channel_id=1, source_target_pairs={{0,1},{1,0},{2,3},{3,2},{4,5},{5,4},{6,7},{7,6},{8,9},{9,8},{10,11... | collective-permute-start | bytes 1191944 | tf_op jit(solution)/shard_map/ppermute | solution.py:555
  33.4 5.8 %collective-permute-start.17 = (bf16[128,128]{1,0:T(8,128)(2,1)S(1)}, bf16[128,128]{1,0:T(8,128)(2,1)S(1)}, u32[]{:S(2)}, u32[]{:S(2)}) collective-permute-start(bf16[128,128]{1,0:T(8,128)(2,1)S(1)} %get-tuple-element.109), channel_id=1, source_target_pairs={{0,2},{2,0},{4,6},{6,4},{8,10},{10,8},{12,14},{14,12},{16,18},{18,... | collective-permute-start | bytes 98312 | tf_op jit(solution)/shard_map/ppermute | solution.py:57
  33.4 5.8 %collective-permute-start.18 = (bf16[128,128]{1,0:T(8,128)(2,1)S(1)}, bf16[128,128]{1,0:T(8,128)(2,1)S(1)}, u32[]{:S(2)}, u32[]{:S(2)}) collective-permute-start(bf16[128,128]{1,0:T(8,128)(2,1)S(1)} %get-tuple-element.110), channel_id=1, source_target_pairs={{0,8},{8,0},{2,10},{10,2},{4,12},{12,4},{6,14},{14,6},{16,24},{24,... | collective-permute-start | bytes 98312 | tf_op jit(solution)/shard_map/ppermute | solution.py:57
  34.4 4.8 %collective-permute-start.19 = (bf16[128,128]{1,0:T(8,128)(2,1)S(1)}, bf16[128,128]{1,0:T(8,128)(2,1)S(1)}, u32[]{:S(2)}, u32[]{:S(2)}) collective-permute-start(bf16[128,128]{1,0:T(8,128)(2,1)S(1)} %get-tuple-element.111), channel_id=1, source_target_pairs={{0,4},{4,0},{2,6},{6,2},{8,12},{12,8},{10,14},{14,10},{16,20},{20,... | collective-permute-start | bytes 98312 | tf_op jit(solution)/shard_map/ppermute | solution.py:57
  35.0 5.1 %collective-permute-start.20 = (bf16[128,128]{1,0:T(8,128)(2,1)S(1)}, bf16[128,128]{1,0:T(8,128)(2,1)S(1)}, u32[]{:S(2)}, u32[]{:S(2)}) collective-permute-start(bf16[128,128]{1,0:T(8,128)(2,1)S(1)} %get-tuple-element.112), channel_id=1, source_target_pairs={{0,16},{16,0},{2,18},{18,2},{4,20},{20,4},{6,22},{22,6},{8,24},{24... | collective-permute-start | bytes 98312 | tf_op jit(solution)/shard_map/ppermute | solution.py:57
  40.2 5.0 %collective-permute-start.22 = (bf16[8,64,128]{2,1,0:T(8,128)(2,1)S(1)}, bf16[8,64,128]{2,1,0:T(8,128)(2,1)S(1)}, u32[]{:S(2)}, u32[]{:S(2)}) collective-permute-start(bf16[8,64,128]{2,1,0:T(8,128)(2,1)S(1)} %bitcast.13), channel_id=1, source_target_pairs={{0,1},{1,0},{2,3},{3,2},{4,5},{5,4},{6,7},{7,6},{8,9},{9,8},{10,11... | collective-permute-start | bytes 393224 | tf_op jit(solution)/shard_map/ppermute | solution.py:591
